TPU v7x, 32 devices: a whole 2x2x4 slice. The times are simulated.
32 devices in a mesh: tok: 8 (over y, x, core), bkt: 4 (over z).
Axes of the slice: x: 2, y: 2, z: 4, core: 2. Of those that a mesh axis runs over, the one named last changes fastest.
Arguments:
- block_in: bfloat16 [8192, 2048], P(('tok', 'bkt')), may hold values from -6 to 6
- cotangent: float32 [8192, 2048], P(('tok', 'bkt')), may hold values from -8 to 8
- buckets: int32 [8], P('tok'), may hold values from 0 to 3, as said below
- qkv_weight: float32 [3, 2048, 2048], P(None, 'tok', 'bkt'), may hold values from -0.125 to 0.125
- qkv_first: float32 [3, 2048, 2048], P(None, 'tok', 'bkt'), may hold values from -0.00024414062 to 0.00024414062
- qkv_second: float32 [3, 2048, 2048], P(None, 'tok', 'bkt'), may hold values from 1.0449831e-09 to 4.1719854e-09
- out_weight: float32 [2048, 2048], P('bkt', 'tok'), may hold values from -0.5 to 0.5
- out_first: float32 [2048, 2048], P('bkt', 'tok'), may hold values from -0.00024414062 to 0.00024414062
- out_second: float32 [2048, 2048], P('bkt', 'tok'), may hold values from 1.0449831e-09 to 4.1719854e-09
- up_weight: float32 [2048, 8192], P('tok', 'bkt'), may hold values from -0.125 to 0.125
- up_first: float32 [2048, 8192], P('tok', 'bkt'), may hold values from -0.00024414062 to 0.00024414062
- up_second: float32 [2048, 8192], P('tok', 'bkt'), may hold values from 1.0449831e-09 to 4.1719854e-09
- down_weight: float32 [8192, 2048], P('bkt', 'tok'), may hold values from -0.0625 to 0.0625
- down_first: float32 [8192, 2048], P('bkt', 'tok'), may hold values from -0.00024414062 to 0.00024414062
- down_second: float32 [8192, 2048], P('bkt', 'tok'), may hold values from 1.0449831e-09 to 4.1719854e-09
- norm_gains: float32 [2, 2048], P(None, 'tok'), may hold values from 0.25 to 1.75
- gains_first: float32 [2, 2048], P(None, 'tok'), may hold values from -0.0007324219 to 0.0007324219
- gains_second: float32 [2, 2048], P(None, 'tok'), may hold values from 9.337301e-09 to 3.7746535e-08
Outputs:
- block_out: float32 [8192, 2048], P(('tok', 'bkt'))
- block_in_grad: float32 [8192, 2048], P(('tok', 'bkt'))
- grad_norm: float32 [], replicated
- qkv_new: float32 [3, 2048, 2048], P(None, 'tok', 'bkt')
- qkv_copy: bfloat16 [3, 2048, 2048], P(None, 'tok', 'bkt')
- qkv_first_new: float32 [3, 2048, 2048], P(None, 'tok', 'bkt')
- qkv_second_new: float32 [3, 2048, 2048], P(None, 'tok', 'bkt')
- out_new: float32 [2048, 2048], P('bkt', 'tok')
- out_copy: bfloat16 [2048, 2048], P('bkt', 'tok')
- out_first_new: float32 [2048, 2048], P('bkt', 'tok')
- out_second_new: float32 [2048, 2048], P('bkt', 'tok')
- up_new: float32 [2048, 8192], P('tok', 'bkt')
- up_copy: bfloat16 [2048, 8192], P('tok', 'bkt')
- up_first_new: float32 [2048, 8192], P('tok', 'bkt')
- up_second_new: float32 [2048, 8192], P('tok', 'bkt')
- down_new: float32 [8192, 2048], P('bkt', 'tok')
- down_copy: bfloat16 [8192, 2048], P('bkt', 'tok')
- down_first_new: float32 [8192, 2048], P('bkt', 'tok')
- down_second_new: float32 [8192, 2048], P('bkt', 'tok')
- gains_new: float32 [2, 2048], P(None, 'tok')
- gains_copy: bfloat16 [2, 2048], P(None, 'tok')
- gains_first_new: float32 [2, 2048], P(None, 'tok')
- gains_second_new: float32 [2, 2048], P(None, 'tok')
Inputs may be any that keep to these rules, and one draw needn't show every extreme that they name: `buckets`: each of the 4 widths is chosen by exactly 2 sequences.
All inputs are finite; a program needn't handle non-finite values.
Results may differ from a plain program's by a relative error of at most 0.019.
Values may be sent and summed in bfloat16 or wider, within the bound.
No kernel may reach another device: no remote copies, remote signals or barrier semaphores. Data moves between devices by JAX's collectives and lax.ppermute only.
A program may use at most 192 MiB of HBM per device.

v0:
```python
import jax
import jax.numpy as jnp
from jax import lax
from jax.sharding import PartitionSpec as P

D = 2048
H = 16
HD = 128
FF = 8192
STEP = 10


NORM_EPS = 1e-05
ADAM_EPS = 1e-08
CLIP_NORM = 1.0
BETA_ONE = 0.9
BETA_TWO = 0.95
DECAY_RATE = 0.1
GAIN_RATE = 0.3
ROPE_BASE = 10000.0


def rms_scale(values, gain):
    return values * lax.rsqrt(jnp.mean(values * values, axis=-1, keepdims=True) + NORM_EPS) * gain


def rotary_tables(length):
    positions = jnp.arange(length).astype(jnp.float32)[:, None]
    freq_index = jnp.arange(HD // 2).astype(jnp.float32)
    angles = positions * (ROPE_BASE ** (-2.0 * freq_index / HD))[None, :]
    cosine = jnp.cos(angles)
    sine = jnp.sin(angles)
    return (jnp.concatenate([cosine, cosine], axis=-1), jnp.concatenate([sine, sine], axis=-1))


def rotate(values, cosine, sine):
    half = values.shape[-1] // 2
    turned = jnp.concatenate([-values[..., half:], values[..., :half]], axis=-1)
    return values * cosine[:, None, :] + turned * sine[:, None, :]


def adam_step(weight, grad, first, second, factor, rate, decay):
    clipped = grad * factor
    first_new = BETA_ONE * first + (1.0 - BETA_ONE) * clipped
    second_new = BETA_TWO * second + (1.0 - BETA_TWO) * clipped * clipped
    first_hat = first_new / (1.0 - BETA_ONE**STEP)
    second_hat = second_new / (1.0 - BETA_TWO**STEP)
    weight_new = weight - rate * (first_hat / (jnp.sqrt(second_hat) + ADAM_EPS) + decay * weight)
    return (weight_new, weight_new.astype(jnp.bfloat16), first_new, second_new)


def per_device(
    block_in,
    cotangent,
    buckets,
    qkv_weight,
    qkv_first,
    qkv_second,
    out_weight,
    out_first,
    out_second,
    up_weight,
    up_first,
    up_second,
    down_weight,
    down_first,
    down_second,
    norm_gains,
    gains_first,
    gains_second,
):
    low_type = jnp.bfloat16
    full_type = jnp.float32
    shards = (
        qkv_weight.astype(low_type),
        out_weight.astype(low_type),
        up_weight.astype(low_type),
        down_weight.astype(low_type),
        norm_gains.astype(low_type),
    )
    qkv_full, out_full, up_full, down_full, gain_full = (
        lax.all_gather(shards[0], "tok", axis=1, tiled=True),
        lax.all_gather(shards[1], "tok", axis=1, tiled=True),
        lax.all_gather(shards[2], "tok", axis=0, tiled=True),
        lax.all_gather(shards[3], "tok", axis=1, tiled=True),
        lax.all_gather(shards[4], "tok", axis=1, tiled=True),
    )
    gain_float = gain_full.astype(full_type)
    group = lax.axis_index("bkt")
    rows_dev = block_in.shape[0]
    residual_in = block_in.astype(full_type)
    normed_one, norm_pull_one = jax.vjp(rms_scale, residual_in, gain_float[0])
    seq_one = lax.all_gather(normed_one.astype(low_type), "bkt", axis=0, tiled=True)
    length = seq_one.shape[0]
    heads = qkv_full.shape[2] // HD
    project = jnp.einsum("td,cdh->cth", seq_one, qkv_full, preferred_element_type=full_type)
    query = project[0].reshape(length, heads, HD)
    keys = project[1].reshape(length, heads, HD)
    values = project[2].astype(low_type).reshape(length, heads, HD)
    cosine, sine = rotary_tables(length)

    def turn_both(first_part, second_part):
        return (rotate(first_part, cosine, sine), rotate(second_part, cosine, sine))

    turned, turn_pull = jax.vjp(turn_both, query, keys)
    query_turn = turned[0].astype(low_type)
    key_turn = turned[1].astype(low_type)
    block_rows = min(512, length)
    blocks = length // block_rows
    scale = HD ** (-0.5)
    key_place = jnp.arange(length)
    query_blocks = query_turn.reshape(blocks, block_rows, heads, HD)
    block_ids = jnp.arange(blocks)

    def block_scores(query_block, block_id):
        raw = (
            jnp.einsum("qhe,khe->hqk", query_block, key_turn, preferred_element_type=full_type)
            * scale
        )
        place = block_id * block_rows + jnp.arange(block_rows)
        return jnp.where((place[:, None] >= key_place[None, :])[None], raw, -1e30)

    def attend(item):
        query_block, block_id = item
        scores = block_scores(query_block, block_id)
        peak = jnp.max(scores, axis=-1, keepdims=True)
        expo = jnp.exp(scores - peak)
        total = jnp.sum(expo, axis=-1, keepdims=True)
        probs = (expo / total).astype(low_type)
        mixed_block = jnp.einsum("hqk,khe->qhe", probs, values, preferred_element_type=full_type)
        return (mixed_block, peak + jnp.log(total))

    mixed_blocks, log_totals = lax.map(attend, (query_blocks, block_ids))
    mixed = mixed_blocks.reshape(length, heads * HD).astype(low_type)
    piece = mixed
    middle = residual_in + lax.psum_scatter(
        jnp.dot(piece, out_full, preferred_element_type=full_type).astype(jnp.bfloat16),
        "bkt",
        scatter_dimension=0,
        tiled=True,
    ).astype(jnp.float32)
    normed_two, norm_pull_two = jax.vjp(rms_scale, middle, gain_float[1])
    own_rows = normed_two.astype(low_type)
    own_back = cotangent.astype(low_type)
    own_tags = jnp.full((rows_dev,), buckets[0].astype(low_type), low_type)
    seq_two, seq_tags, seq_back = (
        lax.all_gather(own_rows, "bkt", axis=0, tiled=True),
        lax.all_gather(own_tags, "bkt", axis=0, tiled=True),
        lax.all_gather(own_back, "bkt", axis=0, tiled=True),
    )
    live = (seq_tags.astype(full_type) >= group.astype(full_type)).astype(full_type)[:, None]
    inner = jnp.dot(seq_two, up_full, preferred_element_type=full_type)
    hidden = (jnp.square(jax.nn.relu(inner)) * live).astype(low_type)
    piece = hidden
    ffn_part = lax.psum_scatter(
        jnp.dot(piece, down_full, preferred_element_type=full_type).astype(jnp.bfloat16),
        "bkt",
        scatter_dimension=0,
        tiled=True,
    ).astype(jnp.float32)
    block_out = middle + ffn_part
    back_hidden = jnp.einsum("td,fd->tf", seq_back, down_full, preferred_element_type=full_type)
    back_inner = (back_hidden * 2.0 * jax.nn.relu(inner) * live).astype(low_type)
    up_grad = jnp.einsum("td,tf->df", seq_two, back_inner, preferred_element_type=full_type)
    down_grad = jnp.einsum("tf,td->fd", hidden, seq_back, preferred_element_type=full_type)
    piece = back_inner
    back_two = lax.psum_scatter(
        jnp.einsum("tf,df->td", piece, up_full, preferred_element_type=full_type).astype(
            jnp.bfloat16
        ),
        "bkt",
        scatter_dimension=0,
        tiled=True,
    ).astype(jnp.float32)
    middle_part, gain_grad_two = norm_pull_two(back_two)
    middle_grad = cotangent + middle_part
    seq_mid = lax.all_gather(middle_grad.astype(low_type), "bkt", axis=0, tiled=True)
    back_mixed = jnp.einsum(
        "td,hd->th", seq_mid, out_full, preferred_element_type=full_type
    ).astype(low_type)
    out_grad = jnp.einsum("th,td->hd", mixed, seq_mid, preferred_element_type=full_type)
    back_blocks = back_mixed.reshape(blocks, block_rows, heads, HD)

    def attend_back(carry, item):
        key_acc, value_acc = carry
        query_block, back_block, log_total, block_id = item
        scores = block_scores(query_block, block_id)
        probs = jnp.exp(scores - log_total)
        back_probs = jnp.einsum(
            "qhe,khe->hqk", back_block, values, preferred_element_type=full_type
        )
        centre = jnp.sum(probs * back_probs, axis=-1, keepdims=True)
        back_scores = (probs * (back_probs - centre)).astype(low_type)
        query_grad_block = (
            jnp.einsum("hqk,khe->qhe", back_scores, key_turn, preferred_element_type=full_type)
            * scale
        )
        key_acc = (
            key_acc
            + jnp.einsum("hqk,qhe->khe", back_scores, query_block, preferred_element_type=full_type)
            * scale
        )
        value_acc = value_acc + jnp.einsum(
            "hqk,qhe->khe", probs.astype(low_type), back_block, preferred_element_type=full_type
        )
        return ((key_acc, value_acc), query_grad_block)

    start_acc = jnp.zeros((length, heads, HD), full_type)
    (key_grad_turn, value_grad), query_grad_blocks = lax.scan(
        attend_back, (start_acc, start_acc), (query_blocks, back_blocks, log_totals, block_ids)
    )
    query_grad, key_grad = turn_pull((query_grad_blocks.reshape(length, heads, HD), key_grad_turn))
    back_project = jnp.stack(
        [
            query_grad.reshape(length, heads * HD),
            key_grad.reshape(length, heads * HD),
            value_grad.reshape(length, heads * HD),
        ]
    ).astype(low_type)
    qkv_grad = jnp.einsum("td,cth->cdh", seq_one, back_project, preferred_element_type=full_type)
    piece = back_project
    back_one = lax.psum_scatter(
        jnp.einsum("cth,cdh->td", piece, qkv_full, preferred_element_type=full_type).astype(
            jnp.bfloat16
        ),
        "bkt",
        scatter_dimension=0,
        tiled=True,
    ).astype(jnp.float32)
    in_part, gain_grad_one = norm_pull_one(back_one)
    block_in_grad = middle_grad + in_part
    gain_grad = jnp.stack([gain_grad_one, gain_grad_two])
    qkv_part, out_part, up_part, down_part = (
        lax.psum_scatter(
            qkv_grad.astype(jnp.bfloat16), "tok", scatter_dimension=1, tiled=True
        ).astype(jnp.float32),
        lax.psum_scatter(
            out_grad.astype(jnp.bfloat16), "tok", scatter_dimension=1, tiled=True
        ).astype(jnp.float32),
        lax.psum_scatter(
            up_grad.astype(jnp.bfloat16), "tok", scatter_dimension=0, tiled=True
        ).astype(jnp.float32),
        lax.psum_scatter(
            down_grad.astype(jnp.bfloat16), "tok", scatter_dimension=1, tiled=True
        ).astype(jnp.float32),
    )
    weight_squares = jnp.sum(qkv_part * qkv_part) + jnp.sum(out_part * out_part)
    weight_squares = weight_squares + jnp.sum(up_part * up_part) + jnp.sum(down_part * down_part)
    gain_total, all_squares = lax.psum((gain_grad, weight_squares), ("tok", "bkt"))
    total = all_squares + jnp.sum(gain_total * gain_total)
    grad_norm = jnp.sqrt(total)
    factor = jnp.minimum(1.0, CLIP_NORM / grad_norm)
    gain_width = norm_gains.shape[1]
    gain_part = lax.dynamic_slice_in_dim(
        gain_total, lax.axis_index("tok") * gain_width, gain_width, 1
    )
    qkv_out = adam_step(
        qkv_weight, qkv_part, qkv_first, qkv_second, factor, D ** (-0.5), DECAY_RATE
    )
    out_out = adam_step(
        out_weight, out_part, out_first, out_second, factor, (H * HD // 16) ** (-0.5), DECAY_RATE
    )
    up_out = adam_step(up_weight, up_part, up_first, up_second, factor, D ** (-0.5), DECAY_RATE)
    down_out = adam_step(
        down_weight, down_part, down_first, down_second, factor, FF ** (-0.5), DECAY_RATE
    )
    gain_out = adam_step(norm_gains, gain_part, gains_first, gains_second, factor, GAIN_RATE, 0.0)
    return (
        block_out,
        block_in_grad,
        grad_norm,
        qkv_out[0],
        qkv_out[1],
        qkv_out[2],
        qkv_out[3],
        out_out[0],
        out_out[1],
        out_out[2],
        out_out[3],
        up_out[0],
        up_out[1],
        up_out[2],
        up_out[3],
        down_out[0],
        down_out[1],
        down_out[2],
        down_out[3],
        gain_out[0],
        gain_out[1],
        gain_out[2],
        gain_out[3],
    )


def solution(mesh):
    return jax.shard_map(
        per_device,
        mesh=mesh,
        in_specs=(
            P(("tok", "bkt"), None),
            P(("tok", "bkt"), None),
            P("tok"),
            P(None, "tok", "bkt"),
            P(None, "tok", "bkt"),
            P(None, "tok", "bkt"),
            P("bkt", "tok"),
            P("bkt", "tok"),
            P("bkt", "tok"),
            P("tok", "bkt"),
            P("tok", "bkt"),
            P("tok", "bkt"),
            P("bkt", "tok"),
            P("bkt", "tok"),
            P("bkt", "tok"),
            P(None, "tok"),
            P(None, "tok"),
            P(None, "tok"),
        ),
        out_specs=(
            P(("tok", "bkt"), None),
            P(("tok", "bkt"), None),
            P(),
            P(None, "tok", "bkt"),
            P(None, "tok", "bkt"),
            P(None, "tok", "bkt"),
            P(None, "tok", "bkt"),
            P("bkt", "tok"),
            P("bkt", "tok"),
            P("bkt", "tok"),
            P("bkt", "tok"),
            P("tok", "bkt"),
            P("tok", "bkt"),
            P("tok", "bkt"),
            P("tok", "bkt"),
            P("bkt", "tok"),
            P("bkt", "tok"),
            P("bkt", "tok"),
            P("bkt", "tok"),
            P(None, "tok"),
            P(None, "tok"),
            P(None, "tok"),
            P(None, "tok"),
        ),
        check_vma=False,
    )
```

profile of v0, /device:TPU:0, one launch (start us, length us, event | category | flops | bytes accessed | tf_op | source)
XLA Modules:
  0.0 1264.2 jit_solution(16580294443447594086)
XLA Ops:
  34.4 70.0 %all-gather.10.cloned.1.call-done = bf16[1024,2048]{1,0:T(8,128)(2,1)} async-done(((bf16[256,2048]{1,0:T(8,128)(2,1)}), bf16[1024,2048]{1,0:T(8,128)(2,1)}) %all-gather.10.cloned.1.call-update) | async-done | bytes 4194320 | tf_op jit(solution)/shard_map/all_gather | solution.py:93
  104.4 47.6 %all-gather.12.cloned.1.call-done = bf16[3,2048,512]{1,2,0:T(8,128)(2,1)} async-done(((bf16[3,256,512]{1,2,0:T(8,128)(2,1)}), bf16[3,2048,512]{1,2,0:T(8,128)(2,1)}) %all-gather.12.cloned.1.call-update) | async-done | bytes 6291472 | tf_op jit(solution)/shard_map/all_gather | solution.py:82
  186.8 20.2 %while.28 = (s32[]{:T(128)}, bf16[2,512,4,128]{3,1,2,0:T(8,128)(2,1)}, f32[2,4,512,1]{2,1,3,0:T(4,128)S(1)}, s32[2]{0:T(128)S(1)}, bf16[2,512,4,128]{3,1,2,0:T(8...) while((s32[]{:T(128)}, ...), condition=%wide.region_4.5_spmd.clone, body=%wide.region_1.4_spmd.clone.sunk | while | flops 1099430400 | bytes 39391428 | solution.py:133
  220.0 74.0 %reduce-scatter.9.cloned.1.call-done = bf16[256,2048]{1,0:T(8,128)(2,1)} async-done(((bf16[1024,2048]{1,0:T(8,128)(2,1)}), bf16[256,2048]{1,0:T(8,128)(2,1)}) %reduce-scatter.9.cloned.1.call-update) | async-done | bytes 1048592 | tf_op jit(solution)/shard_map/reduce_scatter | solution.py:136
  313.7 37.7 %all-gather.18.cloned.1.call-done = bf16[2048,2048]{1,0:T(8,128)(2,1)} async-done(((bf16[256,2048]{1,0:T(8,128)(2,1)}), bf16[2048,2048]{1,0:T(8,128)(2,1)}) %all-gather.18.cloned.1.call-update) | async-done | bytes 8388624 | tf_op jit(solution)/shard_map/all_gather | solution.py:84
  351.5 82.9 %all-gather.16.cloned.1.call-done = bf16[1024,2048]{1,0:T(8,128)(2,1)} async-done(((bf16[256,2048]{1,0:T(8,128)(2,1)}), bf16[1024,2048]{1,0:T(8,128)(2,1)}) %all-gather.16.cloned.1.call-update) | async-done | bytes 4194320 | tf_op jit(solution)/shard_map/all_gather | solution.py:147
  434.3 14.6 %fusion.105 = f32[1024,2048]{1,0:T(8,128)} fusion(bf16[1024,2048]{1,0:T(8,128)(2,1)} %all-gather.16.cloned.1.call-done, bf16[2048,2048]{1,0:T(8,128)(2,1)} %all-gather.18.cloned.1.call-done), kind=kOutput, calls=%fused_computation.181 | convolution fusion | flops 8589934592 | bytes 20971520 | tf_op jit(solution)/shard_map/dot_general | solution.py:152
  448.9 67.0 %all-gather.22.cloned.1.call-done = bf16[1024,2048]{1,0:T(8,128)(2,1)} async-done(((bf16[256,2048]{1,0:T(8,128)(2,1)}), bf16[1024,2048]{1,0:T(8,128)(2,1)}) %all-gather.22.cloned.1.call-update) | async-done | bytes 4194320 | tf_op jit(solution)/shard_map/all_gather | solution.py:149
  515.9 57.1 %all-gather.20.cloned.1.call-done = bf16[2048,2048]{1,0:T(8,128)(2,1)} async-done(((bf16[2048,256]{1,0:T(8,128)(2,1)}), bf16[2048,2048]{1,0:T(8,128)(2,1)}) %all-gather.20.cloned.1.call-update) | async-done | bytes 8388624 | tf_op jit(solution)/shard_map/all_gather | solution.py:85
  573.0 14.1 %multiply_convert_fusion.1 = bf16[1024,2048]{1,0:T(8,128)(2,1)S(1)} fusion(f32[1024,2048]{1,0:T(8,128)} %fusion.105, bf16[1024,2048]{1,0:T(8,128)(2,1)} %all-gather.22.cloned.1.call-done, bf16[2048,2048]{1,0:T(8,128)(2,1)} %all-gather.20.cloned.1.call-done, f32[1024]{0:T(1024)S(1)} %bitcast.163), kind=kOutput, calls=%fused_computation.49 | convolution fusion | flops 8600420352 | bytes 25169920 | tf_op jit(solution)/shard_map/td,fd->tf/dot_general | solution.py:162
  599.8 76.7 %reduce-scatter.13.cloned.1.call-done = bf16[256,2048]{1,0:T(8,128)(2,1)} async-done(((bf16[1024,2048]{1,0:T(8,128)(2,1)}), bf16[256,2048]{1,0:T(8,128)(2,1)}) %reduce-scatter.13.cloned.1.call-update) | async-done | bytes 1048592 | tf_op jit(solution)/shard_map/reduce_scatter | solution.py:167
  681.8 14.2 %convolution_convert_fusion.1 = bf16[2048,2048]{1,0:T(8,128)(2,1)} fusion(bf16[1024,2048]{1,0:T(8,128)(2,1)} %all-gather.16.cloned.1.call-done, bf16[1024,2048]{1,0:T(8,128)(2,1)} %copy-done.60), kind=kOutput, calls=%fused_computation.52 | convolution fusion | flops 8594128896 | bytes 16777216 | tf_op jit(solution)/shard_map/td,tf->df/dot_general | solution.py:164
  696.1 15.0 %convolution_convert_fusion = bf16[2048,2048]{1,0:T(8,128)(2,1)} fusion(bf16[1024,2048]{1,0:T(8,128)(2,1)} %all-gather.22.cloned.1.call-done, f32[1024,2048]{1,0:T(8,128)} %fusion.105, f32[1024]{0:T(1024)S(1)} %bitcast.164), kind=kOutput, calls=%fused_computation.51 | convolution fusion | flops 8602517504 | bytes 20975616 | tf_op jit(solution)/shard_map/tf,td->fd/dot_general | solution.py:165
  711.6 51.6 %all-gather.24.cloned.1.call-done = bf16[1024,2048]{1,0:T(8,128)(2,1)} async-done(((bf16[256,2048]{1,0:T(8,128)(2,1)}), bf16[1024,2048]{1,0:T(8,128)(2,1)}) %all-gather.24.cloned.1.call-update) | async-done | bytes 4194320 | tf_op jit(solution)/shard_map/all_gather | solution.py:177
  771.6 39.8 %while.29 = (s32[]{:T(128)}, f32[1024,4,128]{0,2,1:T(8,128)S(1)}, f32[1024,4,128]{0,2,1:T(8,128)}, f32[2,512,4,128]{3,1,0,2:T(8,128)}, bf16[2,512,4,128]{3,1,2,0...) while((s32[]{:T(128)}, f32[1024,4,128]{0,2,1:T(8,128)S(1)}, ...), condition=%wide.region_12.13_spmd.clone, body=%wide.region_10.12_spmd.clone.sunk | while | flops 2719218176 | bytes 105967912 | solution.py:209
  838.7 11.1 bitcast_convert_fusion
  851.3 11.6 convert_bitcast_fusion
  863.6 16.2 %convolution_convert_fusion.3 = bf16[1024,2048]{1,0:T(8,128)(2,1)} fusion(bf16[2048,2048]{1,0:T(8,128)(2,1)} %all-gather.20.cloned.1.call-done, f32[1024,2048]{1,0:T(8,128)} %fusion.105, f32[1024]{0:T(1024)S(1)} %bitcast.165), kind=kOutput, calls=%fused_computation.63 | convolution fusion | flops 8600420352 | bytes 20975616 | tf_op jit(solution)/shard_map/dot_general | solution.py:156
  887.0 24.5 %reduce-scatter.23.cloned.1.call-done = bf16[2048,256]{1,0:T(8,128)(2,1)} async-done(((bf16[2048,2048]{1,0:T(8,128)(2,1)}), bf16[2048,256]{1,0:T(8,128)(2,1)}) %reduce-scatter.23.cloned.1.call-update) | async-done | bytes 1048592 | tf_op jit(solution)/shard_map/reduce_scatter | solution.py:243
  913.9 42.7 %reduce-scatter.19.cloned.1.call-done = bf16[512,256]{1,0:T(8,128)(2,1)} async-done(((bf16[512,2048]{1,0:T(8,128)(2,1)}), bf16[512,256]{1,0:T(8,128)(2,1)}) %reduce-scatter.19.cloned.1.call-update) | async-done | bytes 262160 | tf_op jit(solution)/shard_map/reduce_scatter | solution.py:237
  958.3 77.4 %reduce-scatter.15.cloned.1.call-done = bf16[256,2048]{1,0:T(8,128)(2,1)} async-done(((bf16[1024,2048]{1,0:T(8,128)(2,1)}), bf16[256,2048]{1,0:T(8,128)(2,1)}) %reduce-scatter.15.cloned.1.call-update) | async-done | bytes 1048592 | tf_op jit(solution)/shard_map/reduce_scatter | solution.py:222
  1038.0 63.2 %reduce-scatter.17.cloned.1.call-done = bf16[3,256,512]{1,2,0:T(8,128)(2,1)} async-done(((bf16[3,2048,512]{1,2,0:T(8,128)(2,1)}), bf16[3,256,512]{1,2,0:T(8,128)(2,1)}) %reduce-scatter.17.cloned.1.call-update) | async-done | bytes 786448 | tf_op jit(solution)/shard_map/reduce_scatter | solution.py:234
  1105.9 74.3 %reduce-scatter.11.cloned.1.call-done = bf16[256,2048]{1,0:T(8,128)(2,1)} async-done(((bf16[1024,2048]{1,0:T(8,128)(2,1)}), bf16[256,2048]{1,0:T(8,128)(2,1)}) %reduce-scatter.11.cloned.1.call-update) | async-done | bytes 1048592 | tf_op jit(solution)/shard_map/reduce_scatter | solution.py:155
  1185.8 41.3 %all-reduce.4 = (f32[]{:T(128)}, f32[2,2048]{1,0:T(2,128)S(1)}) all-reduce(f32[]{:T(128)S(6)} %add.215, f32[2,2048]{1,0:T(2,128)S(1)} %pad_maximum_fusion.7), channel_id=1, replica_groups=mesh['tok'=8,'bkt'=4] {'tok','bkt'}, use_global_device_ids=true, to_apply=%region_23.24 | all-reduce | flops 4097 | bytes 32776 | tf_op jit(solution)/shard_map/psum | solution.py:249
  (289 shorter events, 255.7 us)
Async XLA Ops:
  7.2 97.2 %all-gather.10.cloned.1.call-start = ((), (), s32[]{:S(2)}) async-start(), calls=%async_computation.8 | async-start | bytes 5242880 | tf_op jit(solution)/shard_map/all_gather | solution.py:93
  20.0 659.5 %copy-start.41 = (f32[1,2048]{1,0:T(1,128)}, f32[1,2048]{1,0:T(1,128)S(1)}, u32[]{:S(2)}) copy-start(f32[1,2048]{1,0:T(1,128)S(1)} %get-tuple-element.381) | copy-start | bytes 24580
  23.1 128.9 %all-gather.12.cloned.1.call-start = ((), (), s32[]{:S(2)}) async-start(), calls=%async_computation.9 | async-start | bytes 7077888 | tf_op jit(solution)/shard_map/all_gather | solution.py:82
  24.6 186.1 %all-gather.14.cloned.1.call-start = ((), (), s32[]{:S(2)}) async-start(), calls=%async_computation.10 | async-start | bytes 2359296 | tf_op jit(solution)/shard_map/all_gather | solution.py:83
  25.8 268.2 %reduce-scatter.9.cloned.1.call-start = ((), (), s32[]{:S(2)}) async-start(), calls=%async_computation.11 | async-start | bytes 5242880 | tf_op jit(solution)/shard_map/reduce_scatter | solution.py:136
  217.1 134.3 %all-gather.18.cloned.1.call-start = ((), (), s32[]{:S(2)}) async-start(), calls=%async_computation.13 | async-start | bytes 9437184 | tf_op jit(solution)/shard_map/all_gather | solution.py:84
  220.0 214.4 %all-gather.16.cloned.1.call-start = ((), (), s32[]{:S(2)}) async-start(), calls=%async_computation.12 | async-start | bytes 5242880 | tf_op jit(solution)/shard_map/all_gather | solution.py:147
  295.8 383.6 %copy-start.46 = (f32[256]{0:T(256)}, f32[256]{0:T(256)S(1)}, u32[]{:S(2)}) copy-start(f32[256]{0:T(256)S(1)} %fusion.83) | copy-start | bytes 3076
  297.3 218.6 %all-gather.22.cloned.1.call-start = ((), (), s32[]{:S(2)}) async-start(), calls=%async_computation.16 | async-start | bytes 5242880 | tf_op jit(solution)/shard_map/all_gather | solution.py:149
  300.1 272.9 %all-gather.20.cloned.1.call-start = ((), (), s32[]{:S(2)}) async-start(), calls=%async_computation.14 | async-start | bytes 9437184 | tf_op jit(solution)/shard_map/all_gather | solution.py:85
  302.9 373.6 %reduce-scatter.13.cloned.1.call-start = ((), (), s32[]{:S(2)}) async-start(), calls=%async_computation.17 | async-start | bytes 5242880 | tf_op jit(solution)/shard_map/reduce_scatter | solution.py:167
  313.7 382.4 %copy-start.55 = (f32[4,1,256]{2,1,0:T(1,128)}, f32[4,1,256]{2,1,0:T(1,128)S(1)}, u32[]{:S(2)}) copy-start(f32[4,1,256]{2,1,0:T(1,128)S(1)} %compare_convert_fusion) | copy-start | bytes 12292
  599.6 163.7 %all-gather.24.cloned.1.call-start = ((), (), s32[]{:S(2)}) async-start(), calls=%async_computation.18 | async-start | bytes 5242880 | tf_op jit(solution)/shard_map/all_gather | solution.py:177
  681.8 202.8 %reduce-scatter.21.cloned.1.call-start = ((), (), s32[]{:S(2)}) async-start(), calls=%async_computation.22 | async-start | bytes 9437184 | tf_op jit(solution)/shard_map/reduce_scatter | solution.py:240
  696.0 215.5 %reduce-scatter.23.cloned.1.call-start = ((), (), s32[]{:S(2)}) async-start(), calls=%async_computation.23 | async-start | bytes 9437184 | tf_op jit(solution)/shard_map/reduce_scatter | solution.py:243
  711.1 245.5 %reduce-scatter.19.cloned.1.call-start = ((), (), s32[]{:S(2)}) async-start(), calls=%async_computation.21 | async-start | bytes 2359296 | tf_op jit(solution)/shard_map/reduce_scatter | solution.py:237
  819.2 216.5 %reduce-scatter.15.cloned.1.call-start = ((), (), s32[]{:S(2)}) async-start(), calls=%async_computation.19 | async-start | bytes 5242880 | tf_op jit(solution)/shard_map/reduce_scatter | solution.py:222
  849.9 251.3 %reduce-scatter.17.cloned.1.call-start = ((), (), s32[]{:S(2)}) async-start(), calls=%async_computation.20 | async-start | bytes 7077888 | tf_op jit(solution)/shard_map/reduce_scatter | solution.py:234
  862.9 317.3 %reduce-scatter.11.cloned.1.call-start = ((), (), s32[]{:S(2)}) async-start(), calls=%async_computation.15 | async-start | bytes 5242880 | tf_op jit(solution)/shard_map/reduce_scatter | solution.py:155
  887.0 293.2 %copy-start.8 = (bf16[256,2048]{1,0:T(8,128)(2,1)S(1)}, bf16[256,2048]{1,0:T(8,128)(2,1)}, u32[]{:S(2)}) copy-start(bf16[256,2048]{1,0:T(8,128)(2,1)} %reduce-scatter.9.cloned.1.call-done) | copy-start | bytes 3145732
  887.0 293.2 %copy-start.13 = (bf16[256,2048]{1,0:T(8,128)(2,1)S(1)}, bf16[256,2048]{1,0:T(8,128)(2,1)}, u32[]{:S(2)}) copy-start(bf16[256,2048]{1,0:T(8,128)(2,1)} %reduce-scatter.13.cloned.1.call-done) | copy-start | bytes 3145732
  887.0 293.2 %copy-start.42 = (f32[1,2048]{1,0:T(1,128)S(1)}, f32[1,2048]{1,0:T(1,128)}, u32[]{:S(2)}) copy-start(f32[1,2048]{1,0:T(1,128)} %copy-done.41) | copy-start | bytes 24580
  887.0 293.2 %copy-start.47 = (f32[256]{0:T(256)S(1)}, f32[256]{0:T(256)}, u32[]{:S(2)}) copy-start(f32[256]{0:T(256)} %copy-done.46) | copy-start | bytes 3076
  887.0 293.2 %copy-start.53 = (f32[256]{0:T(256)S(1)}, f32[256]{0:T(256)}, u32[]{:S(2)}) copy-start(f32[256]{0:T(256)} %copy-done.52) | copy-start | bytes 3076
  (59 other events, 1031.6 us)
Sparse Core Ops, SparseCore 0:
  23.2 81.1 all-gather.9
  106.8 45.1 all-gather.11
  154.4 28.1 all-gather.13
  217.2 76.7 reduce-scatter.8
  296.5 54.8 all-gather.17
  353.5 80.7 all-gather.15
  436.6 79.2 all-gather.21
  518.5 54.4 all-gather.19
  599.7 76.7 reduce-scatter.12
  681.9 81.2 all-gather.23
  766.7 69.7 reduce-scatter.20
  840.2 71.2 reduce-scatter.22
  915.4 41.1 reduce-scatter.18
  958.9 76.7 reduce-scatter.14
  1038.9 62.2 reduce-scatter.16
  1103.4 76.7 reduce-scatter.10
where the time goes:
time: 1270 us; the launch traced here: 1260 us
  waiting for transfers between devices  847 us (67%)
  matrix products  172 us (14%)
  other arithmetic  98.7 us (8%)
  blocking collectives  61.8 us (5%)
  local copies, waits for them, and re-layouts  60 us (5%)
  between operations  20.8 us (2%)
    all_gather x1, waiting for transfers between devices, per_device(): lax.all_gather(own_rows, 'bkt', axis=0, tiled=True)  82.9 us
    reduce_scatter x1, waiting for transfers between devices, per_device(): lax.psum_scatter(jnp.einsum('cth,cdh->td', piece, qkv_full, preferred_ele...  77.4 us
    reduce_scatter x1, waiting for transfers between devices, per_device(): lax.psum_scatter(jnp.einsum('tf,df->td', piece, up_full, preferred_elemen...  76.7 us
    reduce_scatter x1, waiting for transfers between devices, per_device(): lax.psum_scatter(jnp.dot(piece, down_full, preferred_element_type=full_ty...  74.3 us
    reduce_scatter x1, waiting for transfers between devices, per_device(): lax.psum_scatter(jnp.dot(piece, out_full, preferred_element_type=full_typ...  74 us
    all_gather x1, waiting for transfers between devices, per_device(): lax.all_gather(normed_one.astype(low_type), 'bkt', axis=0, tiled=True)  70 us
    all_gather x1, waiting for transfers between devices, per_device(): lax.all_gather(own_back, 'bkt', axis=0, tiled=True)  67 us
    reduce_scatter x1, waiting for transfers between devices, per_device(): lax.psum_scatter(qkv_grad.astype(jnp.bfloat16), 'tok', scatter_dimension=...  63.2 us
  transfers between devices with their start and end apart: 16, of which 14 were waited for; matrix products, arithmetic and copies ran while one was open for 19% of the time, Pallas kernels for 0%

commit v1 on v0

v1 whole, which is shorter than its diff:
```python
import functools
import jax
import jax.numpy as jnp
from jax import lax
from jax.experimental import pallas as pl
from jax.experimental.pallas import tpu as pltpu
from jax.sharding import PartitionSpec as P

D = 2048
H = 16
HD = 128
FF = 8192
STEP = 10

NORM_EPS = 1e-05
ADAM_EPS = 1e-08
CLIP_NORM = 1.0
BETA_ONE = 0.9
BETA_TWO = 0.95
DECAY_RATE = 0.1
GAIN_RATE = 0.3
ROPE_BASE = 10000.0

LOW = jnp.bfloat16
FULL = jnp.float32
SCALE = HD ** (-0.5)
VMEM_BYTES = 48 * 1024 * 1024
NT = (((1,), (1,)), ((), ()))
TN = (((0,), (0,)), ((), ()))


def rotary_tables(length):
    positions = jnp.arange(length).astype(FULL)[:, None]
    freq_index = jnp.arange(HD // 2).astype(FULL)
    angles = positions * (ROPE_BASE ** (-2.0 * freq_index / HD))[None, :]
    cosine = jnp.cos(angles)
    sine = jnp.sin(angles)
    return (jnp.concatenate([cosine, cosine], axis=-1), jnp.concatenate([-sine, sine], axis=-1))


def params(vmem=VMEM_BYTES):
    return pltpu.CompilerParams(vmem_limit_bytes=vmem)


def project_body(place_ref, x_ref, gain_ref, w_ref, cos_ref, sin_ref, *rest):
    normed_ref, out_ref, seq_ref = rest[-3:]
    part = pl.program_id(0)

    @pl.when(part == 0)
    def _():
        low = x_ref[...]
        seq_ref[...] = low
        values = low.astype(FULL)
        inverse = lax.rsqrt(jnp.mean(values * values, axis=-1, keepdims=True) + NORM_EPS)
        normed_ref[...] = (values * inverse * gain_ref[...]).astype(LOW)

    product = jnp.dot(normed_ref[...], w_ref[0], preferred_element_type=FULL)

    @pl.when(part < 2)
    def _():
        for head in range(product.shape[1] // HD):
            one = product[:, head * HD : (head + 1) * HD]
            turned = one * cos_ref[...] + pltpu.roll(one, HD // 2, 1) * sin_ref[...]
            out_ref[0, :, head * HD : (head + 1) * HD] = turned.astype(LOW)

    @pl.when(part == 2)
    def _():
        out_ref[0] = product.astype(LOW)


def project(place, x, gain, weight, cosine, sine, carried):
    rows, width = x.shape
    length = cosine.shape[0]
    cols = weight.shape[2]
    shapes = [
        jax.ShapeDtypeStruct((length, width), LOW),
        jax.ShapeDtypeStruct((3, length, cols), LOW),
        jax.ShapeDtypeStruct((length, width), LOW),
    ]
    in_specs = [
        pl.BlockSpec((rows, width), lambda c, p: (0, 0)),
        pl.BlockSpec((1, width), lambda c, p: (0, 0)),
        pl.BlockSpec((1, width, cols), lambda c, p: (c, 0, 0)),
        pl.BlockSpec((rows, HD), lambda c, p: (p[0], 0)),
        pl.BlockSpec((rows, HD), lambda c, p: (p[0], 0)),
    ]
    aliases = {}
    if carried is not None:
        in_specs += [pl.BlockSpec(memory_space=pl.ANY)] * 3
        aliases = {6: 0, 7: 1, 8: 2}
    return pl.pallas_call(
        project_body,
        grid_spec=pltpu.PrefetchScalarGridSpec(
            num_scalar_prefetch=1,
            grid=(3,),
            in_specs=in_specs,
            out_specs=[
                pl.BlockSpec((rows, width), lambda c, p: (p[0], 0)),
                pl.BlockSpec((1, rows, cols), lambda c, p: (c, p[0], 0)),
                pl.BlockSpec((rows, width), lambda c, p: (p[0], 0)),
            ],
        ),
        out_shape=shapes,
        input_output_aliases=aliases,
        compiler_params=params(),
        cost_estimate=pl.CostEstimate(
            flops=2 * rows * width * cols * 3, bytes_accessed=3 * width * cols * 2, transcendentals=0
        ),
    )(place, x, gain, weight, cosine, sine, *(carried or ()))


def attend_body(half, blocks, q_ref, k_ref, v_ref, mixed_ref, log_ref):
    length = q_ref.shape[1]
    block = length // blocks
    rows = block // 2
    for index in range(blocks):
        first = index * block + half * rows
        last = first + rows
        query = q_ref[0, first:last]
        scores = (
            lax.dot_general(query, k_ref[0, :last], NT, preferred_element_type=FULL) * SCALE
        )
        row = lax.broadcasted_iota(jnp.int32, scores.shape, 0) + first
        col = lax.broadcasted_iota(jnp.int32, scores.shape, 1)
        scores = jnp.where(row >= col, scores, -1e30)
        peak = jnp.max(scores, axis=-1, keepdims=True)
        expo = jnp.exp(scores - peak)
        total = jnp.sum(expo, axis=-1, keepdims=True)
        probs = (expo / total).astype(LOW)
        mixed = jnp.dot(probs, v_ref[0, :last], preferred_element_type=FULL)
        mixed_ref[index * rows : (index + 1) * rows] = mixed.astype(LOW)
        log_ref[index * rows : (index + 1) * rows] = jnp.broadcast_to(
            peak + jnp.log(total), (rows, HD)
        )


def attend(half, blocks, qkv):
    _, length, cols = qkv.shape
    heads = cols // HD
    return pl.pallas_call(
        functools.partial(attend_body, half, blocks),
        grid=(heads,),
        in_specs=[
            pl.BlockSpec((1, length, HD), lambda h: (0, 0, h)),
            pl.BlockSpec((1, length, HD), lambda h: (1, 0, h)),
            pl.BlockSpec((1, length, HD), lambda h: (2, 0, h)),
        ],
        out_specs=[
            pl.BlockSpec((length // 2, HD), lambda h: (0, h)),
            pl.BlockSpec((length // 2, HD), lambda h: (0, h)),
        ],
        out_shape=[
            jax.ShapeDtypeStruct((length // 2, cols), LOW),
            jax.ShapeDtypeStruct((length // 2, cols), FULL),
        ],
        compiler_params=params(),
        cost_estimate=pl.CostEstimate(
            flops=2 * length * length * cols, bytes_accessed=8 * length * cols, transcendentals=length * length * 2
        ),
    )(qkv, qkv, qkv)


def attend_back_body(
    blocks, q_ref, k_ref, v_ref, back_ref, log_a_ref, log_b_ref, cos_ref, sin_ref, out_ref, key_acc, value_acc
):
    length = q_ref.shape[1]
    block = length // blocks
    rows = block // 2

    def turn_back(one, cosine, sine):
        return one * cosine - pltpu.roll(one, HD // 2, 1) * sine

    for index in range(blocks):
        first, last = index * block, (index + 1) * block
        query = q_ref[0, first:last]
        back = back_ref[first:last]
        keys = k_ref[0, :last]
        log_total = jnp.concatenate(
            [
                log_a_ref[index * rows : (index + 1) * rows, :1],
                log_b_ref[index * rows : (index + 1) * rows, :1],
            ],
            axis=0,
        )
        scores = lax.dot_general(query, keys, NT, preferred_element_type=FULL) * SCALE
        row = lax.broadcasted_iota(jnp.int32, scores.shape, 0) + first
        col = lax.broadcasted_iota(jnp.int32, scores.shape, 1)
        probs = jnp.exp(jnp.where(row >= col, scores, -1e30) - log_total)
        back_probs = lax.dot_general(back, v_ref[0, :last], NT, preferred_element_type=FULL)
        centre = jnp.sum(probs * back_probs, axis=-1, keepdims=True)
        back_scores = (probs * (back_probs - centre)).astype(LOW)
        query_grad = jnp.dot(back_scores, keys, preferred_element_type=FULL) * SCALE
        out_ref[0, first:last] = turn_back(query_grad, cos_ref[first:last], sin_ref[first:last]).astype(LOW)
        key_part = lax.dot_general(back_scores, query, TN, preferred_element_type=FULL)
        value_part = lax.dot_general(probs.astype(LOW), back, TN, preferred_element_type=FULL)
        if index > 0:
            key_acc[:first] += key_part[:first]
            value_acc[:first] += value_part[:first]
        key_acc[first:last] = key_part[first:]
        value_acc[first:last] = value_part[first:]
    out_ref[1] = turn_back(key_acc[...] * SCALE, cos_ref[...], sin_ref[...]).astype(LOW)
    out_ref[2] = value_acc[...].astype(LOW)


def attend_back(blocks, qkv, back, log_a, log_b, cosine, sine):
    _, length, cols = qkv.shape
    heads = cols // HD
    column = lambda h: (0, h)
    return pl.pallas_call(
        functools.partial(attend_back_body, blocks),
        grid=(heads,),
        in_specs=[
            pl.BlockSpec((1, length, HD), lambda h: (0, 0, h)),
            pl.BlockSpec((1, length, HD), lambda h: (1, 0, h)),
            pl.BlockSpec((1, length, HD), lambda h: (2, 0, h)),
            pl.BlockSpec((length, HD), column),
            pl.BlockSpec((length // 2, HD), column),
            pl.BlockSpec((length // 2, HD), column),
            pl.BlockSpec((length, HD), lambda h: (0, 0)),
            pl.BlockSpec((length, HD), lambda h: (0, 0)),
        ],
        out_specs=pl.BlockSpec((3, length, HD), lambda h: (0, 0, h)),
        out_shape=jax.ShapeDtypeStruct((3, length, cols), LOW),
        scratch_shapes=[pltpu.VMEM((length, HD), FULL), pltpu.VMEM((length, HD), FULL)],
        compiler_params=params(),
        cost_estimate=pl.CostEstimate(
            flops=5 * length * length * cols, bytes_accessed=14 * length * cols, transcendentals=length * length * 4
        ),
    )(qkv, qkv, qkv, back, log_a, log_b, cosine, sine)


def adam_step(weight, grad, first, second, factor, rate, decay):
    clipped = grad * factor
    first_new = BETA_ONE * first + (1.0 - BETA_ONE) * clipped
    second_new = BETA_TWO * second + (1.0 - BETA_TWO) * clipped * clipped
    first_hat = first_new / (1.0 - BETA_ONE**STEP)
    second_hat = second_new / (1.0 - BETA_TWO**STEP)
    weight_new = weight - rate * (first_hat / (jnp.sqrt(second_hat) + ADAM_EPS) + decay * weight)
    return (weight_new, weight_new.astype(LOW), first_new, second_new)


def per_device(
    toks,
    bkts,
    block_in,
    cotangent,
    buckets,
    qkv_weight,
    qkv_first,
    qkv_second,
    out_weight,
    out_first,
    out_second,
    up_weight,
    up_first,
    up_second,
    down_weight,
    down_first,
    down_second,
    norm_gains,
    gains_first,
    gains_second,
):
    group = lax.axis_index("bkt")
    rows, width = block_in.shape
    half = rows // 2
    length = rows * bkts
    ring = [(i, (i + 1) % bkts) for i in range(bkts)]

    def pass_on(value):
        return lax.ppermute(value, "bkt", ring)

    def owner(step):
        return lax.rem(group - step + bkts, bkts)

    def ring_gather(value):
        held = [value]
        for _ in range(bkts - 1):
            held.append(pass_on(held[-1]))
        return held

    def ring_sum(part_of):
        total = part_of(owner(1)).astype(LOW)
        for step in range(1, bkts):
            total = pass_on(total).astype(FULL) + part_of(owner(step + 1)).astype(FULL)
            if step < bkts - 1:
                total = total.astype(LOW)
        return total

    qkv_full = lax.all_gather(qkv_weight.astype(LOW), "tok", axis=1, tiled=True)
    gain_float = lax.all_gather(norm_gains.astype(LOW), "tok", axis=1, tiled=True).astype(FULL)
    x_held = ring_gather(block_in)
    out_held = ring_gather(out_weight.astype(LOW))
    out_depth, out_width = out_weight.shape
    out_line = jnp.zeros((bkts, out_depth, out_width), LOW)
    for step in range(bkts):
        out_line = lax.dynamic_update_slice(out_line, out_held[step][None], (owner(step), 0, 0))
    out_full = lax.all_gather(out_line.reshape(bkts * out_depth, out_width), "tok", axis=1, tiled=True)
    up_full = lax.all_gather(up_weight.astype(LOW), "tok", axis=0, tiled=True)
    down_full = lax.all_gather(down_weight.astype(LOW), "tok", axis=1, tiled=True)
    cosine, sine = rotary_tables(length)

    carried = None
    for step in range(bkts):
        carried = project(
            owner(step).reshape(1), x_held[step], gain_float[0:1], qkv_full, cosine, sine, carried
        )
    normed_one, qkv, seq_in = carried
    cols = qkv.shape[2]

    back_held = ring_gather(cotangent.astype(LOW))
    seq_back = jnp.zeros((bkts, rows, width), LOW)
    for step in range(bkts):
        seq_back = lax.dynamic_update_slice(seq_back, back_held[step][None], (owner(step), 0, 0))
    seq_in = seq_in.reshape(bkts, rows, width)

    live = (buckets[0] >= group).astype(FULL)
    mixed_own, logs, own_middle, own_two = [], [], [], []
    normed_two, hidden, back_inner, back_half = [], [], [], []
    mixed_halves, middles, back_twos = [], [], []
    for part in range(2):
        mixed, log_total = attend(part, bkts, qkv)
        logs.append(log_total)
        mixed_held = ring_gather(mixed)
        acc = seq_in[:, part * half : (part + 1) * half].reshape(bkts * half, width).astype(FULL)
        own_cols = []
        for step in range(bkts):
            weight = lax.dynamic_slice_in_dim(out_full, owner(step) * cols, cols, 0)
            acc = acc + jnp.dot(mixed_held[step], weight, preferred_element_type=FULL)
            own_cols.append(lax.dynamic_slice_in_dim(mixed_held[step], group * half, half, 0))
        mixed_rows = jnp.zeros((half, bkts * cols), LOW)
        for step in range(bkts):
            mixed_rows = lax.dynamic_update_slice(mixed_rows, own_cols[step], (0, owner(step) * cols))
        mixed_halves.append(mixed_rows)
        middles.append(lax.dynamic_slice_in_dim(acc, group * half, half, 0))
        inverse = lax.rsqrt(jnp.mean(acc * acc, axis=-1, keepdims=True) + NORM_EPS)
        normed = (acc * inverse * gain_float[1]).astype(LOW)
        normed_two.append(normed)
        inner = jax.nn.relu(jnp.dot(normed, up_full, preferred_element_type=FULL))
        hidden.append((inner * inner * live).astype(LOW))
        back_low = seq_back[:, part * half : (part + 1) * half].reshape(bkts * half, width)
        back_half.append(back_low)
        back_hidden = lax.dot_general(back_low, down_full, NT, preferred_element_type=FULL)
        back_inner.append((back_hidden * 2.0 * inner * live).astype(LOW))
        back_two_part = lax.dot_general(back_inner[-1], up_full, NT, preferred_element_type=FULL).astype(LOW)
        back_twos.append(
            ring_sum(lambda place: lax.dynamic_slice_in_dim(back_two_part, place * half, half, 0))
        )
    middle = jnp.concatenate(middles)
    back_two = jnp.concatenate(back_twos)
    mixed_rows = jnp.concatenate(mixed_halves)
    normed_two = jnp.concatenate(normed_two)
    back_inner = jnp.concatenate(back_inner)
    hidden = jnp.concatenate(hidden)
    back_half = jnp.concatenate(back_half)

    inverse = lax.rsqrt(jnp.mean(middle * middle, axis=-1, keepdims=True) + NORM_EPS)
    normal = middle * inverse
    scaled = gain_float[1] * back_two
    middle_grad = cotangent + inverse * (
        scaled - normal * jnp.mean(normal * scaled, axis=-1, keepdims=True)
    )
    gain_grad_two = jnp.sum(back_two * normal, axis=0)
    middle_low = middle_grad.astype(LOW)
    back_mixed = lax.dot_general(middle_low, out_full, NT, preferred_element_type=FULL).astype(LOW)
    back_seq = jnp.zeros((bkts, rows, cols), LOW)
    for step in range(bkts):
        piece = lax.dynamic_slice_in_dim(back_mixed, lax.rem(group + step, bkts) * cols, cols, 1)
        if step > 0:
            piece = lax.ppermute(piece, "bkt", [(i, (i + step) % bkts) for i in range(bkts)])
        back_seq = lax.dynamic_update_slice(back_seq, piece[None], (owner(step), 0, 0))

    up_grad = lax.dot_general(normed_two, back_inner, TN, preferred_element_type=FULL).astype(LOW)
    up_part = lax.psum_scatter(up_grad, "tok", scatter_dimension=0, tiled=True).astype(FULL)
    down_grad = lax.dot_general(hidden, back_half, TN, preferred_element_type=FULL).astype(LOW)
    down_part = lax.psum_scatter(down_grad, "tok", scatter_dimension=1, tiled=True).astype(FULL)
    out_grad = lax.dot_general(mixed_rows, middle_low, TN, preferred_element_type=FULL).astype(LOW)
    out_sum = lax.psum_scatter(out_grad, "tok", scatter_dimension=1, tiled=True)
    out_part = ring_sum(lambda place: lax.dynamic_slice_in_dim(out_sum, place * out_depth, out_depth, 0))

    down_prod = jnp.dot(hidden, down_full, preferred_element_type=FULL).astype(LOW)
    down_prod = down_prod.reshape(2, bkts, half, width)
    ffn_part = ring_sum(lambda place: lax.dynamic_slice_in_dim(down_prod, place, 1, 1)[:, 0])
    block_out = middle + ffn_part.reshape(rows, width)

    back_project = attend_back(
        bkts, qkv, back_seq.reshape(length, cols), logs[0], logs[1], cosine, sine
    )

    def back_one_part(place):
        piece = lax.dynamic_slice_in_dim(back_project, place * rows, rows, 1)
        return jnp.einsum("cth,cdh->td", piece, qkv_full, preferred_element_type=FULL)

    back_one = ring_sum(back_one_part)
    qkv_grad = jnp.einsum("td,cth->cdh", normed_one, back_project, preferred_element_type=FULL)
    qkv_part = lax.psum_scatter(
        qkv_grad.astype(LOW), "tok", scatter_dimension=1, tiled=True
    ).astype(FULL)
    residual_in = block_in.astype(FULL)
    inverse = lax.rsqrt(jnp.mean(residual_in * residual_in, axis=-1, keepdims=True) + NORM_EPS)
    normal = residual_in * inverse
    scaled = gain_float[0] * back_one
    block_in_grad = middle_grad + inverse * (
        scaled - normal * jnp.mean(normal * scaled, axis=-1, keepdims=True)
    )
    gain_grad_one = jnp.sum(back_one * normal, axis=0)

    weight_squares = jnp.sum(qkv_part * qkv_part) + jnp.sum(out_part * out_part)
    weight_squares = weight_squares + jnp.sum(up_part * up_part) + jnp.sum(down_part * down_part)
    packed = jnp.concatenate(
        [gain_grad_one, gain_grad_two, jnp.broadcast_to(weight_squares, (HD,))]
    )
    for axis, size in (("tok", toks), ("bkt", bkts)):
        if size & (size - 1):
            packed = lax.psum(packed, axis)
        else:
            step = 1
            while step < size:
                packed = packed + lax.ppermute(packed, axis, [(i, i ^ step) for i in range(size)])
                step *= 2
    gain_total = packed[: 2 * width].reshape(2, width)
    grad_norm = jnp.sqrt(packed[2 * width] + jnp.sum(gain_total * gain_total))
    factor = jnp.minimum(1.0, CLIP_NORM / grad_norm)
    gain_width = norm_gains.shape[1]
    gain_part = lax.dynamic_slice_in_dim(
        gain_total, lax.axis_index("tok") * gain_width, gain_width, 1
    )
    qkv_out = adam_step(
        qkv_weight, qkv_part, qkv_first, qkv_second, factor, D ** (-0.5), DECAY_RATE
    )
    out_out = adam_step(
        out_weight, out_part, out_first, out_second, factor, (H * HD // 16) ** (-0.5), DECAY_RATE
    )
    up_out = adam_step(up_weight, up_part, up_first, up_second, factor, D ** (-0.5), DECAY_RATE)
    down_out = adam_step(
        down_weight, down_part, down_first, down_second, factor, FF ** (-0.5), DECAY_RATE
    )
    gain_out = adam_step(norm_gains, gain_part, gains_first, gains_second, factor, GAIN_RATE, 0.0)
    return (block_out, block_in_grad, grad_norm, *qkv_out, *out_out, *up_out, *down_out, *gain_out)


def solution(mesh):
    rows = P(("tok", "bkt"), None)
    qkv = P(None, "tok", "bkt")
    tall = P("bkt", "tok")
    wide = P("tok", "bkt")
    gains = P(None, "tok")
    return jax.shard_map(
        functools.partial(per_device, mesh.shape["tok"], mesh.shape["bkt"]),
        mesh=mesh,
        in_specs=(rows, rows, P("tok"), *[qkv] * 3, *[tall] * 3, *[wide] * 3, *[tall] * 3, *[gains] * 3),
        out_specs=(rows, rows, P(), *[qkv] * 4, *[tall] * 4, *[wide] * 4, *[tall] * 4, *[gains] * 4),
        check_vma=False,
    )
```

time: 1270 us -> 850 us (0.67)
  waiting for transfers between devices: 847 us -> 454 us
  Pallas kernels: 0 us -> 57.5 us
  blocking collectives: 61.8 us -> 8.47 us
  other arithmetic: 98.7 us -> 51.1 us
  starting transfers between devices: 1.28 us -> 31.7 us
    all_gather x8 -> x4, waiting for transfers between devices: 414 us -> 0.01 us  [the longest x1 0.01 us: per_device(): lax.all_gather(out_line.reshape(bkts * out_depth, out_width), 'tok', axis...]
    ppermute x0 -> x38, waiting for transfers between devices: none -> 365 us  [the longest x30 343 us: pass_on(): return lax.ppermute(value, 'bkt', ring)]
    reduce_scatter x8 -> x4, waiting for transfers between devices: 433 us -> 88.7 us  [the longest x1 63.1 us: per_device(): lax.psum_scatter(qkv_grad.astype(LOW), 'tok', scatter_dimension=1, tiled=...]
    pallas_call x0 -> x7, Pallas kernels: none -> 57.5 us  [the longest x4 27.5 us: project(): pl.pallas_call(project_body, grid_spec=pltpu.PrefetchScalarGridSpec(num_s...]
    psum x1 -> x0, blocking collectives: 41.3 us -> none  [per_device(): lax.psum((gain_grad, weight_squares), ('tok', 'bkt'))]
    ppermute x0 -> x38, starting transfers between devices: none -> 31.4 us  [the longest x30 20.3 us: pass_on(): return lax.ppermute(value, 'bkt', ring)]
    dynamic_update_slice x0 -> x18, local copies, waits for them, and re-layouts: none -> 14.5 us  [the longest x3 7.01 us: per_device(): lax.dynamic_update_slice(seq_back, back_held[step][None], (owner(step), 0...]
    reduce_sum x7 -> x3, other arithmetic: 13.9 us -> 1.1 us  [the longest x1 0.6 us: per_device(): gain_grad_two = jnp.sum(back_two * normal, axis=0)]
  transfers between devices with their start and end apart: 16 -> 46, of which waited for: 14 -> 31; matrix products, arithmetic and copies ran while one was open for 19% -> 24% of each run, Pallas kernels for 0% -> 7%
where the time goes in v1:
time: 850 us; the launch traced here: 846 us
  waiting for transfers between devices  454 us (53%)
  matrix products  165 us (19%)
  local copies, waits for them, and re-layouts  58.1 us (7%)
  Pallas kernels  57.5 us (7%)
  other arithmetic  51.1 us (6%)
  starting transfers between devices  31.7 us (4%)
  between operations  21.2 us (2%)
    ppermute x30, waiting for transfers between devices, pass_on(): return lax.ppermute(value, 'bkt', ring)  343 us
    reduce_scatter x1, waiting for transfers between devices, per_device(): lax.psum_scatter(qkv_grad.astype(LOW), 'tok', scatter_dimension=1, tiled=...  63.1 us
    unnamed x117, local copies, waits for them, and re-layouts  27.9 us
    pallas_call x4, Pallas kernels, project(): pl.pallas_call(project_body, grid_spec=pltpu.PrefetchScalarGridSpec(num_s...  27.5 us
    reduce_scatter x1, waiting for transfers between devices, per_device(): lax.psum_scatter(down_grad, 'tok', scatter_dimension=1, tiled=True)  25.6 us
    dot_general x4, matrix products, back_one_part(): jnp.einsum('cth,cdh->td', piece, qkv_full, preferred_element_type=FULL)  23.3 us
    dot_general x2, matrix products, per_device(): inner = jax.nn.relu(jnp.dot(normed, up_full, preferred_element_type=FULL))  21.1 us
    ppermute x30, starting transfers between devices, pass_on(): return lax.ppermute(value, 'bkt', ring)  20.3 us
  transfers between devices with their start and end apart: 46, of which 31 were waited for; matrix products, arithmetic and copies ran while one was open for 24% of the time, Pallas kernels for 7%

profile of v1, /device:TPU:0, one launch (start us, length us, event | category | flops | bytes accessed | tf_op | source)
XLA Modules:
  0.0 846.5 jit_solution(2848270351613906029)
XLA Ops:
  47.2 26.7 %collective-permute-done.15 = bf16[256,2048]{1,0:T(8,128)(2,1)S(1)} collective-permute-done((bf16[256,2048]{1,0:T(8,128)(2,1)S(1)}, bf16[256,2048]{1,0:T(8,128)(2,1)S(1)}, u32[]{:S(2)}, u32[]{:S(2)}) %collective-permute-start.15) | collective-permute-done | bytes 1048608 | tf_op jit(solution)/shard_map/ppermute | solution.py:271
  84.3 12.1 %collective-permute-done.x_ref = bf16[256,2048]{1,0:T(8,128)(2,1)S(1)} collective-permute-done((bf16[256,2048]{1,0:T(8,128)(2,1)S(1)}, bf16[256,2048]{1,0:T(8,128)(2,1)S(1)}, u32[]{:S(2)}, u32[]{:S(2)}) %collective-permute-start) | collective-permute-done | bytes 1048608 | tf_op jit(solution)/shard_map/ppermute | solution.py:271
  96.3 22.6 %collective-permute-done.16 = bf16[256,2048]{1,0:T(8,128)(2,1)} collective-permute-done((bf16[256,2048]{1,0:T(8,128)(2,1)S(1)}, bf16[256,2048]{1,0:T(8,128)(2,1)}, u32[]{:S(2)}, u32[]{:S(2)}) %collective-permute-start.16) | collective-permute-done | bytes 1048608 | tf_op jit(solution)/shard_map/ppermute | solution.py:271
  122.3 19.0 %collective-permute-done.1.x_ref = bf16[256,2048]{1,0:T(8,128)(2,1)} collective-permute-done((bf16[256,2048]{1,0:T(8,128)(2,1)S(1)}, bf16[256,2048]{1,0:T(8,128)(2,1)}, u32[]{:S(2)}, u32[]{:S(2)}) %collective-permute-start.1) | collective-permute-done | bytes 1048608 | tf_op jit(solution)/shard_map/ppermute | solution.py:271
  143.7 20.1 %collective-permute-done.17 = bf16[256,2048]{1,0:T(8,128)(2,1)} collective-permute-done((bf16[256,2048]{1,0:T(8,128)(2,1)}, bf16[256,2048]{1,0:T(8,128)(2,1)}, u32[]{:S(2)}, u32[]{:S(2)}) %collective-permute-start.17) | collective-permute-done | bytes 1048608 | tf_op jit(solution)/shard_map/ppermute | solution.py:271
  201.3 10.4 %collective-permute-start.9 = (bf16[512,512]{1,0:T(8,128)(2,1)S(1)}, bf16[512,512]{1,0:T(8,128)(2,1)S(1)}, u32[]{:S(2)}, u32[]{:S(2)}) collective-permute-start(bf16[512,512]{1,0:T(8,128)(2,1)S(1)} %get-tuple-element.51), channel_id=1, source_target_pairs={{0,1},{1,2},{2,3},{3,0},{4,5},{5,6},{6,7},{7,4},{8,9},{9,10},{10,1... | collective-permute-start | bytes 1572872 | tf_op jit(solution)/shard_map/ppermute | solution.py:271
  227.3 11.2 %collective-permute-done.6 = bf16[512,512]{1,0:T(8,128)(2,1)S(1)} collective-permute-done((bf16[512,512]{1,0:T(8,128)(2,1)S(1)}, bf16[512,512]{1,0:T(8,128)(2,1)S(1)}, u32[]{:S(2)}, u32[]{:S(2)}) %collective-permute-start.6) | collective-permute-done | bytes 524320 | tf_op jit(solution)/shard_map/ppermute | solution.py:271
  305.4 11.5 %multiply_convert_fusion.4 = (bf16[512,2048]{1,0:T(8,128)(2,1)}, f32[512,2048]{1,0:T(8,128)}) fusion(f32[]{:T(128)S(6)} %convert_element_type.272, bf16[512,2048]{1,0:T(8,128)(2,1)} %get-tuple-element.117, bf16[2048,2048]{1,0:T(8,128)(2,1)} %all-gather.9.cloned.1.call-done), kind=kOutput, calls=%fused_computation.28 | convolution fusion | flops 4299161600 | bytes 16777220 | tf_op jit(solution)/shard_map/dot_general | solution.py:339
  347.6 11.2 %convolution_convert_fusion.3 = bf16[1024,2048]{1,0:T(8,128)(2,1)S(1)} fusion(bf16[2048,2048]{1,0:T(8,128)(2,1)} %all-gather.11.cloned.1.call-done, bf16[512,2048]{1,0:T(8,128)(2,1)S(1)} %get-tuple-element.128, bf16[512,2048]{1,0:T(8,128)(2,1)S(1)} %copy-done.53), kind=kOutput, calls=%fused_computation.31 | convolution fusion | flops 8600420352 | bytes 16777216 | tf_op jit(solution)/shard_map/dot_general | solution.py:381
  383.7 12.7 %collective-permute-done.21 = bf16[128,2048]{1,0:T(8,128)(2,1)S(1)} collective-permute-done((bf16[128,2048]{1,0:T(8,128)(2,1)S(1)}, bf16[128,2048]{1,0:T(8,128)(2,1)S(1)}, u32[]{:S(2)}, u32[]{:S(2)}) %collective-permute-start.21) | collective-permute-done | bytes 524320 | tf_op jit(solution)/shard_map/ppermute | solution.py:271
  407.9 11.0 %collective-permute-done.22 = bf16[128,2048]{1,0:T(8,128)(2,1)S(1)} collective-permute-done((bf16[128,2048]{1,0:T(8,128)(2,1)S(1)}, bf16[128,2048]{1,0:T(8,128)(2,1)S(1)}, u32[]{:S(2)}, u32[]{:S(2)}) %collective-permute-start.22) | collective-permute-done | bytes 524320 | tf_op jit(solution)/shard_map/ppermute | solution.py:271
  419.2 22.3 %collective-permute-done.13 = bf16[2,128,2048]{2,1,0:T(8,128)(2,1)S(1)} collective-permute-done((bf16[2,128,2048]{2,1,0:T(8,128)(2,1)S(1)}, bf16[2,128,2048]{2,1,0:T(8,128)(2,1)S(1)}, u32[]{:S(2)}, u32[]{:S(2)}) %collective-permute-start.13) | collective-permute-done | bytes 1048608 | tf_op jit(solution)/shard_map/ppermute | solution.py:271
  442.1 10.6 %collective-permute-done.20 = bf16[128,2048]{1,0:T(8,128)(2,1)S(1)} collective-permute-done((bf16[128,2048]{1,0:T(8,128)(2,1)S(1)}, bf16[128,2048]{1,0:T(8,128)(2,1)S(1)}, u32[]{:S(2)}, u32[]{:S(2)}) %collective-permute-start.20) | collective-permute-done | bytes 524320 | tf_op jit(solution)/shard_map/ppermute | solution.py:271
  452.8 11.1 %collective-permute-done.23 = bf16[128,2048]{1,0:T(8,128)(2,1)S(1)} collective-permute-done((bf16[128,2048]{1,0:T(8,128)(2,1)S(1)}, bf16[128,2048]{1,0:T(8,128)(2,1)S(1)}, u32[]{:S(2)}, u32[]{:S(2)}) %collective-permute-start.23) | collective-permute-done | bytes 524320 | tf_op jit(solution)/shard_map/ppermute | solution.py:271
  464.6 17.7 %collective-permute-done.14 = bf16[2,128,2048]{2,1,0:T(8,128)(2,1)S(1)} collective-permute-done((bf16[2,128,2048]{2,1,0:T(8,128)(2,1)S(1)}, bf16[2,128,2048]{2,1,0:T(8,128)(2,1)S(1)}, u32[]{:S(2)}, u32[]{:S(2)}) %collective-permute-start.14) | collective-permute-done | bytes 1048608 | tf_op jit(solution)/shard_map/ppermute | solution.py:271
  493.0 14.1 %convolution_convert_fusion.1 = bf16[2048,2048]{1,0:T(8,128)(2,1)} fusion(bf16[512,2048]{1,0:T(8,128)(2,1)} %get-tuple-element.118, bf16[512,2048]{1,0:T(8,128)(2,1)} %get-tuple-element.117, bf16[512,2048]{1,0:T(8,128)(2,1)} %copy-done.52, bf16[512,2048]{1,0:T(8,128)(2,1)} %copy-done.51), kind=kOutput, calls=%fused_computation.1 | convolution fusion | flops 8610906112 | bytes 16777216 | tf_op jit(solution)/shard_map/dot_general | solution.py:373
  507.2 14.2 %convolution_convert_fusion = bf16[2048,2048]{1,0:T(8,128)(2,1)} fusion(bf16[512,2048]{1,0:T(8,128)(2,1)} %bitcast.127, bf16[512,2048]{1,0:T(8,128)(2,1)} %bitcast.126, bf16[512,2048]{1,0:T(8,128)(2,1)} %copy-done.54, bf16[512,2048]{1,0:T(8,128)(2,1)} %get-tuple-element.130), kind=kOutput, calls=%fused_computation | convolution fusion | flops 8610906112 | bytes 16777216 | tf_op jit(solution)/shard_map/dot_general | solution.py:375
  552.6 14.8 %shard_map.359 = bf16[3,1024,512]{2,1,0:T(8,128)(2,1)} custom-call(bf16[3,1024,512]{2,1,0:T(8,128)(2,1)} %copy-done, bf16[3,1024,512]{2,1,0:T(8,128)(2,1)} %copy-done, bf16[3,1024,512]{2,1,0:T(8,128)(2,1)} %copy-done, bf16[1024,512]{1,0:T(8,128)(2,1)S(1)} %bitcast.114, f32[512,512]{1,0:T(8,128)S(1)} %copy-done.3, ...), custom_call_target="tpu_custom_call" | custom-call | flops 2684354560 | bytes 7340032 | tf_op jit(solution)/shard_map/pallas_call | solution.py:209
  567.5 10.5 %convert_bitcast_fusion = bf16[3,2048,512]{1,2,0:T(8,128)(2,1)} fusion(bf16[3,1024,512]{2,1,0:T(8,128)(2,1)} %shard_map.359, bf16[1024,2048]{1,0:T(8,128)(2,1)S(1)} %copy-done.9), kind=kOutput, calls=%fused_computation.3 | convolution fusion | flops 6445596672 | bytes 13631488 | tf_op jit(solution)/shard_map/td,cth->cdh/dot_general | solution.py:395
  584.0 25.5 %collective-permute-done.27 = bf16[256,2048]{1,0:T(8,128)(2,1)S(1)} collective-permute-done((bf16[256,2048]{1,0:T(8,128)(2,1)S(1)}, bf16[256,2048]{1,0:T(8,128)(2,1)S(1)}, u32[]{:S(2)}, u32[]{:S(2)}) %collective-permute-start.27) | collective-permute-done | bytes 1048608 | tf_op jit(solution)/shard_map/ppermute | solution.py:271
  614.5 24.6 %collective-permute-done.28 = bf16[256,2048]{1,0:T(8,128)(2,1)S(1)} collective-permute-done((bf16[256,2048]{1,0:T(8,128)(2,1)S(1)}, bf16[256,2048]{1,0:T(8,128)(2,1)S(1)}, u32[]{:S(2)}, u32[]{:S(2)}) %collective-permute-start.28) | collective-permute-done | bytes 1048608 | tf_op jit(solution)/shard_map/ppermute | solution.py:271
  646.3 28.1 %collective-permute-done.30 = bf16[512,256]{1,0:T(8,128)(2,1)S(1)} collective-permute-done((bf16[512,256]{1,0:T(8,128)(2,1)S(1)}, bf16[512,256]{1,0:T(8,128)(2,1)S(1)}, u32[]{:S(2)}, u32[]{:S(2)}) %collective-permute-start.30) | collective-permute-done | bytes 262176 | tf_op jit(solution)/shard_map/ppermute | solution.py:271
  686.0 25.6 %reduce-scatter.11.cloned.1.call-done = bf16[2048,256]{1,0:T(8,128)(2,1)} async-done(((bf16[2048,2048]{1,0:T(8,128)(2,1)}), bf16[2048,256]{1,0:T(8,128)(2,1)}) %reduce-scatter.11.cloned.1.call-update) | async-done | bytes 1048592 | tf_op jit(solution)/shard_map/reduce_scatter | solution.py:376
  714.0 63.1 %reduce-scatter.5.cloned.1.call-done = bf16[3,256,512]{1,2,0:T(8,128)(2,1)} async-done(((bf16[3,2048,512]{1,2,0:T(8,128)(2,1)}), bf16[3,256,512]{1,2,0:T(8,128)(2,1)}) %reduce-scatter.5.cloned.1.call-update) | async-done | bytes 786448 | tf_op jit(solution)/shard_map/reduce_scatter | solution.py:396
  (310 shorter events, 374.6 us)
Async XLA Ops:
  7.2 159.0 %all-gather.5.cloned.1.call-start = ((), (), s32[]{:S(2)}) async-start(), calls=%async_computation.4 | async-start | bytes 7077888 | tf_op jit(solution)/shard_map/all_gather | solution.py:290
  9.7 270.6 %all-gather.7.cloned.1.call-start = ((), (), s32[]{:S(2)}) async-start(), calls=%async_computation.5 | async-start | bytes 9437184 | tf_op jit(solution)/shard_map/all_gather | solution.py:298
  40.0 265.3 %all-gather.9.cloned.1.call-start = ((), (), s32[]{:S(2)}) async-start(), calls=%async_computation.6 | async-start | bytes 9437184 | tf_op jit(solution)/shard_map/all_gather | solution.py:299
  42.9 273.9 %all-gather.11.cloned.1.call-start = ((), (), s32[]{:S(2)}) async-start(), calls=%async_computation.7 | async-start | bytes 9437184 | tf_op jit(solution)/shard_map/all_gather | solution.py:300
  44.1 600.8 %reduce-scatter.7.cloned.1.call-start = ((), (), s32[]{:S(2)}) async-start(), calls=%async_computation.9 | async-start | bytes 9437184 | tf_op jit(solution)/shard_map/reduce_scatter | solution.py:378
  45.9 27.9 %collective-permute-start.15 = (bf16[256,2048]{1,0:T(8,128)(2,1)S(1)}, bf16[256,2048]{1,0:T(8,128)(2,1)S(1)}, u32[]{:S(2)}, u32[]{:S(2)}) collective-permute-start(bf16[256,2048]{1,0:T(8,128)(2,1)S(1)} %get-tuple-element.103), channel_id=1, source_target_pairs={{0,1},{1,2},{2,3},{3,0},{4,5},{5,6},{6,7},{7,4},{8,9},{9,10},{10,1... | collective-permute-start | bytes 3145736 | tf_op jit(solution)/shard_map/ppermute | solution.py:271
  47.2 49.2 %collective-permute-start = (bf16[256,2048]{1,0:T(8,128)(2,1)S(1)}, bf16[256,2048]{1,0:T(8,128)(2,1)S(1)}, u32[]{:S(2)}, u32[]{:S(2)}) collective-permute-start(bf16[256,2048]{1,0:T(8,128)(2,1)S(1)} %copy-done.1), channel_id=1, source_target_pairs={{0,1},{1,2},{2,3},{3,0},{4,5},{5,6},{6,7},{7,4},{8,9},{9,10},{10,1... | collective-permute-start | bytes 3145736 | tf_op jit(solution)/shard_map/ppermute | solution.py:271
  73.9 45.0 %collective-permute-start.16 = (bf16[256,2048]{1,0:T(8,128)(2,1)S(1)}, bf16[256,2048]{1,0:T(8,128)(2,1)}, u32[]{:S(2)}, u32[]{:S(2)}) collective-permute-start(bf16[256,2048]{1,0:T(8,128)(2,1)S(1)} %collective-permute-done.15), channel_id=1, source_target_pairs={{0,1},{1,2},{2,3},{3,0},{4,5},{5,6},{6,7},{7,4},{8,9},{9,10},{10,1... | collective-permute-start | bytes 3145736 | tf_op jit(solution)/shard_map/ppermute | solution.py:271
  96.3 45.0 %collective-permute-start.1 = (bf16[256,2048]{1,0:T(8,128)(2,1)S(1)}, bf16[256,2048]{1,0:T(8,128)(2,1)}, u32[]{:S(2)}, u32[]{:S(2)}) collective-permute-start(bf16[256,2048]{1,0:T(8,128)(2,1)S(1)} %collective-permute-done.x_ref), channel_id=1, source_target_pairs={{0,1},{1,2},{2,3},{3,0},{4,5},{5,6},{6,7},{7,4},{8,9},{9,10},{10,1... | collective-permute-start | bytes 3145736 | tf_op jit(solution)/shard_map/ppermute | solution.py:271
  118.9 44.9 %collective-permute-start.17 = (bf16[256,2048]{1,0:T(8,128)(2,1)}, bf16[256,2048]{1,0:T(8,128)(2,1)}, u32[]{:S(2)}, u32[]{:S(2)}) collective-permute-start(bf16[256,2048]{1,0:T(8,128)(2,1)} %collective-permute-done.16), channel_id=1, source_target_pairs={{0,1},{1,2},{2,3},{3,0},{4,5},{5,6},{6,7},{7,4},{8,9},{9,10},{10,1... | collective-permute-start | bytes 3145736 | tf_op jit(solution)/shard_map/ppermute | solution.py:271
  141.4 45.3 %collective-permute-start.2 = (bf16[256,2048]{1,0:T(8,128)(2,1)}, bf16[256,2048]{1,0:T(8,128)(2,1)}, u32[]{:S(2)}, u32[]{:S(2)}) collective-permute-start(bf16[256,2048]{1,0:T(8,128)(2,1)} %collective-permute-done.1.x_ref), channel_id=1, source_target_pairs={{0,1},{1,2},{2,3},{3,0},{4,5},{5,6},{6,7},{7,4},{8,9},{9,10},{10,1... | collective-permute-start | bytes 3145736 | tf_op jit(solution)/shard_map/ppermute | solution.py:271
  336.1 44.0 %collective-permute-start.18 = (bf16[128,2048]{1,0:T(8,128)(2,1)S(1)}, bf16[128,2048]{1,0:T(8,128)(2,1)S(1)}, u32[]{:S(2)}, u32[]{:S(2)}) collective-permute-start(bf16[128,2048]{1,0:T(8,128)(2,1)S(1)} %constant_dynamic-slice_fusion.6), channel_id=1, source_target_pairs={{0,1},{1,2},{2,3},{3,0},{4,5},{5,6},{6,7},{7,4},{8,9},{9,10},{10,1... | collective-permute-start | bytes 1572872 | tf_op jit(solution)/shard_map/ppermute | solution.py:271
  358.9 37.8 %collective-permute-start.12 = (bf16[2,128,2048]{2,1,0:T(8,128)(2,1)S(1)}, bf16[2,128,2048]{2,1,0:T(8,128)(2,1)S(1)}, u32[]{:S(2)}, u32[]{:S(2)}) collective-permute-start(bf16[2,128,2048]{2,1,0:T(8,128)(2,1)S(1)} %dynamic-slice_bitcast_fusion), channel_id=1, source_target_pairs={{0,1},{1,2},{2,3},{3,0},{4,5},{5,6},{6,7},{7,4},{8,9},{9,10},{10,1... | collective-permute-start | bytes 3145736 | tf_op jit(solution)/shard_map/ppermute | solution.py:271
  380.2 27.5 %collective-permute-start.19 = (bf16[128,2048]{1,0:T(8,128)(2,1)S(1)}, bf16[128,2048]{1,0:T(8,128)(2,1)S(1)}, u32[]{:S(2)}, u32[]{:S(2)}) collective-permute-start(bf16[128,2048]{1,0:T(8,128)(2,1)S(1)} %add_convert_fusion.3), channel_id=1, source_target_pairs={{0,1},{1,2},{2,3},{3,0},{4,5},{5,6},{6,7},{7,4},{8,9},{9,10},{10,1... | collective-permute-start | bytes 1572872 | tf_op jit(solution)/shard_map/ppermute | solution.py:271
  397.1 44.3 %collective-permute-start.13 = (bf16[2,128,2048]{2,1,0:T(8,128)(2,1)S(1)}, bf16[2,128,2048]{2,1,0:T(8,128)(2,1)S(1)}, u32[]{:S(2)}, u32[]{:S(2)}) collective-permute-start(bf16[2,128,2048]{2,1,0:T(8,128)(2,1)S(1)} %fusion.40), channel_id=1, source_target_pairs={{0,1},{1,2},{2,3},{3,0},{4,5},{5,6},{6,7},{7,4},{8,9},{9,10},{10,1... | collective-permute-start | bytes 3145736 | tf_op jit(solution)/shard_map/ppermute | solution.py:271
  407.9 44.8 %collective-permute-start.20 = (bf16[128,2048]{1,0:T(8,128)(2,1)S(1)}, bf16[128,2048]{1,0:T(8,128)(2,1)S(1)}, u32[]{:S(2)}, u32[]{:S(2)}) collective-permute-start(bf16[128,2048]{1,0:T(8,128)(2,1)S(1)} %add_convert_fusion.2), channel_id=1, source_target_pairs={{0,1},{1,2},{2,3},{3,0},{4,5},{5,6},{6,7},{7,4},{8,9},{9,10},{10,1... | collective-permute-start | bytes 1572872 | tf_op jit(solution)/shard_map/ppermute | solution.py:271
  419.1 44.8 %collective-permute-start.23 = (bf16[128,2048]{1,0:T(8,128)(2,1)S(1)}, bf16[128,2048]{1,0:T(8,128)(2,1)S(1)}, u32[]{:S(2)}, u32[]{:S(2)}) collective-permute-start(bf16[128,2048]{1,0:T(8,128)(2,1)S(1)} %add_convert_fusion), channel_id=1, source_target_pairs={{0,1},{1,2},{2,3},{3,0},{4,5},{5,6},{6,7},{7,4},{8,9},{9,10},{10,1... | collective-permute-start | bytes 1572872 | tf_op jit(solution)/shard_map/ppermute | solution.py:271
  441.8 40.5 %collective-permute-start.14 = (bf16[2,128,2048]{2,1,0:T(8,128)(2,1)S(1)}, bf16[2,128,2048]{2,1,0:T(8,128)(2,1)S(1)}, u32[]{:S(2)}, u32[]{:S(2)}) collective-permute-start(bf16[2,128,2048]{2,1,0:T(8,128)(2,1)S(1)} %fusion.39), channel_id=1, source_target_pairs={{0,1},{1,2},{2,3},{3,0},{4,5},{5,6},{6,7},{7,4},{8,9},{9,10},{10,1... | collective-permute-start | bytes 3145736 | tf_op jit(solution)/shard_map/ppermute | solution.py:271
  492.9 189.5 %reduce-scatter.9.cloned.1.call-start = ((), (), s32[]{:S(2)}) async-start(), calls=%async_computation.10 | async-start | bytes 9437184 | tf_op jit(solution)/shard_map/reduce_scatter | solution.py:374
  507.1 204.5 %reduce-scatter.11.cloned.1.call-start = ((), (), s32[]{:S(2)}) async-start(), calls=%async_computation.11 | async-start | bytes 9437184 | tf_op jit(solution)/shard_map/reduce_scatter | solution.py:376
  521.4 255.7 %reduce-scatter.5.cloned.1.call-start = ((), (), s32[]{:S(2)}) async-start(), calls=%async_computation.8 | async-start | bytes 7077888 | tf_op jit(solution)/shard_map/reduce_scatter | solution.py:396
  644.9 30.9 %collective-permute-start.29 = (bf16[256,2048]{1,0:T(8,128)(2,1)}, bf16[256,2048]{1,0:T(8,128)(2,1)S(1)}, u32[]{:S(2)}, u32[]{:S(2)}) collective-permute-start(bf16[256,2048]{1,0:T(8,128)(2,1)} %fusion.22), channel_id=1, source_target_pairs={{0,1},{1,2},{2,3},{3,0},{4,5},{5,6},{6,7},{7,4},{8,9},{9,10},{10,1... | collective-permute-start | bytes 3145736 | tf_op jit(solution)/shard_map/ppermute | solution.py:271
  646.0 28.5 %collective-permute-start.30 = (bf16[512,256]{1,0:T(8,128)(2,1)S(1)}, bf16[512,256]{1,0:T(8,128)(2,1)S(1)}, u32[]{:S(2)}, u32[]{:S(2)}) collective-permute-start(bf16[512,256]{1,0:T(8,128)(2,1)S(1)} %constant_dynamic-slice_fusion), channel_id=1, source_target_pairs={{0,1},{1,2},{2,3},{3,0},{4,5},{5,6},{6,7},{7,4},{8,9},{9,10},{10,1... | collective-permute-start | bytes 786440 | tf_op jit(solution)/shard_map/ppermute | solution.py:271
  686.0 93.3 %collective-permute-start.32 = (bf16[512,256]{1,0:T(8,128)(2,1)S(1)}, bf16[512,256]{1,0:T(8,128)(2,1)S(1)}, u32[]{:S(2)}, u32[]{:S(2)}) collective-permute-start(bf16[512,256]{1,0:T(8,128)(2,1)S(1)} %add_convert_fusion.4), channel_id=1, source_target_pairs={{0,1},{1,2},{2,3},{3,0},{4,5},{5,6},{6,7},{7,4},{8,9},{9,10},{10,1... | collective-permute-start | bytes 786440 | tf_op jit(solution)/shard_map/ppermute | solution.py:271
  (77 other events, 983.3 us)
Sparse Core Ops, SparseCore 0:
  10.5 48.2 all-gather.4
  61.2 55.9 all-gather.6
  119.7 54.3 all-gather.8
  176.4 56.0 all-gather.10
  493.1 68.7 reduce-scatter.6
  565.5 71.2 reduce-scatter.8
  640.3 71.2 reduce-scatter.10
  715.4 61.7 reduce-scatter.4

commit v2 on v1

v2 whole, which is shorter than its diff:
```python
import functools
import jax
import jax.numpy as jnp
from jax import lax
from jax.experimental import pallas as pl
from jax.experimental.pallas import tpu as pltpu
from jax.sharding import Mesh, PartitionSpec as P

D = 2048
H = 16
HD = 128
FF = 8192
STEP = 10

NORM_EPS = 1e-05
ADAM_EPS = 1e-08
CLIP_NORM = 1.0
BETA_ONE = 0.9
BETA_TWO = 0.95
DECAY_RATE = 0.1
GAIN_RATE = 0.3
ROPE_BASE = 10000.0

LOW = jnp.bfloat16
FULL = jnp.float32
SCALE = HD ** (-0.5)
VMEM_BYTES = 48 * 1024 * 1024
NN = (((1,), (0,)), ((), ()))
NT = (((1,), (1,)), ((), ()))
TN = (((0,), (0,)), ((), ()))


def rotary_tables(length):
    positions = jnp.arange(length).astype(FULL)[:, None]
    freq_index = jnp.arange(HD // 2).astype(FULL)
    angles = positions * (ROPE_BASE ** (-2.0 * freq_index / HD))[None, :]
    cosine = jnp.cos(angles)
    sine = jnp.sin(angles)
    return (jnp.concatenate([cosine, cosine], axis=-1), jnp.concatenate([-sine, sine], axis=-1))


LIGHT = pl.CostEstimate(flops=1, bytes_accessed=1, transcendentals=0)


def params(vmem=VMEM_BYTES):
    return pltpu.CompilerParams(vmem_limit_bytes=vmem)


def project_body(place_ref, x_ref, gain_ref, w_ref, cos_ref, sin_ref, *rest):
    normed_ref, out_ref, seq_ref = rest[-3:]
    part = pl.program_id(0)

    @pl.when(part == 0)
    def _():
        low = x_ref[...]
        seq_ref[...] = low
        values = low.astype(FULL)
        inverse = lax.rsqrt(jnp.mean(values * values, axis=-1, keepdims=True) + NORM_EPS)
        normed_ref[...] = (values * inverse * gain_ref[...]).astype(LOW)

    product = jnp.dot(normed_ref[...], w_ref[0], preferred_element_type=FULL)

    @pl.when(part < 2)
    def _():
        for head in range(product.shape[1] // HD):
            one = product[:, head * HD : (head + 1) * HD]
            turned = one * cos_ref[...] + pltpu.roll(one, HD // 2, 1) * sin_ref[...]
            out_ref[0, :, head * HD : (head + 1) * HD] = turned.astype(LOW)

    @pl.when(part == 2)
    def _():
        out_ref[0] = product.astype(LOW)


def project(place, x, gain, weight, cosine, sine, carried):
    rows, width = x.shape
    length = cosine.shape[0]
    cols = weight.shape[2]
    shapes = [
        jax.ShapeDtypeStruct((length, width), LOW),
        jax.ShapeDtypeStruct((3, length, cols), LOW),
        jax.ShapeDtypeStruct((length, width), LOW),
    ]
    in_specs = [
        pl.BlockSpec((rows, width), lambda c, p: (0, 0)),
        pl.BlockSpec((1, width), lambda c, p: (0, 0)),
        pl.BlockSpec((1, width, cols), lambda c, p: (c, 0, 0)),
        pl.BlockSpec((rows, HD), lambda c, p: (p[0], 0)),
        pl.BlockSpec((rows, HD), lambda c, p: (p[0], 0)),
    ]
    aliases = {}
    if carried is not None:
        in_specs += [pl.BlockSpec(memory_space=pl.ANY)] * 3
        aliases = {6: 0, 7: 1, 8: 2}
    return pl.pallas_call(
        project_body,
        grid_spec=pltpu.PrefetchScalarGridSpec(
            num_scalar_prefetch=1,
            grid=(3,),
            in_specs=in_specs,
            out_specs=[
                pl.BlockSpec((rows, width), lambda c, p: (p[0], 0)),
                pl.BlockSpec((1, rows, cols), lambda c, p: (c, p[0], 0)),
                pl.BlockSpec((rows, width), lambda c, p: (p[0], 0)),
            ],
        ),
        out_shape=shapes,
        input_output_aliases=aliases,
        compiler_params=params(),
        cost_estimate=LIGHT,
    )(place, x, gain, weight, cosine, sine, *(carried or ()))


def attend_body(half, blocks, count, q_ref, k_ref, v_ref, *rest):
    cotangents, (ring_ref, log_ref) = rest[:count], rest[count:]
    length = q_ref.shape[1]
    block = length // blocks
    rows = block // 2
    for index in range(count):
        first = length // 2 + index * rows
        ring_ref[first : first + rows] = cotangents[index][...].astype(LOW)
    for index in range(blocks):
        first = index * block + half * rows
        last = first + rows
        query = q_ref[0, first:last]
        scores = (
            lax.dot_general(query, k_ref[0, :last], NT, preferred_element_type=FULL) * SCALE
        )
        row = lax.broadcasted_iota(jnp.int32, scores.shape, 0) + first
        col = lax.broadcasted_iota(jnp.int32, scores.shape, 1)
        scores = jnp.where(row >= col, scores, -1e30)
        peak = jnp.max(scores, axis=-1, keepdims=True)
        expo = jnp.exp(scores - peak)
        total = jnp.sum(expo, axis=-1, keepdims=True)
        probs = (expo / total).astype(LOW)
        mixed = jnp.dot(probs, v_ref[0, :last], preferred_element_type=FULL)
        ring_ref[index * rows : (index + 1) * rows] = mixed.astype(LOW)
        log_ref[index * rows : (index + 1) * rows] = jnp.broadcast_to(
            peak + jnp.log(total), (rows, HD)
        )


def attend(half, blocks, qkv, cotangent):
    _, length, cols = qkv.shape
    heads = cols // HD
    rows, width = cotangent.shape
    count = width // cols

    def cotangent_spec(index):
        return pl.BlockSpec((rows // 2, HD), lambda h: (half, index * heads + h))

    return pl.pallas_call(
        functools.partial(attend_body, half, blocks, count),
        grid=(heads,),
        in_specs=[
            pl.BlockSpec((1, length, HD), lambda h: (0, 0, h)),
            pl.BlockSpec((1, length, HD), lambda h: (1, 0, h)),
            pl.BlockSpec((1, length, HD), lambda h: (2, 0, h)),
        ]
        + [cotangent_spec(index) for index in range(count)],
        out_specs=[
            pl.BlockSpec((length // 2 + count * rows // 2, HD), lambda h: (0, h)),
            pl.BlockSpec((length // 2, HD), lambda h: (0, h)),
        ],
        out_shape=[
            jax.ShapeDtypeStruct((length // 2 + count * rows // 2, cols), LOW),
            jax.ShapeDtypeStruct((length // 2, cols), FULL),
        ],
        compiler_params=params(),
        cost_estimate=LIGHT,
    )(qkv, qkv, qkv, *[cotangent] * count)


def attend_back_body(blocks, place_ref, q_ref, k_ref, v_ref, log_a_ref, log_b_ref, cos_ref, sin_ref, *rest):
    pieces = rest[: 2 * blocks]
    out_ref, key_acc, value_acc, back_ref = rest[2 * blocks :]
    length = q_ref.shape[1]
    block = length // blocks
    rows = block // 2
    for half in range(2):
        for step in range(blocks):
            first = pl.multiple_of(place_ref[step] * block + half * rows, rows)
            back_ref[pl.ds(first, rows), :] = pieces[half * blocks + step][...]

    def turn_back(one, cosine, sine):
        return one * cosine - pltpu.roll(one, HD // 2, 1) * sine

    for index in range(blocks):
        first, last = index * block, (index + 1) * block
        query = q_ref[0, first:last]
        back = back_ref[first:last]
        keys = k_ref[0, :last]
        log_total = jnp.concatenate(
            [
                log_a_ref[index * rows : (index + 1) * rows, :1],
                log_b_ref[index * rows : (index + 1) * rows, :1],
            ],
            axis=0,
        )
        scores = lax.dot_general(query, keys, NT, preferred_element_type=FULL) * SCALE
        row = lax.broadcasted_iota(jnp.int32, scores.shape, 0) + first
        col = lax.broadcasted_iota(jnp.int32, scores.shape, 1)
        probs = jnp.exp(jnp.where(row >= col, scores, -1e30) - log_total)
        back_probs = lax.dot_general(back, v_ref[0, :last], NT, preferred_element_type=FULL)
        centre = jnp.sum(probs * back_probs, axis=-1, keepdims=True)
        back_scores = (probs * (back_probs - centre)).astype(LOW)
        query_grad = jnp.dot(back_scores, keys, preferred_element_type=FULL) * SCALE
        out_ref[0, first:last] = turn_back(query_grad, cos_ref[first:last], sin_ref[first:last]).astype(LOW)
        key_part = lax.dot_general(back_scores, query, TN, preferred_element_type=FULL)
        value_part = lax.dot_general(probs.astype(LOW), back, TN, preferred_element_type=FULL)
        if index > 0:
            key_acc[:first] += key_part[:first]
            value_acc[:first] += value_part[:first]
        key_acc[first:last] = key_part[first:]
        value_acc[first:last] = value_part[first:]
    out_ref[1] = turn_back(key_acc[...] * SCALE, cos_ref[...], sin_ref[...]).astype(LOW)
    out_ref[2] = value_acc[...].astype(LOW)


def attend_back(places, qkv, pieces, logs, cosine, sine):
    _, length, cols = qkv.shape
    heads = cols // HD
    blocks = len(pieces) // 2
    column = lambda h, p: (0, h)
    return pl.pallas_call(
        functools.partial(attend_back_body, blocks),
        grid_spec=pltpu.PrefetchScalarGridSpec(
            num_scalar_prefetch=1,
            grid=(heads,),
            in_specs=[
                pl.BlockSpec((1, length, HD), lambda h, p: (0, 0, h)),
                pl.BlockSpec((1, length, HD), lambda h, p: (1, 0, h)),
                pl.BlockSpec((1, length, HD), lambda h, p: (2, 0, h)),
                pl.BlockSpec((length // 2, HD), column),
                pl.BlockSpec((length // 2, HD), column),
                pl.BlockSpec((length, HD), lambda h, p: (0, 0)),
                pl.BlockSpec((length, HD), lambda h, p: (0, 0)),
            ]
            + [pl.BlockSpec((length // blocks // 2, HD), column)] * (2 * blocks),
            out_specs=pl.BlockSpec((3, length, HD), lambda h, p: (0, 0, h)),
            scratch_shapes=[
                pltpu.VMEM((length, HD), FULL),
                pltpu.VMEM((length, HD), FULL),
                pltpu.VMEM((length, HD), LOW),
            ],
        ),
        out_shape=jax.ShapeDtypeStruct((3, length, cols), LOW),
        compiler_params=params(),
        cost_estimate=LIGHT,
    )(places, qkv, qkv, qkv, logs[0], logs[1], cosine, sine, *pieces)


def mix_first_body(count, place_ref, seq_ref, *rest):
    slabs, weights, acc_ref = rest[:count], rest[count : 2 * count], rest[2 * count]
    blocks, rows, width = seq_ref.shape
    shards, _, _, shard = weights[0].shape
    for index in range(shards):
        span = slice(index * shard, (index + 1) * shard)
        total = seq_ref[:, :, span].reshape(blocks * rows, shard).astype(FULL)
        for slab, weight in zip(slabs, weights):
            total = total + jnp.dot(slab[...], weight[index, 0], preferred_element_type=FULL)
        acc_ref[:, span] = total


def mix_first(part, places, seq_in, slabs, weight):
    blocks, block, width = seq_in.shape
    half = block // 2
    shards, _, cols, shard = weight.shape
    tile = max(1, 512 // shard)
    count = len(slabs)

    def weight_spec(step):
        return pl.BlockSpec((tile, 1, cols, shard), lambda i, p: (i, p[step], 0, 0))

    return pl.pallas_call(
        functools.partial(mix_first_body, count),
        grid_spec=pltpu.PrefetchScalarGridSpec(
            num_scalar_prefetch=1,
            grid=(shards // tile,),
            in_specs=[pl.BlockSpec((blocks, half, tile * shard), lambda i, p: (0, part, i))]
            + [pl.BlockSpec((blocks * half, cols), lambda i, p: (0, 0))] * count
            + [weight_spec(step) for step in range(count)],
            out_specs=pl.BlockSpec((blocks * half, tile * shard), lambda i, p: (0, i)),
        ),
        out_shape=jax.ShapeDtypeStruct((blocks * half, width), FULL),
        compiler_params=params(),
        cost_estimate=LIGHT,
    )(places, seq_in, *slabs, *[weight] * count)


def mix_last_body(count, place_ref, acc_ref, gain_ref, weight_ref, *rest):
    slabs = rest[:count]
    normed_ref, middle_ref, mixed_ref = rest[count:]
    cols = slabs[0].shape[1]
    slab = slabs[-1][...]
    parts = [
        jnp.dot(slab, weight_ref[index, 0], preferred_element_type=FULL)
        for index in range(weight_ref.shape[0])
    ]
    middle = acc_ref[...] + jnp.concatenate(parts, axis=1)
    inverse = lax.rsqrt(jnp.mean(middle * middle, axis=-1, keepdims=True) + NORM_EPS)
    normed_ref[...] = (middle * inverse * gain_ref[...]).astype(LOW)

    @pl.when(pl.program_id(0) == place_ref[0])
    def _():
        middle_ref[...] = middle
        for step in range(count):
            first = pl.multiple_of(place_ref[step] * cols, cols)
            mixed_ref[:, pl.ds(first, cols)] = slabs[step][...]


def mix_last(places, acc, gain, slabs, weight):
    length, width = acc.shape
    shards, count, cols, shard = weight.shape
    rows = length // count
    return pl.pallas_call(
        functools.partial(mix_last_body, count),
        grid_spec=pltpu.PrefetchScalarGridSpec(
            num_scalar_prefetch=1,
            grid=(count,),
            in_specs=[
                pl.BlockSpec((rows, width), lambda i, p: (i, 0)),
                pl.BlockSpec((1, width), lambda i, p: (0, 0)),
                pl.BlockSpec((shards, 1, cols, shard), lambda i, p: (0, p[count - 1], 0, 0)),
            ]
            + [pl.BlockSpec((rows, cols), lambda i, p: (i, 0))] * count,
            out_specs=[
                pl.BlockSpec((rows, width), lambda i, p: (i, 0)),
                pl.BlockSpec((rows, width), lambda i, p: (0, 0)),
                pl.BlockSpec((rows, count * cols), lambda i, p: (0, 0)),
            ],
        ),
        out_shape=[
            jax.ShapeDtypeStruct((length, width), LOW),
            jax.ShapeDtypeStruct((rows, width), FULL),
            jax.ShapeDtypeStruct((rows, count * cols), LOW),
        ],
        compiler_params=params(),
        cost_estimate=LIGHT,
    )(places, acc, gain, weight, *slabs)


def hidden_body(count, place_ref, live_ref, normed_ref, up_ref, down_ref, *rest):
    pieces = rest[:count]
    hidden_ref, inner_ref, back_ref = rest[count:]
    cols = pieces[0].shape[1]
    rows = pieces[0].shape[0] * cols // back_ref.shape[1]

    @pl.when(pl.program_id(0) == 0)
    def _():
        for step in range(count):
            first = pl.multiple_of(place_ref[step] * rows, rows)
            for index in range(pieces[0].shape[0] // rows):
                span = slice(index * rows, (index + 1) * rows)
                back_ref[pl.ds(first, rows), index * cols : (index + 1) * cols] = pieces[step][span]

    inner = jnp.dot(normed_ref[...], up_ref[...], preferred_element_type=FULL)
    inner = jnp.maximum(inner, 0.0) * live_ref[0]
    hidden_ref[...] = (inner * inner).astype(LOW)
    back = lax.dot_general(back_ref[...], down_ref[...], NT, preferred_element_type=FULL)
    inner_ref[...] = (back * 2.0 * inner).astype(LOW)


def hidden_units(places, live, normed, up, down, pieces):
    length, width = normed.shape
    units = up.shape[1]
    tile = min(512, units)
    count = len(pieces)
    cols = pieces[0].shape[1]
    below = pieces[0].shape[0] - length
    whole = lambda i, p, l: (0, 0)
    column = lambda i, p, l: (0, i)
    return pl.pallas_call(
        functools.partial(hidden_body, count),
        grid_spec=pltpu.PrefetchScalarGridSpec(
            num_scalar_prefetch=2,
            grid=(units // tile,),
            in_specs=[
                pl.BlockSpec((length, width), whole),
                pl.BlockSpec((width, tile), column),
                pl.BlockSpec((tile, width), lambda i, p, l: (i, 0)),
            ]
            + [pl.BlockSpec((below, cols), lambda i, p, l: (length // below, 0))] * count,
            out_specs=[
                pl.BlockSpec((length, tile), column),
                pl.BlockSpec((length, tile), column),
                pl.BlockSpec((length, width), whole),
            ],
        ),
        out_shape=[
            jax.ShapeDtypeStruct((length, units), LOW),
            jax.ShapeDtypeStruct((length, units), LOW),
            jax.ShapeDtypeStruct((length, width), LOW),
        ],
        compiler_params=params(),
        cost_estimate=LIGHT,
    )(places, live, normed, up, down, *pieces)


def product_body(dims, left_ref, right_ref, out_ref):
    out_ref[...] = lax.dot_general(
        left_ref[...], right_ref[...], dims, preferred_element_type=FULL
    ).astype(LOW)


def product(left, right, turned):
    length, depth = left.shape
    width = right.shape[0] if turned else right.shape[1]
    tile = min(512, width)
    if turned:
        spec = pl.BlockSpec((tile, depth), lambda i: (i, 0))
    else:
        spec = pl.BlockSpec((depth, tile), lambda i: (0, i))
    return pl.pallas_call(
        functools.partial(product_body, NT if turned else NN),
        grid=(width // tile,),
        in_specs=[pl.BlockSpec((length, depth), lambda i: (0, 0)), spec],
        out_specs=pl.BlockSpec((length, tile), lambda i: (0, i)),
        out_shape=jax.ShapeDtypeStruct((length, width), LOW),
        compiler_params=params(),
        cost_estimate=LIGHT,
    )(left, right)


def split_shards(core, total, axis, first, kept_ref, sent_refs):
    shard = kept_ref.shape[1 + axis]
    count = total.shape[axis] // (2 * shard)

    def cut(index):
        span = slice(index * shard, (index + 1) * shard)
        return total[span] if axis == 0 else total[:, span]

    for index in range(count):
        even, odd = cut(2 * index), cut(2 * index + 1)
        kept_ref[index] = jnp.where(core == 0, even, odd).astype(LOW)
        sent = jnp.where(core == 0, odd, even).astype(LOW)
        if axis == 1:
            sent_refs[index][...] = sent
        else:
            for chip in range(index, len(sent_refs), count):

                @pl.when(first + index == chip)
                def _():
                    sent_refs[chip][...] = sent


def grad_body(count, axis, core_ref, *refs):
    total = None
    for index in range(count):
        product = lax.dot_general(
            refs[index][...], refs[count + index][...], TN, preferred_element_type=FULL
        )
        total = product if total is None else total + product
    kept_ref, sent_refs = refs[2 * count], refs[2 * count + 1 :]
    first = pl.program_id(0) * kept_ref.shape[0] if axis == 0 else 0
    split_shards(core_ref[0], total, axis, first, kept_ref, sent_refs)


def weight_grad(core, lefts, rights, chips, axis):
    depth = lefts[0].shape[1]
    width = rights[0].shape[1]
    tile = min(512, depth)
    shards = 2 * chips
    if axis == 1:
        shape = (depth, width // shards)
        spec = pl.BlockSpec((chips, tile, width // shards), lambda i, c: (0, i, 0))
        sent = pl.BlockSpec((tile, width // shards), lambda i, c: (i, 0))
    else:
        shape = (depth // shards, width)
        spec = pl.BlockSpec((tile * chips // depth, depth // shards, width), lambda i, c: (i, 0, 0))
        sent = pl.BlockSpec(shape, lambda i, c: (0, 0))
    out = pl.pallas_call(
        functools.partial(grad_body, len(lefts), axis),
        grid_spec=pltpu.PrefetchScalarGridSpec(
            num_scalar_prefetch=1,
            grid=(depth // tile,),
            in_specs=[pl.BlockSpec((left.shape[0], tile), lambda i, c: (0, i)) for left in lefts]
            + [pl.BlockSpec(right.shape, lambda i, c: (0, 0)) for right in rights],
            out_specs=[spec] + [sent] * chips,
        ),
        out_shape=[jax.ShapeDtypeStruct((chips, *shape), LOW)] + [jax.ShapeDtypeStruct(shape, LOW)] * chips,
        compiler_params=params(),
        cost_estimate=LIGHT,
    )(core, *lefts, *rights)
    return out[0], out[1:]


def project_grad_body(core_ref, left_ref, right_ref, kept_ref, *sent_refs):
    products = [
        lax.dot_general(left_ref[...], right_ref[part], TN, preferred_element_type=FULL)
        for part in range(3)
    ]
    first = pl.program_id(0) * kept_ref.shape[0]
    split_shards(core_ref[0], jnp.concatenate(products, axis=1), 0, first, kept_ref, sent_refs)


def project_grad(core, left, right, chips):
    length, depth = left.shape
    cols = right.shape[2]
    tile = min(512, depth)
    shards = 2 * chips
    shape = (depth // shards, 3 * cols)
    out = pl.pallas_call(
        project_grad_body,
        grid_spec=pltpu.PrefetchScalarGridSpec(
            num_scalar_prefetch=1,
            grid=(depth // tile,),
            in_specs=[
                pl.BlockSpec((length, tile), lambda i, c: (0, i)),
                pl.BlockSpec(right.shape, lambda i, c: (0, 0, 0)),
            ],
            out_specs=[pl.BlockSpec((tile * chips // depth, *shape), lambda i, c: (i, 0, 0))]
            + [pl.BlockSpec(shape, lambda i, c: (0, 0))] * chips,
        ),
        out_shape=[jax.ShapeDtypeStruct((chips, *shape), LOW)] + [jax.ShapeDtypeStruct(shape, LOW)] * chips,
        compiler_params=params(),
        cost_estimate=LIGHT,
    )(core, left, right)
    return out[0], out[1:]


def core_add_body(kept_ref, *refs):
    for index, arrived in enumerate(refs[:-1]):
        refs[-1][index] = (kept_ref[index].astype(FULL) + arrived[...].astype(FULL)).astype(LOW)


def core_add_kernel(kept, arrived):
    chips, rows, width = kept.shape
    tile = min(rows, max(16, rows // 4))
    spec = pl.BlockSpec((chips, tile, width), lambda i: (0, i, 0))
    return pl.pallas_call(
        core_add_body,
        grid=(rows // tile,),
        in_specs=[spec] + [pl.BlockSpec((tile, width), lambda i: (i, 0))] * chips,
        out_specs=spec,
        out_shape=jax.ShapeDtypeStruct(kept.shape, LOW),
        compiler_params=params(),
        cost_estimate=LIGHT,
    )(kept, *arrived)


def core_add_apart_body(count, chip_ref, kept_ref, *refs):
    for index in range(count):
        total = (kept_ref[index].astype(FULL) + refs[index][...].astype(FULL)).astype(LOW)
        for mask in range(count):

            @pl.when((chip_ref[0] ^ index) == mask)
            def _():
                refs[count + mask][...] = total


def core_add_apart(chip, kept, arrived):
    chips, rows, width = kept.shape
    tile = min(rows, max(16, rows // 4))
    spec = pl.BlockSpec((tile, width), lambda i, c: (i, 0))
    return pl.pallas_call(
        functools.partial(core_add_apart_body, chips),
        grid_spec=pltpu.PrefetchScalarGridSpec(
            num_scalar_prefetch=1,
            grid=(rows // tile,),
            in_specs=[pl.BlockSpec((chips, tile, width), lambda i, c: (0, i, 0))] + [spec] * chips,
            out_specs=[spec] * chips,
        ),
        out_shape=[jax.ShapeDtypeStruct((rows, width), LOW)] * chips,
        compiler_params=params(),
        cost_estimate=LIGHT,
    )(chip.reshape(1).astype(jnp.int32), kept, *arrived)


def add_many_body(*refs):
    total = refs[0][...].astype(FULL)
    for ref in refs[1:-1]:
        total = total + ref[...].astype(FULL)
    refs[-1][...] = total.astype(LOW)


def add_many(values):
    rows, width = values[0].shape
    tile = max(16, rows // 4)
    spec = pl.BlockSpec((tile, width), lambda i: (i, 0))
    return pl.pallas_call(
        add_many_body,
        grid=(rows // tile,),
        in_specs=[spec] * len(values),
        out_specs=spec,
        out_shape=jax.ShapeDtypeStruct((rows, width), LOW),
        compiler_params=params(),
        cost_estimate=LIGHT,
    )(*values)


def ring_add_body(place_ref, arrived_ref, part_ref, out_ref):
    out_ref[...] = (arrived_ref[...].astype(FULL) + part_ref[...].astype(FULL)).astype(out_ref.dtype)


def ring_add(place, arrived, part, kind):
    rows, width = arrived.shape
    return pl.pallas_call(
        ring_add_body,
        grid_spec=pltpu.PrefetchScalarGridSpec(
            num_scalar_prefetch=1,
            grid=(1,),
            in_specs=[
                pl.BlockSpec((rows, width), lambda i, p: (0, 0)),
                pl.BlockSpec((rows, width), lambda i, p: (p[0], 0)),
            ],
            out_specs=pl.BlockSpec((rows, width), lambda i, p: (0, 0)),
        ),
        out_shape=jax.ShapeDtypeStruct((rows, width), kind),
        compiler_params=params(),
        cost_estimate=LIGHT,
    )(place.reshape(1).astype(jnp.int32), arrived, part)


def pair_add_body(count, place_ref, *refs):
    out_ref = refs[-1]
    rows = refs[0].shape[0]
    for half in range(2):
        span = slice(half * rows, (half + 1) * rows)
        total = refs[half][...].astype(FULL)
        if count > 2:
            total = total + refs[2][span].astype(FULL)
        if count > 3:
            total = total + refs[3 + half][...]
        out_ref[span] = total.astype(out_ref.dtype)


def pair_add(place, block_rows, parts, arrived, bases, kind):
    rows, width = 2 * block_rows, parts[0].shape[1]
    block = pl.BlockSpec((rows // 2, width), lambda i, p: (p[0], 0))
    whole = pl.BlockSpec((rows, width), lambda i, p: (0, 0))
    half = pl.BlockSpec((rows // 2, width), lambda i, p: (0, 0))
    operands, in_specs = list(parts), [block, block]
    if arrived is not None:
        operands.append(arrived)
        in_specs.append(whole)
    if bases is not None:
        operands += bases
        in_specs += [half, half]
    return pl.pallas_call(
        functools.partial(pair_add_body, len(operands)),
        grid_spec=pltpu.PrefetchScalarGridSpec(
            num_scalar_prefetch=1, grid=(1,), in_specs=in_specs, out_specs=whole
        ),
        out_shape=jax.ShapeDtypeStruct((rows, width), kind),
        compiler_params=params(),
        cost_estimate=LIGHT,
    )(place.reshape(1).astype(jnp.int32), *operands)


def round_body(count, in_ref, *out_refs):
    rows = in_ref.shape[0] // count
    for index in range(count):
        out_refs[index][...] = in_ref[index * rows : (index + 1) * rows].astype(LOW)


def round_low(value, count):
    rows, width = value.shape
    tile = min(width, 512)
    return pl.pallas_call(
        functools.partial(round_body, count),
        grid=(width // tile,),
        in_specs=[pl.BlockSpec((rows, tile), lambda i: (0, i))],
        out_specs=[pl.BlockSpec((rows // count, tile), lambda i: (0, i))] * count,
        out_shape=[jax.ShapeDtypeStruct((rows // count, width), LOW)] * count,
        compiler_params=params(),
        cost_estimate=LIGHT,
    )(value)


def norm_back_body(count, steps, place_ref, source_ref, arrived_ref, part_ref, gain_ref, *refs):
    bases, out_refs = refs[:count], refs[count:]
    base = bases[0][...]
    if count == 2:
        base = jnp.where(pl.program_id(0) < steps // 2, base, bases[1][...])
    source = source_ref[...].astype(FULL)
    back = arrived_ref[...].astype(FULL) + part_ref[...].astype(FULL)
    inverse = lax.rsqrt(jnp.mean(source * source, axis=-1, keepdims=True) + NORM_EPS)
    normal = source * inverse
    scaled = gain_ref[...] * back
    grad = base + inverse * (scaled - normal * jnp.mean(normal * scaled, axis=-1, keepdims=True))
    out_refs[0][...] = grad
    total = jnp.sum(back * normal, axis=0, keepdims=True)

    @pl.when(pl.program_id(0) == 0)
    def _():
        out_refs[1][...] = total

    @pl.when(pl.program_id(0) > 0)
    def _():
        out_refs[1][...] += total

    if len(out_refs) > 2:
        out_refs[2][...] = grad.astype(LOW)


def norm_back(place, source, arrived, part, gain, bases, base_first, low):
    rows, width = source.shape
    tile = min(rows, 64)
    steps = rows // tile
    row = pl.BlockSpec((tile, width), lambda i, p: (i, 0))
    whole = pl.BlockSpec((1, width), lambda i, p: (0, 0))
    shapes = [jax.ShapeDtypeStruct((rows, width), FULL), jax.ShapeDtypeStruct((1, width), FULL)]
    out_specs = [row, whole]
    if len(bases) == 1:
        base_specs = [pl.BlockSpec((tile, width), lambda i, p: (base_first // tile + i, 0))]
    else:
        base_specs = [
            pl.BlockSpec((tile, width), lambda i, p: (jnp.minimum(i, steps // 2 - 1), 0)),
            pl.BlockSpec((tile, width), lambda i, p: (jnp.maximum(i - steps // 2, 0), 0)),
        ]
    if low:
        shapes.append(jax.ShapeDtypeStruct((rows, width), LOW))
        out_specs.append(row)
    return pl.pallas_call(
        functools.partial(norm_back_body, len(bases), steps),
        grid_spec=pltpu.PrefetchScalarGridSpec(
            num_scalar_prefetch=1,
            grid=(steps,),
            in_specs=[
                row,
                row,
                pl.BlockSpec((tile, width), lambda i, p: (p[0] * steps + i, 0)),
                whole,
            ]
            + base_specs,
            out_specs=out_specs,
        ),
        out_shape=shapes,
        compiler_params=params(),
        cost_estimate=LIGHT,
    )(place.reshape(1).astype(jnp.int32), source, arrived, part, gain, *bases)


def mix_back_body(place_ref, low_ref, weight_ref, *out_refs):
    total = None
    shards, _, _, shard = weight_ref.shape
    for index in range(shards):
        left = low_ref[:, index * shard : (index + 1) * shard]
        product = lax.dot_general(left, weight_ref[index, 0], NT, preferred_element_type=FULL)
        total = product if total is None else total + product
    value = total.astype(LOW)
    for step, out in enumerate(out_refs):

        @pl.when(pl.program_id(0) == step)
        def _():
            out[...] = value


def mix_back(targets, low, weight):
    rows, width = low.shape
    shards, count, cols, shard = weight.shape
    spec = pl.BlockSpec((rows, cols), lambda i, p: (0, 0))
    return pl.pallas_call(
        mix_back_body,
        grid_spec=pltpu.PrefetchScalarGridSpec(
            num_scalar_prefetch=1,
            grid=(count,),
            in_specs=[
                pl.BlockSpec((rows, width), lambda i, p: (0, 0)),
                pl.BlockSpec((shards, 1, cols, shard), lambda i, p: (0, p[i], 0, 0)),
            ],
            out_specs=[spec] * count,
        ),
        out_shape=[jax.ShapeDtypeStruct((rows, cols), LOW)] * count,
        compiler_params=params(),
        cost_estimate=LIGHT,
    )(targets, low, weight)


def project_back_body(place_ref, back_ref, weight_ref, out_ref):
    total = None
    for part in range(3):
        product = lax.dot_general(back_ref[part], weight_ref[part], NT, preferred_element_type=FULL)
        total = product if total is None else total + product
    out_ref[...] = total.astype(LOW)


def project_back(place, back, weight, rows):
    _, width, cols = weight.shape
    tile = min(512, width)
    return pl.pallas_call(
        project_back_body,
        grid_spec=pltpu.PrefetchScalarGridSpec(
            num_scalar_prefetch=1,
            grid=(width // tile,),
            in_specs=[
                pl.BlockSpec((3, rows, cols), lambda i, p: (0, p[0], 0)),
                pl.BlockSpec((3, tile, cols), lambda i, p: (0, i, 0)),
            ],
            out_specs=pl.BlockSpec((rows, tile), lambda i, p: (0, i)),
        ),
        out_shape=jax.ShapeDtypeStruct((rows, width), LOW),
        compiler_params=params(),
        cost_estimate=LIGHT,
    )(place.reshape(1), back, weight)


def adam_step(weight, grad, first, second, factor, rate, decay):
    clipped = grad * factor
    first_new = BETA_ONE * first + (1.0 - BETA_ONE) * clipped
    second_new = BETA_TWO * second + (1.0 - BETA_TWO) * clipped * clipped
    first_hat = first_new / (1.0 - BETA_ONE**STEP)
    second_hat = second_new / (1.0 - BETA_TWO**STEP)
    weight_new = weight - rate * (first_hat / (jnp.sqrt(second_hat) + ADAM_EPS) + decay * weight)
    return (weight_new, weight_new.astype(LOW), first_new, second_new)


def adam_body(rates, factor_ref, *refs):
    count = len(rates)
    factor = factor_ref[0]
    for index, rate in enumerate(rates):
        weight, grad, first, second = refs[4 * index : 4 * index + 4]
        outs = refs[4 * count + 4 * index : 4 * count + 4 * index + 4]
        if len(weight.shape) == 3:
            cols = weight.shape[2]
            for part in range(weight.shape[0]):
                piece = grad[:, part * cols : (part + 1) * cols].astype(FULL)
                new = adam_step(weight[part], piece, first[part], second[part], factor, rate, DECAY_RATE)
                for out, value in zip(outs, new):
                    out[part] = value
        else:
            new = adam_step(weight[...], grad[...].astype(FULL), first[...], second[...], factor, rate, DECAY_RATE)
            for out, value in zip(outs, new):
                out[...] = value


def adam_all(factor, groups, rates):
    steps = 8
    for weight, _, _, _ in groups:
        steps = min(steps, weight.shape[-2] // 16)
    in_specs, out_specs, shapes, operands = [], [], [], []
    for weight, grad, first, second in groups:
        rows, cols = weight.shape[-2] // steps, weight.shape[-1]
        if weight.ndim == 3:
            spec = pl.BlockSpec((weight.shape[0], rows, cols), lambda i, f: (0, i, 0))
        else:
            spec = pl.BlockSpec((rows, cols), lambda i, f: (i, 0))
        grad_spec = pl.BlockSpec((rows, grad.shape[1]), lambda i, f: (i, 0))
        in_specs += [spec, grad_spec, spec, spec]
        out_specs += [spec] * 4
        operands += [weight, grad, first, second]
        for kind in (FULL, LOW, FULL, FULL):
            shapes.append(jax.ShapeDtypeStruct(weight.shape, kind))
    out = pl.pallas_call(
        functools.partial(adam_body, rates),
        grid_spec=pltpu.PrefetchScalarGridSpec(
            num_scalar_prefetch=1, grid=(steps,), in_specs=in_specs, out_specs=out_specs
        ),
        out_shape=shapes,
        compiler_params=params(),
        cost_estimate=LIGHT,
    )(factor.reshape(1), *operands)
    return [tuple(out[4 * index : 4 * index + 4]) for index in range(len(groups))]


def lay_body(spots, me_ref, *refs):
    count = len(spots)
    out_ref = refs[count]
    for piece, spot in zip(refs, spots):
        if isinstance(spot, tuple):
            rows = piece.shape[0]
            out_ref[me_ref[0] ^ spot[0], spot[1] * rows : (spot[1] + 1) * rows] = piece[...]
        else:
            out_ref[lax.rem(me_ref[0] + count - spot, count)] = piece[...]


def lay(me, pieces, spots):
    rows, width = pieces[0].shape
    if isinstance(spots[0], tuple):
        shape = (len(pieces) // 2, 2 * rows, width)
    else:
        shape = (len(pieces), rows, width)
    return pl.pallas_call(
        functools.partial(lay_body, spots),
        in_specs=[pl.BlockSpec(memory_space=pltpu.SMEM)] + [pl.BlockSpec(memory_space=pltpu.VMEM)] * len(pieces),
        out_specs=pl.BlockSpec(memory_space=pltpu.VMEM),
        out_shape=jax.ShapeDtypeStruct(shape, LOW),
        compiler_params=params(),
        cost_estimate=LIGHT,
    )(me.reshape(1).astype(jnp.int32), *pieces)


def lay_cores_body(core_ref, mine_ref, other_ref, out_ref):
    mine, other = mine_ref[...], other_ref[...]
    out_ref[0, 0] = jnp.where(core_ref[0] == 0, mine, other)[0]
    out_ref[0, 1] = jnp.where(core_ref[0] == 0, other, mine)[0]


def lay_cores(core, mine, other):
    chips, rows, width = mine.shape
    spec = pl.BlockSpec((1, rows, width), lambda i, c: (i, 0, 0))
    return pl.pallas_call(
        lay_cores_body,
        grid_spec=pltpu.PrefetchScalarGridSpec(
            num_scalar_prefetch=1,
            grid=(chips,),
            in_specs=[spec, spec],
            out_specs=pl.BlockSpec((1, 2, rows, width), lambda i, c: (i, 0, 0, 0)),
        ),
        out_shape=jax.ShapeDtypeStruct((chips, 2, rows, width), LOW),
        compiler_params=params(),
        cost_estimate=LIGHT,
    )(core, mine, other)


def squares(value):
    wide = value.astype(FULL)
    return jnp.sum(wide * wide)


def after(value, *others):
    if not others:
        return value
    return lax.optimization_barrier((value, *others))[0]


def per_device(
    chips,
    cores,
    bkts,
    block_in,
    cotangent,
    buckets,
    qkv_weight,
    qkv_first,
    qkv_second,
    out_weight,
    out_first,
    out_second,
    up_weight,
    up_first,
    up_second,
    down_weight,
    down_first,
    down_second,
    norm_gains,
    gains_first,
    gains_second,
):
    toks = chips * cores
    tok = ("chip", "core")
    group = lax.axis_index("bkt")
    core = lax.axis_index("core")
    chip = lax.axis_index("chip")
    core_id = core.reshape(1).astype(jnp.int32)
    rows, width = block_in.shape
    half = rows // 2
    length = rows * bkts
    ring = [(i, (i + 1) % bkts) for i in range(bkts)]

    last = []

    def at(value, *others):
        return after(value, *last, *others)

    def did(value):
        last[:] = [value]
        return value

    def wait(value):
        return did(after(value, *last))

    def pass_on(name, value, *others):
        with jax.named_scope(name):
            return lax.ppermute(at(value, *others), "bkt", ring)

    def owner(step):
        return lax.rem(group - step + bkts, bkts)

    places = jnp.stack([owner(step) for step in range(bkts)]).astype(jnp.int32)

    def rows_of(value, step):
        size = value.shape[0] // bkts
        return lax.dynamic_slice_in_dim(value, owner(step) * size, size, 0)

    def add(arrived, value, step):
        return did(ring_add(owner(step), at(arrived), value, LOW))

    def add_final(arrived, value):
        return did(ring_add(owner(0), at(arrived), value, FULL))

    def swap(name, values):
        with jax.named_scope(name + "_swap"):
            return [lax.ppermute(at(value), "core", [(0, 1), (1, 0)]) for value in values]

    def core_add(kept, arrived):
        return did(core_add_kernel(at(kept), arrived))

    def chip_sum(value):
        value = value.reshape(chips * value.shape[1], *value.shape[2:])
        return lax.psum_scatter(value, "chip", scatter_dimension=0, tiled=True)

    by_bits = chips & (chips - 1) == 0

    qkv_full = lax.all_gather(did(qkv_weight.astype(LOW)), tok, axis=1, tiled=True)
    x_held = [block_in, pass_on("x1", block_in)]
    (out_low,) = round_low(at(out_weight), 1)
    did(out_low)
    x_held[1] = wait(x_held[1])
    x_held.append(pass_on("x2", x_held[1]))
    out_held = [out_low, pass_on("out1", out_low)]
    (up_low,) = round_low(at(up_weight), 1)
    up_full = lax.all_gather(did(up_low), tok, axis=0, tiled=True)
    gain_width = norm_gains.shape[1]
    gain_line = jnp.zeros((toks, 2, gain_width), FULL)
    gain_line = lax.dynamic_update_slice(
        gain_line, norm_gains.astype(LOW).astype(FULL)[None], (lax.axis_index(tok), 0, 0)
    )
    if by_bits:
        for axis, size in (("core", cores), ("chip", chips)):
            for bit in range(size.bit_length() - 1):
                perm = [(i, i ^ (1 << bit)) for i in range(size)]
                with jax.named_scope("gains"):
                    gain_line = did(gain_line + lax.ppermute(at(gain_line), axis, perm))
    else:
        gain_line = did(lax.psum(at(gain_line), tok))
    gain_float = did(gain_line.transpose(1, 0, 2).reshape(2, width))
    cosine, sine = rotary_tables(length)
    for step in range(3, bkts):
        x_held[-1] = wait(x_held[-1])
        out_held[-1] = wait(out_held[-1])
        x_held.append(pass_on("x" + str(step), x_held[-1], cosine, sine))
        out_held.append(pass_on("out" + str(step - 1), out_held[-1]))

    carried = None
    for step in range(bkts - 1):
        carried = project(
            owner(step).reshape(1), at(x_held[step]), gain_float[0:1], qkv_full, cosine, sine, carried
        )
        did(carried[0])
    x_held[-1] = wait(x_held[-1])
    out_held[-1] = wait(out_held[-1])
    out_held.append(pass_on("out" + str(bkts - 1), out_held[-1]))
    normed_one, qkv, seq_in = project(
        owner(bkts - 1).reshape(1), at(x_held[-1]), gain_float[0:1], qkv_full, cosine, sine, carried
    )
    did(normed_one)
    out_held[-1] = wait(out_held[-1])
    out_depth, out_width = out_weight.shape
    out_line = did(lay(group, [at(out_held[0])] + out_held[1:], list(range(bkts))))
    out_full = lax.all_gather(after(out_line, up_full), tok, axis=0, tiled=False)
    (down_low,) = round_low(at(down_weight), 1)
    down_full = lax.all_gather(did(down_low), tok, axis=1, tiled=True)
    cols = qkv.shape[2]
    seq_in = seq_in.reshape(bkts, rows, width)

    slab, log_a = attend(0, bkts, at(qkv), cotangent)
    slabs = [[did(slab)], []]

    def next_slab(part):
        held = slabs[part]
        if len(held) > 1:
            held[-1] = wait(held[-1])
        held.append(pass_on("slab" + "ab"[part] + str(len(held)), held[-1]))

    next_slab(0)
    slab, log_b = attend(1, bkts, at(qkv), cotangent)
    slabs[1].append(did(slab))
    logs = [log_a, log_b]
    for step in range(2, bkts):
        next_slab(0)
    slabs[0][-1] = wait(slabs[0][-1])
    for step in range(1, bkts - 2):
        next_slab(1)

    live = (buckets >= group).astype(FULL)
    acc = did(mix_first(0, places, at(seq_in), slabs[0][:-1], out_full))
    normed_a, middle_a, mixed_a = mix_last(places, acc, gain_float[1:2], slabs[0], out_full)
    did(normed_a)
    next_slab(1)
    hidden_a, inner_a, low_a = hidden_units(places, live, at(normed_a), up_full, down_full, slabs[0])
    did(inner_a)
    next_slab(1)
    back_a = did(product(at(inner_a), up_full, True))
    sum_a = did(rows_of(back_a, 1))
    arrived_a = pass_on("sum_a1", sum_a)
    acc = did(mix_first(1, places, at(seq_in), slabs[1][:-1], out_full))
    prod_a = did(product(at(hidden_a), down_full, False))
    slabs[1][-1] = wait(slabs[1][-1])
    normed_b, middle_b, mixed_b = mix_last(places, at(acc), gain_float[1:2], slabs[1], out_full)
    did(normed_b)
    sum_a = add(arrived_a, back_a, 2)
    arrived_a = pass_on("sum_a2", sum_a)

    hidden_b, inner_b, low_b = hidden_units(places, live, at(normed_b), up_full, down_full, slabs[1])
    did(inner_b)
    sum_a = add(arrived_a, back_a, 3)
    arrived_a = pass_on("sum_a3", sum_a)
    back_b = did(product(at(inner_b), up_full, True))
    prod_b = did(product(at(hidden_b), down_full, False))
    arrived_a = wait(arrived_a)
    sum_b = did(rows_of(at(back_b), 1))
    arrived_b = pass_on("sum_b1", sum_b)

    first = jnp.zeros((), jnp.int32)
    targets = jnp.stack([lax.rem(group + step, bkts) for step in range(bkts)]).astype(jnp.int32)

    def middle_back(part, middle, arrived, back):
        grad, gain_sum, low = norm_back(
            owner(0), middle, at(arrived), back, gain_float[1:2], [cotangent], part * half, True
        )
        found = list(mix_back(targets, low, out_full))
        did(found[0])
        return grad, low, gain_sum, found

    def exchange(part, found):
        with jax.named_scope("exchange" + str(part)):
            for step in range(1, bkts):
                found[step] = lax.ppermute(
                    at(found[step]), "bkt", [(i, (i + step) % bkts) for i in range(bkts)]
                )

    grad_a, mid_low_a, gain_a, pieces_a = middle_back(0, middle_a, arrived_a, back_a)
    sum_b = add(arrived_b, back_b, 2)
    exchange(0, pieces_a)
    arrived_b = pass_on("sum_b2", sum_b)
    up_kept, up_sent = weight_grad(core_id, [normed_a, normed_b], [at(inner_a), inner_b], chips, 0)
    did(up_kept)
    pieces_a = pieces_a[:1] + [wait(piece) for piece in pieces_a[1:]]
    sum_b = add(arrived_b, back_b, 3)
    up_arrived = swap("up_grad", up_sent)
    arrived_b = pass_on("sum_b3", sum_b)
    down_kept, down_sent = weight_grad(core_id, [hidden_a, hidden_b], [at(low_a), low_b], chips, 1)
    did(down_kept)
    arrived_b = wait(arrived_b)
    up_core = core_add(up_kept, up_arrived)
    up_part = chip_sum(up_core)
    grad_b, mid_low_b, gain_b, pieces_b = middle_back(1, middle_b, arrived_b, back_b)
    exchange(1, pieces_b)
    out_kept, out_sent = weight_grad(
        core_id, [at(mixed_a), mixed_b], [mid_low_a, mid_low_b], chips, 1
    )
    did(out_kept)
    prods = [prod_a, prod_b]
    ffn = did(pair_add(owner(1), half, [at(prod_a), prod_b], None, None, LOW))
    pieces_b = pieces_b[:1] + [wait(piece) for piece in pieces_b[1:]]
    down_arrived = swap("down_grad", down_sent)
    out_arrived = swap("out_grad", out_sent)
    arrived_f = pass_on("ffn1", ffn)

    back_project = did(attend_back(places, at(qkv), pieces_a + pieces_b, logs, cosine, sine))
    total = did(project_back(owner(1), at(back_project), qkv_full, rows))
    arrived_f = wait(arrived_f)
    down_core = core_add(down_kept, down_arrived)
    down_part = chip_sum(down_core)
    direct = chips <= 4 and by_bits

    def out_plane(mask):
        with jax.named_scope("out_plane"):
            out_apart[mask] = lax.ppermute(
                at(out_apart[mask]), "chip", [(i, i ^ mask) for i in range(chips)]
            )

    if direct:
        out_apart = list(core_add_apart(chip, at(out_kept), out_arrived))
        did(out_apart[0])
        for mask in range(1, chips):
            if mask & (mask - 1) == 0:
                out_plane(mask)
    else:
        out_sum = chip_sum(core_add(out_kept, out_arrived))
    arrived = pass_on("back1", total)
    qkv_kept, qkv_sent = project_grad(core_id, normed_one, at(back_project), chips)
    did(qkv_kept)
    own = did(project_back(owner(2), at(back_project), qkv_full, rows))
    total = did(ring_add(first, at(arrived), own, LOW))
    if direct:
        for mask in range(1, chips):
            if mask & (mask - 1) == 0:
                out_apart[mask] = wait(out_apart[mask])
            else:
                out_plane(mask)
    qkv_arrived = swap("qkv_grad", qkv_sent)
    arrived = pass_on("back2", total)
    own = did(project_back(owner(3), at(back_project), qkv_full, rows))
    qkv_core = core_add(qkv_kept, qkv_arrived)
    qkv_part = chip_sum(qkv_core)
    last_own = did(project_back(owner(0), at(back_project), qkv_full, rows))
    total = did(ring_add(first, at(arrived), own, LOW))
    if direct:
        out_sum = add_many([at(out_apart[0])] + out_apart[1:])
    did(out_sum)
    arrived = pass_on("back3", total)
    arrived_out = pass_on("out_sum1", rows_of(out_sum, 1))
    for step in range(2, bkts):
        arrived_out = pass_on("out_sum" + str(step), add(arrived_out, out_sum, step))
    out_part = add_final(arrived_out, out_sum)
    out_squares = did(squares(at(out_part)))
    block_in_grad, gain_one = norm_back(
        first, block_in, at(arrived), last_own, gain_float[0:1], [grad_a, grad_b], 0, False
    )
    did(gain_one)
    ffn = did(pair_add(owner(2), half, prods, at(arrived_f), None, LOW))
    arrived_f = pass_on("ffn2", ffn)
    up_squares = did(squares(at(up_part)))
    down_squares = did(squares(at(down_part)))
    gain_grad_one = gain_one[0]
    gain_grad_two = (gain_a + gain_b)[0]

    weight_squares = did(up_squares + down_squares + out_squares + squares(at(qkv_part)))
    packed = jnp.concatenate(
        [gain_grad_one, gain_grad_two, jnp.broadcast_to(weight_squares, (HD,))]
    )
    for axis, size in (("core", cores), ("chip", chips), ("bkt", bkts)):
        if size & (size - 1):
            packed = lax.psum(packed, axis)
        else:
            step = 1
            while step < size:
                packed = packed + lax.ppermute(packed, axis, [(i, i ^ step) for i in range(size)])
                step *= 2
    did(packed)
    ffn = did(pair_add(owner(3), half, prods, at(arrived_f), None, LOW))
    arrived_f = pass_on("ffn3", ffn)
    gain_total = packed[: 2 * width].reshape(2, width)
    grad_norm = jnp.sqrt(packed[2 * width] + jnp.sum(gain_total * gain_total))
    factor = jnp.minimum(1.0, CLIP_NORM / grad_norm)
    gain_part = lax.dynamic_slice_in_dim(gain_total, lax.axis_index(tok) * gain_width, gain_width, 1)
    updated = adam_all(
        factor,
        [
            (qkv_weight, qkv_part, qkv_first, qkv_second),
            (out_weight, out_part, out_first, out_second),
            (up_weight, up_part, up_first, up_second),
            (down_weight, down_part, down_first, down_second),
        ],
        (D ** (-0.5), (H * HD // 16) ** (-0.5), D ** (-0.5), FF ** (-0.5)),
    )
    block_out = pair_add(
        owner(0), half, prods, after(arrived_f, updated[0][0]), [middle_a, middle_b], FULL
    )
    gain_out = adam_step(norm_gains, gain_part, gains_first, gains_second, factor, GAIN_RATE, 0.0)
    return (block_out, block_in_grad, grad_norm, *[value for new in updated for value in new], *gain_out)


def solution(mesh):
    toks, bkts = mesh.shape["tok"], mesh.shape["bkt"]
    cores = 2
    chips = toks // cores
    tok = ("chip", "core")
    rows = P(("chip", "core", "bkt"), None)
    qkv = P(None, tok, "bkt")
    tall = P("bkt", tok)
    wide = P(tok, "bkt")
    gains = P(None, tok)
    return jax.shard_map(
        functools.partial(per_device, chips, cores, bkts),
        mesh=Mesh(mesh.devices.reshape(chips, cores, bkts), ("chip", "core", "bkt")),
        in_specs=(rows, rows, P(tok), *[qkv] * 3, *[tall] * 3, *[wide] * 3, *[tall] * 3, *[gains] * 3),
        out_specs=(rows, rows, P(), *[qkv] * 4, *[tall] * 4, *[wide] * 4, *[tall] * 4, *[gains] * 4),
        check_vma=False,
    )
```

time: 850 us -> 689 us (0.81)
  Pallas kernels: 57.5 us -> 288 us
  waiting for transfers between devices: 454 us -> 247 us
  matrix products: 165 us -> 0 us
  other arithmetic: 51.1 us -> 14.8 us
  starting transfers between devices: 31.7 us -> 50.7 us
    pallas_call x3 -> x49, Pallas kernels: 30 us -> 261 us  [the longest x3 33.8 us: weight_grad(): pl.pallas_call(functools.partial(grad_body, len(lefts), axis), grid_spec=...]
    dot_general x24 -> x0, matrix products: 165 us -> none  [the longest x4 23.3 us: back_one_part(): jnp.einsum('cth,cdh->td', piece, qkv_full, preferred_element_type=FULL)]
    ppermute x33 -> x55, waiting for transfers between devices: 359 us -> 236 us  [the longest x27 195 us: pass_on(): return lax.ppermute(at(value, *others), 'bkt', ring)]
    reduce_scatter x4 -> x3, waiting for transfers between devices: 88.7 us -> 0.04 us  [chip_sum(): return lax.psum_scatter(value, 'chip', scatter_dimension=0, tiled=True)]
    unnamed x117 -> x222, local copies, waits for them, and re-layouts: 27.9 us -> 54.8 us
    convert_element_type x5 -> x1, other arithmetic: 19.5 us -> 0.62 us  [adam_step(): return (weight_new, weight_new.astype(LOW), first_new, second_new)]
    ppermute x33 -> x55, starting transfers between devices: 24.5 us -> 42.6 us  [the longest x27 25 us: pass_on(): return lax.ppermute(at(value, *others), 'bkt', ring)]
    dynamic_update_slice x18 -> x0, local copies, waits for them, and re-layouts: 14.5 us -> none  [the longest x3 7.01 us: per_device(): lax.dynamic_update_slice(seq_back, back_held[step][None], (owner(step), 0...]
  transfers between devices with their start and end apart: 46 -> 67, of which waited for: 31 -> 35; matrix products, arithmetic and copies ran while one was open for 24% -> 2% of each run, Pallas kernels for 7% -> 41%
where the time goes in v2:
time: 689 us; the launch traced here: 678 us
  Pallas kernels  288 us (42%)
  waiting for transfers between devices  247 us (36%)
  local copies, waits for them, and re-layouts  56.3 us (8%)
  starting transfers between devices  50.7 us (7%)
  between operations  21.5 us (3%)
  other arithmetic  14.8 us (2%)
    ppermute x27, waiting for transfers between devices, pass_on(): return lax.ppermute(at(value, *others), 'bkt', ring)  195 us
    unnamed x222, local copies, waits for them, and re-layouts  54.8 us
    pallas_call x3, Pallas kernels, weight_grad(): pl.pallas_call(functools.partial(grad_body, len(lefts), axis), grid_spec=...  33.8 us
    pallas_call x4, Pallas kernels, product(): pl.pallas_call(functools.partial(product_body, NT if turned else NN), gri...  29.5 us
    pallas_call x2, Pallas kernels, hidden_units(): pl.pallas_call(functools.partial(hidden_body, count), grid_spec=pltpu.Pre...  28.7 us
    pallas_call x4, Pallas kernels, project(): pl.pallas_call(project_body, grid_spec=pltpu.PrefetchScalarGridSpec(num_s...  27.4 us
    ppermute x3, waiting for transfers between devices, out_plane(): lax.ppermute(at(out_apart[mask]), 'chip', [(i, i ^ mask) for i in range(c...  25.7 us
    ppermute x27, starting transfers between devices, pass_on(): return lax.ppermute(at(value, *others), 'bkt', ring)  25 us
  transfers between devices with their start and end apart: 67, of which 35 were waited for; matrix products, arithmetic and copies ran while one was open for 2% of the time, Pallas kernels for 41%

profile of v2, /device:TPU:0, one launch (start us, length us, event | category | flops | bytes accessed | tf_op | source)
XLA Modules:
  0.0 678.4 jit_solution(11979366970146585419)
XLA Ops:
  14.0 24.2 %collective-permute-done.x_ref = bf16[256,2048]{1,0:T(8,128)(2,1)} collective-permute-done((bf16[256,2048]{1,0:T(8,128)(2,1)S(1)}, bf16[256,2048]{1,0:T(8,128)(2,1)}, u32[]{:S(2)}, u32[]{:S(2)}) %collective-permute-start) | collective-permute-done | bytes 1048608 | tf_op jit(solution)/shard_map/x1/ppermute | solution.py:966
  44.6 23.6 %collective-permute-done.1.x_ref = bf16[256,2048]{1,0:T(8,128)(2,1)} collective-permute-done((bf16[256,2048]{1,0:T(8,128)(2,1)}, bf16[256,2048]{1,0:T(8,128)(2,1)}, u32[]{:S(2)}, u32[]{:S(2)}) %collective-permute-start.1) | collective-permute-done | bytes 1048608 | tf_op jit(solution)/shard_map/x2/ppermute | solution.py:966
  122.4 8.4 %shard_map.361 = (bf16[1024,512]{1,0:T(8,128)(2,1)S(1)}, f32[512,512]{1,0:T(8,128)S(1)}) custom-call(bf16[3,1024,512]{2,1,0:T(8,128)(2,1)} %copy-done, bf16[3,1024,512]{2,1,0:T(8,128)(2,1)} %copy-done, bf16[3,1024,512]{2,1,0:T(8,128)(2,1)} %copy-done, f32[256,2048]{1,0:T(8,128)S(1)} %copy-done.1, f32[256,2048]{1,0:T(8,128)S(1)} %copy-done.1, ...), custom_call_target="tpu_custom_call" | custom-call | flops 1 | bytes 1 | tf_op jit(solution)/shard_map/pallas_call | solution.py:152
  133.7 8.5 %shard_map.362 = (bf16[1024,512]{1,0:T(8,128)(2,1)S(1)}, f32[512,512]{1,0:T(8,128)S(1)}) custom-call(bf16[3,1024,512]{2,1,0:T(8,128)(2,1)} %copy-done, bf16[3,1024,512]{2,1,0:T(8,128)(2,1)} %copy-done, bf16[3,1024,512]{2,1,0:T(8,128)(2,1)} %copy-done, f32[256,2048]{1,0:T(8,128)S(1)} %copy-done.1, f32[256,2048]{1,0:T(8,128)S(1)} %copy-done.1, ...), custom_call_target="tpu_custom_call" | custom-call | flops 1 | bytes 1 | tf_op jit(solution)/shard_map/pallas_call | solution.py:152
  143.2 14.3 %collective-permute-done.9.rest_1_ = bf16[1024,512]{1,0:T(8,128)(2,1)S(1)} collective-permute-done((bf16[1024,512]{1,0:T(8,128)(2,1)S(1)}, bf16[1024,512]{1,0:T(8,128)(2,1)S(1)}, u32[]{:S(2)}, u32[]{:S(2)}) %collective-permute-start.9) | collective-permute-done | bytes 1048608 | tf_op jit(solution)/shard_map/slaba1/ppermute | solution.py:966
  158.9 23.4 %collective-permute-done.10.rest_2_ = bf16[1024,512]{1,0:T(8,128)(2,1)S(1)} collective-permute-done((bf16[1024,512]{1,0:T(8,128)(2,1)S(1)}, bf16[1024,512]{1,0:T(8,128)(2,1)S(1)}, u32[]{:S(2)}, u32[]{:S(2)}) %collective-permute-start.10) | collective-permute-done | bytes 1048608 | tf_op jit(solution)/shard_map/slaba2/ppermute | solution.py:966
  183.3 22.9 %collective-permute-done.11.rest_3_ = bf16[1024,512]{1,0:T(8,128)(2,1)S(1)} collective-permute-done((bf16[1024,512]{1,0:T(8,128)(2,1)S(1)}, bf16[1024,512]{1,0:T(8,128)(2,1)S(1)}, u32[]{:S(2)}, u32[]{:S(2)}) %collective-permute-start.11) | collective-permute-done | bytes 1048608 | tf_op jit(solution)/shard_map/slaba3/ppermute | solution.py:966
  209.9 8.2 %shard_map.363.acc_ref = f32[512,2048]{1,0:T(8,128)} custom-call(s32[4]{0:T(128)S(1)} %pad_add_fusion.place_ref, bf16[4,256,2048]{2,1,0:T(8,128)(2,1)} %bitcast.46, bf16[1024,512]{1,0:T(8,128)(2,1)S(1)} %get-tuple-element.274.rest_0_, bf16[1024,512]{1,0:T(8,128)(2,1)S(1)} %copy-done.22, bf16[1024,512]{1,0:T(8,128)(2,1)S(1)} %copy-done.25, ...), custom_call_target="tpu_custom_call" | custom-call | flops 1 | bytes 1 | tf_op jit(solution)/shard_map/pallas_call | solution.py:275
  235.9 14.5 %shard_map.365 = (bf16[512,2048]{1,0:T(8,128)(2,1)}, bf16[512,2048]{1,0:T(8,128)(2,1)}, bf16[512,2048]{1,0:T(8,128)(2,1)}) custom-call(s32[4]{0:T(128)S(1)} %pad_add_fusion.place_ref, f32[1]{0:T(128)S(6)} %convert_element_type.48.live_ref, bf16[512,2048]{1,0:T(8,128)(2,1)} %get-tuple-element.287.normed_ref.refs_0_, ...), custom_call_target="tpu_custom_call" | custom-call | flops 1 | bytes 1 | tf_op jit(solution)/shard_map/pallas_call | solution.py:373
  262.4 8.4 %shard_map.367.acc_ref = f32[512,2048]{1,0:T(8,128)} custom-call(s32[4]{0:T(128)S(1)} %pad_add_fusion.place_ref, bf16[4,256,2048]{2,1,0:T(8,128)(2,1)} %bitcast.47, bf16[1024,512]{1,0:T(8,128)(2,1)S(1)} %get-tuple-element.285.rest_0_, bf16[1024,512]{1,0:T(8,128)(2,1)S(1)} %collective-permute-done.12.rest_1_, ...), custom_call_target="tpu_custom_call" | custom-call | flops 1 | bytes 1 | tf_op jit(solution)/shard_map/pallas_call | solution.py:275
  289.3 14.2 %shard_map.371 = (bf16[512,2048]{1,0:T(8,128)(2,1)}, bf16[512,2048]{1,0:T(8,128)(2,1)}, bf16[512,2048]{1,0:T(8,128)(2,1)}) custom-call(s32[4]{0:T(128)S(1)} %pad_add_fusion.place_ref, f32[1]{0:T(128)S(6)} %convert_element_type.48.live_ref, bf16[512,2048]{1,0:T(8,128)(2,1)} %get-tuple-element.301.normed_ref.refs_1_, ...), custom_call_target="tpu_custom_call" | custom-call | flops 1 | bytes 1 | tf_op jit(solution)/shard_map/pallas_call | solution.py:373
  312.3 7.9 %shard_map.374.refs_1_ = bf16[512,2048]{1,0:T(8,128)(2,1)S(1)} custom-call(bf16[512,2048]{1,0:T(8,128)(2,1)S(1)} %copy-done.31, bf16[2048,2048]{1,0:T(8,128)(2,1)} %all-gather.10.cloned.1.call-done.down_ref.right_ref), custom_call_target="tpu_custom_call" | custom-call | flops 1 | bytes 1 | tf_op jit(solution)/shard_map/pallas_call | solution.py:414
  344.3 14.0 %shard_map.378 = (bf16[4,256,2048]{2,1,0:T(8,128)(2,1)}, bf16[256,2048]{1,0:T(8,128)(2,1)S(1)}, bf16[256,2048]{1,0:T(8,128)(2,1)S(1)}, bf16[256,2048]{1,0:T(8,128)(2,1)S(1)}, bf16[256,2048]{1,0:T(8,128)(2,1)}) custom-call(s32[1]{0:T(128)} %bitcast.12.core_ref, bf16[512,2048]{1,0:T(8,128)(2,1)} %get-tuple-element.287.normed_ref.refs_0_, ...), custom_call_target="tpu_custom_call" | custom-call | flops 1 | bytes 1 | tf_op jit(solution)/shard_map/pallas_call | solution.py:472
  365.4 13.4 %shard_map.380 = (bf16[4,2048,256]{2,1,0:T(8,128)(2,1)}, bf16[2048,256]{1,0:T(8,128)(2,1)S(1)}, bf16[2048,256]{1,0:T(8,128)(2,1)}, bf16[2048,256]{1,0:T(8,128)(2,1)}, bf16[2048,256]{1,0:T(8,128)(2,1)}) custom-call(s32[1]{0:T(128)} %bitcast.12.core_ref, bf16[512,2048]{1,0:T(8,128)(2,1)} %get-tuple-element.294.left_ref.refs_0_, ...), custom_call_target="tpu_custom_call" | custom-call | flops 1 | bytes 1 | tf_op jit(solution)/shard_map/pallas_call | solution.py:472
  414.3 15.2 %shard_map.386.back_ref.right_ref = bf16[3,1024,512]{2,1,0:T(8,128)(2,1)} custom-call(s32[4]{0:T(128)S(1)} %copy-done.88, bf16[3,1024,512]{2,1,0:T(8,128)(2,1)} %copy-done, bf16[3,1024,512]{2,1,0:T(8,128)(2,1)} %copy-done, bf16[3,1024,512]{2,1,0:T(8,128)(2,1)} %copy-done, f32[512,512]{1,0:T(8,128)S(1)} %copy-done.59, f32[512,512]{1,0:T(8,128)S(1)} %copy-done.61, ...), custom_call_target="tpu_custom_call" | custom-call | flops 1 | bytes 1 | tf_op jit(solution)/shard_map/pallas_call | solution.py:225
  460.9 11.1 %shard_map.390 = (bf16[4,256,1536]{2,1,0:T(8,128)(2,1)}, bf16[256,1536]{1,0:T(8,128)(2,1)S(1)}, bf16[256,1536]{1,0:T(8,128)(2,1)S(1)}, bf16[256,1536]{1,0:T(8,128)(2,1)S(1)}, bf16[256,1536]{1,0:T(8,128)(2,1)S(1)}) custom-call(s32[1]{0:T(128)} %bitcast.12.core_ref, bf16[1024,2048]{1,0:T(8,128)(2,1)} %get-tuple-element.268.left_ref, ...), custom_call_target="tpu_custom_call" | custom-call | flops 1 | bytes 1 | tf_op jit(solution)/shard_map/pallas_call | solution.py:503
  476.8 9.1 %collective-permute-done.40.arrived_ref = bf16[256,2048]{1,0:T(8,128)(2,1)S(1)} collective-permute-done((bf16[256,2048]{1,0:T(8,128)(2,1)}, bf16[256,2048]{1,0:T(8,128)(2,1)S(1)}, u32[]{:S(2)}, u32[]{:S(2)}) %collective-permute-start.40) | collective-permute-done | bytes 1048608 | tf_op jit(solution)/shard_map/back1/ppermute | solution.py:966
  486.2 10.4 %collective-permute-done.42.refs_1_ = bf16[2048,256]{1,0:T(8,128)(2,1)S(1)} collective-permute-done((bf16[2048,256]{1,0:T(8,128)(2,1)S(1)}, bf16[2048,256]{1,0:T(8,128)(2,1)S(1)}, u32[]{:S(2)}, u32[]{:S(2)}) %collective-permute-start.42) | collective-permute-done | bytes 1048608 | tf_op jit(solution)/shard_map/out_plane/ppermute | solution.py:1151
  516.1 19.2 %collective-permute-done.43.arrived_ref = bf16[256,2048]{1,0:T(8,128)(2,1)S(1)} collective-permute-done((bf16[256,2048]{1,0:T(8,128)(2,1)}, bf16[256,2048]{1,0:T(8,128)(2,1)S(1)}, u32[]{:S(2)}, u32[]{:S(2)}) %collective-permute-start.43) | collective-permute-done | bytes 1048608 | tf_op jit(solution)/shard_map/back2/ppermute | solution.py:966
  536.5 15.3 %collective-permute-done.48.refs_3_ = bf16[2048,256]{1,0:T(8,128)(2,1)S(1)} collective-permute-done((bf16[2048,256]{1,0:T(8,128)(2,1)}, bf16[2048,256]{1,0:T(8,128)(2,1)S(1)}, u32[]{:S(2)}, u32[]{:S(2)}) %collective-permute-start.48) | collective-permute-done | bytes 1048608 | tf_op jit(solution)/shard_map/out_plane/ppermute | solution.py:1151
  555.6 25.9 %collective-permute-done.50.arrived_ref = bf16[512,256]{1,0:T(8,128)(2,1)S(1)} collective-permute-done((bf16[512,256]{1,0:T(8,128)(2,1)S(1)}, bf16[512,256]{1,0:T(8,128)(2,1)S(1)}, u32[]{:S(2)}, u32[]{:S(2)}) %collective-permute-start.50) | collective-permute-done | bytes 262176 | tf_op jit(solution)/shard_map/out_sum1/ppermute | solution.py:966
  582.4 8.5 %collective-permute-done.51.arrived_ref = bf16[512,256]{1,0:T(8,128)(2,1)S(1)} collective-permute-done((bf16[512,256]{1,0:T(8,128)(2,1)S(1)}, bf16[512,256]{1,0:T(8,128)(2,1)S(1)}, u32[]{:S(2)}, u32[]{:S(2)}) %collective-permute-start.51) | collective-permute-done | bytes 262176 | tf_op jit(solution)/shard_map/out_sum2/ppermute | solution.py:966
  591.3 7.8 %collective-permute-done.52.arrived_ref = bf16[512,256]{1,0:T(8,128)(2,1)S(1)} collective-permute-done((bf16[512,256]{1,0:T(8,128)(2,1)S(1)}, bf16[512,256]{1,0:T(8,128)(2,1)S(1)}, u32[]{:S(2)}, u32[]{:S(2)}) %collective-permute-start.52) | collective-permute-done | bytes 262176 | tf_op jit(solution)/shard_map/out_sum3/ppermute | solution.py:966
  646.2 17.7 %shard_map.404 = (f32[3,256,512]{2,1,0:T(8,128)}, bf16[3,256,512]{2,1,0:T(8,128)(2,1)}, f32[3,256,512]{2,1,0:T(8,128)}, f32[3,256,512]{2,1,0:T(8,128)}, f32[512,...) custom-call(f32[1]{0:T(128)} %bitcast.21.factor_ref, ...), custom_call_target="tpu_custom_call" | custom-call | flops 1 | bytes 1 | tf_op jit(solution)/shard_map/pallas_call | solution.py:845
  (424 shorter events, 310.7 us)
Async XLA Ops:
  7.2 74.5 %all-gather.6.cloned.1.call-start = ((), (), s32[]{:S(2)}) async-start(), calls=%async_computation.3 | async-start | bytes 7077888 | tf_op jit(solution)/shard_map/all_gather | solution.py:996
  9.8 108.1 %all-gather.8.cloned.1.call-start = ((), (), s32[]{:S(2)}) async-start(), calls=%async_computation.4 | async-start | bytes 9437184 | tf_op jit(solution)/shard_map/all_gather | solution.py:1004
  9.9 28.4 %collective-permute-start = (bf16[256,2048]{1,0:T(8,128)(2,1)S(1)}, bf16[256,2048]{1,0:T(8,128)(2,1)}, u32[]{:S(2)}, u32[]{:S(2)}) collective-permute-start(bf16[256,2048]{1,0:T(8,128)(2,1)S(1)} %copy-done.40), channel_id=1, source_target_pairs={{0,1},{1,2},{2,3},{3,0},{4,5},{5,6},{6,7},{7,4},{8,9},{9,10},{10,1... | collective-permute-start | bytes 3145736 | tf_op jit(solution)/shard_map/x1/ppermute | solution.py:966
  39.9 167.4 %all-gather.12.cloned.1.call-start = ((), (), s32[]{:S(2)}) async-start(), calls=%async_computation.9 | async-start | bytes 9437184 | tf_op jit(solution)/shard_map/all_gather | solution.py:1042
  40.0 28.3 %collective-permute-start.1 = (bf16[256,2048]{1,0:T(8,128)(2,1)}, bf16[256,2048]{1,0:T(8,128)(2,1)}, u32[]{:S(2)}, u32[]{:S(2)}) collective-permute-start(bf16[256,2048]{1,0:T(8,128)(2,1)} %collective-permute-done.x_ref), channel_id=1, source_target_pairs={{0,1},{1,2},{2,3},{3,0},{4,5},{5,6},{6,7},{7,4},{8,9},{9,10},{10,1... | collective-permute-start | bytes 3145736 | tf_op jit(solution)/shard_map/x2/ppermute | solution.py:966
  40.1 32.0 %collective-permute-start.2 = (bf16[512,256]{1,0:T(8,128)(2,1)S(1)}, bf16[512,256]{1,0:T(8,128)(2,1)}, u32[]{:S(2)}, u32[]{:S(2)}) collective-permute-start(bf16[512,256]{1,0:T(8,128)(2,1)S(1)} %shard_map.353.refs_0_), channel_id=1, source_target_pairs={{0,1},{1,2},{2,3},{3,0},{4,5},{5,6},{6,7},{7,4},{8,9},{9,10},{10,1... | collective-permute-start | bytes 786440 | tf_op jit(solution)/shard_map/out1/ppermute | solution.py:966
  72.1 33.4 %collective-permute-start.3 = (bf16[256,2048]{1,0:T(8,128)(2,1)}, bf16[256,2048]{1,0:T(8,128)(2,1)}, u32[]{:S(2)}, u32[]{:S(2)}) collective-permute-start(bf16[256,2048]{1,0:T(8,128)(2,1)} %collective-permute-done.1.x_ref), channel_id=1, source_target_pairs={{0,1},{1,2},{2,3},{3,0},{4,5},{5,6},{6,7},{7,4},{8,9},{9,10},{10,1... | collective-permute-start | bytes 3145736 | tf_op jit(solution)/shard_map/x3/ppermute | solution.py:966
  118.0 114.3 %all-gather.10.cloned.1.call-start = ((), (), s32[]{:S(2)}) async-start(), calls=%async_computation.5 | async-start | bytes 9437184 | tf_op jit(solution)/shard_map/all_gather | solution.py:1044
  120.7 486.2 %reduce-scatter.4.cloned.1.call-start = ((), (), s32[]{:S(2)}) async-start(), calls=%async_computation.6 | async-start | bytes 5242880 | tf_op jit(solution)/shard_map/reduce_scatter | solution.py:992
  252.8 28.2 %collective-permute-start.14 = (bf16[1024,512]{1,0:T(8,128)(2,1)}, bf16[1024,512]{1,0:T(8,128)(2,1)}, u32[]{:S(2)}, u32[]{:S(2)}) collective-permute-start(bf16[1024,512]{1,0:T(8,128)(2,1)} %collective-permute-done.13.rest_2_), channel_id=1, source_target_pairs={{0,1},{1,2},{2,3},{3,0},{4,5},{5,6},{6,7},{7,4},{8,9},{9,10},{10,1... | collective-permute-start | bytes 3145736 | tf_op jit(solution)/shard_map/slabb3/ppermute | solution.py:966
  261.7 27.4 %collective-permute-start.15 = (bf16[128,2048]{1,0:T(8,128)(2,1)S(1)}, bf16[128,2048]{1,0:T(8,128)(2,1)S(1)}, u32[]{:S(2)}, u32[]{:S(2)}) collective-permute-start(bf16[128,2048]{1,0:T(8,128)(2,1)S(1)} %constant_dynamic-slice_fusion.2), channel_id=1, source_target_pairs={{0,1},{1,2},{2,3},{3,0},{4,5},{5,6},{6,7},{7,4},{8,9},{9,10},{10,1... | collective-permute-start | bytes 1572872 | tf_op jit(solution)/shard_map/sum_a1/ppermute | solution.py:966
  384.6 224.7 %reduce-scatter.6.cloned.1.call-start = ((), (), s32[]{:S(2)}) async-start(), calls=%async_computation.7 | async-start | bytes 5242880 | tf_op jit(solution)/shard_map/reduce_scatter | solution.py:992
  411.3 27.5 %collective-permute-start.35 = (bf16[2048,256]{1,0:T(8,128)(2,1)}, bf16[2048,256]{1,0:T(8,128)(2,1)S(1)}, u32[]{:S(2)}, u32[]{:S(2)}) collective-permute-start(bf16[2048,256]{1,0:T(8,128)(2,1)} %get-tuple-element.377), channel_id=1, source_target_pairs={{0,4},{4,0},{1,5},{5,1},{2,6},{6,2},{3,7},{7,3},{8,12},{12,8},{9,1... | collective-permute-start | bytes 3145736 | tf_op jit(solution)/shard_map/down_grad_swap/ppermute | solution.py:985
  411.4 27.4 %collective-permute-start.34 = (bf16[2048,256]{1,0:T(8,128)(2,1)}, bf16[2048,256]{1,0:T(8,128)(2,1)S(1)}, u32[]{:S(2)}, u32[]{:S(2)}) collective-permute-start(bf16[2048,256]{1,0:T(8,128)(2,1)} %get-tuple-element.375), channel_id=1, source_target_pairs={{0,4},{4,0},{1,5},{5,1},{2,6},{6,2},{3,7},{7,3},{8,12},{12,8},{9,1... | collective-permute-start | bytes 3145736 | tf_op jit(solution)/shard_map/down_grad_swap/ppermute | solution.py:985
  444.4 168.6 %reduce-scatter.8.cloned.1.call-start = ((), (), s32[]{:S(2)}) async-start(), calls=%async_computation.8 | async-start | bytes 3932160 | tf_op jit(solution)/shard_map/reduce_scatter | solution.py:992
  458.9 27.1 %collective-permute-start.40 = (bf16[256,2048]{1,0:T(8,128)(2,1)}, bf16[256,2048]{1,0:T(8,128)(2,1)S(1)}, u32[]{:S(2)}, u32[]{:S(2)}) collective-permute-start(bf16[256,2048]{1,0:T(8,128)(2,1)} %shard_map.387), channel_id=1, source_target_pairs={{0,1},{1,2},{2,3},{3,0},{4,5},{5,6},{6,7},{7,4},{8,9},{9,10},{10,1... | collective-permute-start | bytes 3145736 | tf_op jit(solution)/shard_map/back1/ppermute | solution.py:966
  458.9 37.7 %collective-permute-start.42 = (bf16[2048,256]{1,0:T(8,128)(2,1)S(1)}, bf16[2048,256]{1,0:T(8,128)(2,1)S(1)}, u32[]{:S(2)}, u32[]{:S(2)}) collective-permute-start(bf16[2048,256]{1,0:T(8,128)(2,1)S(1)} %get-tuple-element.396), channel_id=1, source_target_pairs={{0,8},{8,0},{16,24},{24,16},{1,9},{9,1},{17,25},{25,17},{2,10},{10... | collective-permute-start | bytes 3145736 | tf_op jit(solution)/shard_map/out_plane/ppermute | solution.py:1151
  460.4 36.3 %collective-permute-start.41 = (bf16[2048,256]{1,0:T(8,128)(2,1)S(1)}, bf16[2048,256]{1,0:T(8,128)(2,1)S(1)}, u32[]{:S(2)}, u32[]{:S(2)}) collective-permute-start(bf16[2048,256]{1,0:T(8,128)(2,1)S(1)} %get-tuple-element.394), channel_id=1, source_target_pairs={{0,16},{8,24},{16,0},{24,8},{1,17},{9,25},{17,1},{25,9},{2,18},{10... | collective-permute-start | bytes 3145736 | tf_op jit(solution)/shard_map/out_plane/ppermute | solution.py:1151
  508.1 27.1 %collective-permute-start.43 = (bf16[256,2048]{1,0:T(8,128)(2,1)}, bf16[256,2048]{1,0:T(8,128)(2,1)S(1)}, u32[]{:S(2)}, u32[]{:S(2)}) collective-permute-start(bf16[256,2048]{1,0:T(8,128)(2,1)} %copy-done.70), channel_id=1, source_target_pairs={{0,1},{1,2},{2,3},{3,0},{4,5},{5,6},{6,7},{7,4},{8,9},{9,10},{10,1... | collective-permute-start | bytes 3145736 | tf_op jit(solution)/shard_map/back2/ppermute | solution.py:966
  509.7 42.0 %collective-permute-start.48 = (bf16[2048,256]{1,0:T(8,128)(2,1)}, bf16[2048,256]{1,0:T(8,128)(2,1)S(1)}, u32[]{:S(2)}, u32[]{:S(2)}) collective-permute-start(bf16[2048,256]{1,0:T(8,128)(2,1)} %copy-done.103), channel_id=1, source_target_pairs={{0,24},{8,16},{16,8},{24,0},{1,25},{9,17},{17,9},{25,1},{2,26},{10... | collective-permute-start | bytes 3145736 | tf_op jit(solution)/shard_map/out_plane/ppermute | solution.py:1151
  552.4 47.5 %collective-permute-start.49 = (bf16[256,2048]{1,0:T(8,128)(2,1)}, bf16[256,2048]{1,0:T(8,128)(2,1)}, u32[]{:S(2)}, u32[]{:S(2)}) collective-permute-start(bf16[256,2048]{1,0:T(8,128)(2,1)} %shard_map.396), channel_id=1, source_target_pairs={{0,1},{1,2},{2,3},{3,0},{4,5},{5,6},{6,7},{7,4},{8,9},{9,10},{10,1... | collective-permute-start | bytes 3145736 | tf_op jit(solution)/shard_map/back3/ppermute | solution.py:966
  553.9 27.5 %collective-permute-start.50 = (bf16[512,256]{1,0:T(8,128)(2,1)S(1)}, bf16[512,256]{1,0:T(8,128)(2,1)S(1)}, u32[]{:S(2)}, u32[]{:S(2)}) collective-permute-start(bf16[512,256]{1,0:T(8,128)(2,1)S(1)} %constant_dynamic-slice_fusion), channel_id=1, source_target_pairs={{0,1},{1,2},{2,3},{3,0},{4,5},{5,6},{6,7},{7,4},{8,9},{9,10},{10,1... | collective-permute-start | bytes 786440 | tf_op jit(solution)/shard_map/out_sum1/ppermute | solution.py:966
  606.9 27.1 %collective-permute-start.53 = (bf16[256,2048]{1,0:T(8,128)(2,1)}, bf16[256,2048]{1,0:T(8,128)(2,1)}, u32[]{:S(2)}, u32[]{:S(2)}) collective-permute-start(bf16[256,2048]{1,0:T(8,128)(2,1)} %shard_map.402), channel_id=1, source_target_pairs={{0,1},{1,2},{2,3},{3,0},{4,5},{5,6},{6,7},{7,4},{8,9},{9,10},{10,1... | collective-permute-start | bytes 3145736 | tf_op jit(solution)/shard_map/ffn2/ppermute | solution.py:966
  636.6 27.9 %collective-permute-start.59 = (bf16[256,2048]{1,0:T(8,128)(2,1)}, bf16[256,2048]{1,0:T(8,128)(2,1)}, u32[]{:S(2)}, u32[]{:S(2)}) collective-permute-start(bf16[256,2048]{1,0:T(8,128)(2,1)} %shard_map.403), channel_id=1, source_target_pairs={{0,1},{1,2},{2,3},{3,0},{4,5},{5,6},{6,7},{7,4},{8,9},{9,10},{10,1... | collective-permute-start | bytes 3145736 | tf_op jit(solution)/shard_map/ffn3/ppermute | solution.py:966
  (154 other events, 1542.2 us)
Sparse Core Ops, SparseCore 0:
  10.5 48.2 all-gather.5
  61.2 54.7 all-gather.7
  118.5 55.4 all-gather.11
  176.2 55.9 all-gather.9
  384.8 49.9 reduce-scatter.3
  444.6 63.5 reduce-scatter.5
  511.2 58.7 reduce-scatter.7

commit v3 on v2

--- a/solution.py
+++ b/solution.py
@@ -848,7 +848,7 @@
             num_scalar_prefetch=1, grid=(steps,), in_specs=in_specs, out_specs=out_specs
         ),
         out_shape=shapes,
-        compiler_params=params(),
+        compiler_params=params(60 * 1024 * 1024),
         cost_estimate=LIGHT,
     )(factor.reshape(1), *operands)
     return [tuple(out[4 * index : 4 * index + 4]) for index in range(len(groups))]
@@ -1015,7 +1015,7 @@
                     gain_line = did(gain_line + lax.ppermute(at(gain_line), axis, perm))
     else:
         gain_line = did(lax.psum(at(gain_line), tok))
-    gain_float = did(gain_line.transpose(1, 0, 2).reshape(2, width))
+    gain_float = gain_line.transpose(1, 0, 2).reshape(2, width)
     cosine, sine = rotary_tables(length)
     for step in range(3, bkts):
         x_held[-1] = wait(x_held[-1])
@@ -1087,11 +1087,13 @@
     did(inner_b)
     sum_a = add(arrived_a, back_a, 3)
     arrived_a = pass_on("sum_a3", sum_a)
+    up_kept, up_sent = weight_grad(core_id, [normed_a, normed_b], [at(inner_a), inner_b], chips, 0)
+    did(up_kept)
     back_b = did(product(at(inner_b), up_full, True))
-    prod_b = did(product(at(hidden_b), down_full, False))
     arrived_a = wait(arrived_a)
     sum_b = did(rows_of(at(back_b), 1))
     arrived_b = pass_on("sum_b1", sum_b)
+    up_arrived = swap("up_grad", up_sent)
 
     first = jnp.zeros((), jnp.int32)
     targets = jnp.stack([lax.rem(group + step, bkts) for step in range(bkts)]).astype(jnp.int32)
@@ -1113,21 +1115,21 @@
 
     grad_a, mid_low_a, gain_a, pieces_a = middle_back(0, middle_a, arrived_a, back_a)
     sum_b = add(arrived_b, back_b, 2)
+    arrived_b = pass_on("sum_b2", sum_b)
     exchange(0, pieces_a)
-    arrived_b = pass_on("sum_b2", sum_b)
-    up_kept, up_sent = weight_grad(core_id, [normed_a, normed_b], [at(inner_a), inner_b], chips, 0)
-    did(up_kept)
+    up_core = core_add(up_kept, up_arrived)
+    up_part = chip_sum(up_core)
+    down_kept, down_sent = weight_grad(core_id, [hidden_a, hidden_b], [at(low_a), low_b], chips, 1)
+    did(down_kept)
     pieces_a = pieces_a[:1] + [wait(piece) for piece in pieces_a[1:]]
     sum_b = add(arrived_b, back_b, 3)
-    up_arrived = swap("up_grad", up_sent)
     arrived_b = pass_on("sum_b3", sum_b)
-    down_kept, down_sent = weight_grad(core_id, [hidden_a, hidden_b], [at(low_a), low_b], chips, 1)
-    did(down_kept)
-    arrived_b = wait(arrived_b)
-    up_core = core_add(up_kept, up_arrived)
-    up_part = chip_sum(up_core)
+    down_arrived = swap("down_grad", down_sent)
+    prod_b = did(product(at(hidden_b), down_full, False))
     grad_b, mid_low_b, gain_b, pieces_b = middle_back(1, middle_b, arrived_b, back_b)
     exchange(1, pieces_b)
+    down_core = core_add(down_kept, down_arrived)
+    down_part = chip_sum(down_core)
     out_kept, out_sent = weight_grad(
         core_id, [at(mixed_a), mixed_b], [mid_low_a, mid_low_b], chips, 1
     )
@@ -1135,66 +1137,43 @@
     prods = [prod_a, prod_b]
     ffn = did(pair_add(owner(1), half, [at(prod_a), prod_b], None, None, LOW))
     pieces_b = pieces_b[:1] + [wait(piece) for piece in pieces_b[1:]]
-    down_arrived = swap("down_grad", down_sent)
+    arrived_f = pass_on("ffn1", ffn)
     out_arrived = swap("out_grad", out_sent)
-    arrived_f = pass_on("ffn1", ffn)
 
     back_project = did(attend_back(places, at(qkv), pieces_a + pieces_b, logs, cosine, sine))
     total = did(project_back(owner(1), at(back_project), qkv_full, rows))
     arrived_f = wait(arrived_f)
-    down_core = core_add(down_kept, down_arrived)
-    down_part = chip_sum(down_core)
-    direct = chips <= 4 and by_bits
-
-    def out_plane(mask):
-        with jax.named_scope("out_plane"):
-            out_apart[mask] = lax.ppermute(
-                at(out_apart[mask]), "chip", [(i, i ^ mask) for i in range(chips)]
-            )
-
-    if direct:
-        out_apart = list(core_add_apart(chip, at(out_kept), out_arrived))
-        did(out_apart[0])
-        for mask in range(1, chips):
-            if mask & (mask - 1) == 0:
-                out_plane(mask)
-    else:
-        out_sum = chip_sum(core_add(out_kept, out_arrived))
+    up_squares = did(squares(at(up_part)))
+    out_core = core_add(out_kept, out_arrived)
+    out_sum = chip_sum(out_core)
     arrived = pass_on("back1", total)
     qkv_kept, qkv_sent = project_grad(core_id, normed_one, at(back_project), chips)
     did(qkv_kept)
     own = did(project_back(owner(2), at(back_project), qkv_full, rows))
     total = did(ring_add(first, at(arrived), own, LOW))
-    if direct:
-        for mask in range(1, chips):
-            if mask & (mask - 1) == 0:
-                out_apart[mask] = wait(out_apart[mask])
-            else:
-                out_plane(mask)
+    down_squares = did(squares(at(down_part)))
+    arrived = pass_on("back2", total)
     qkv_arrived = swap("qkv_grad", qkv_sent)
-    arrived = pass_on("back2", total)
     own = did(project_back(owner(3), at(back_project), qkv_full, rows))
     qkv_core = core_add(qkv_kept, qkv_arrived)
     qkv_part = chip_sum(qkv_core)
     last_own = did(project_back(owner(0), at(back_project), qkv_full, rows))
+    arrived_out = pass_on("out_sum1", rows_of(out_sum, 1))
     total = did(ring_add(first, at(arrived), own, LOW))
-    if direct:
-        out_sum = add_many([at(out_apart[0])] + out_apart[1:])
-    did(out_sum)
-    arrived = pass_on("back3", total)
-    arrived_out = pass_on("out_sum1", rows_of(out_sum, 1))
-    for step in range(2, bkts):
-        arrived_out = pass_on("out_sum" + str(step), add(arrived_out, out_sum, step))
-    out_part = add_final(arrived_out, out_sum)
-    out_squares = did(squares(at(out_part)))
+    out_part = add(arrived_out, out_sum, 2)
+    arrived_out = pass_on("out_sum2", out_part)
+    arrived = pass_on("back3", total, out_part)
+    ffn = did(pair_add(owner(2), half, prods, at(arrived_f), None, LOW))
+    for step in range(3, bkts):
+        out_part = add(arrived_out, out_sum, step)
+        arrived_out = pass_on("out_sum" + str(step), out_part)
     block_in_grad, gain_one = norm_back(
         first, block_in, at(arrived), last_own, gain_float[0:1], [grad_a, grad_b], 0, False
     )
     did(gain_one)
-    ffn = did(pair_add(owner(2), half, prods, at(arrived_f), None, LOW))
+    out_part = add_final(arrived_out, out_sum)
     arrived_f = pass_on("ffn2", ffn)
-    up_squares = did(squares(at(up_part)))
-    down_squares = did(squares(at(down_part)))
+    out_squares = did(squares(at(out_part)))
     gain_grad_one = gain_one[0]
     gain_grad_two = (gain_a + gain_b)[0]
 
@@ -1209,9 +1188,10 @@
             step = 1
             while step < size:
                 packed = packed + lax.ppermute(packed, axis, [(i, i ^ step) for i in range(size)])
+                if axis == "bkt" and step == 1:
+                    ffn = pair_add(owner(3), half, prods, after(arrived_f, packed), None, LOW)
                 step *= 2
     did(packed)
-    ffn = did(pair_add(owner(3), half, prods, at(arrived_f), None, LOW))
     arrived_f = pass_on("ffn3", ffn)
     gain_total = packed[: 2 * width].reshape(2, width)
     grad_norm = jnp.sqrt(packed[2 * width] + jnp.sum(gain_total * gain_total))

time: 689 us -> 657 us (0.954)
  waiting for transfers between devices: 247 us -> 231 us
  starting transfers between devices: 50.7 us -> 38.3 us
    ppermute x3 -> x0, waiting for transfers between devices: 25.7 us -> none  [out_plane(): lax.ppermute(at(out_apart[mask]), 'chip', [(i, i ^ mask) for i in range(c...]
    reduce_scatter x3 -> x4, waiting for transfers between devices: 0.04 us -> 11.2 us  [chip_sum(): return lax.psum_scatter(value, 'chip', scatter_dimension=0, tiled=True)]
    ppermute x27, starting transfers between devices: 25 us -> 17.2 us  [pass_on(): return lax.ppermute(at(value, *others), 'bkt', ring)]
    ppermute x5, waiting for transfers between devices: 9.93 us -> 17.3 us  [per_device(): lax.ppermute(packed, axis, [(i, i ^ step) for i in range(size)])]
    unnamed x222 -> x198, local copies, waits for them, and re-layouts: 54.8 us -> 47.5 us
    pallas_call x3 -> x4, Pallas kernels: 15.8 us -> 20.9 us  [core_add_kernel(): pl.pallas_call(core_add_body, grid=(rows // tile,), in_specs=[spec] + [pl...]
  transfers between devices with their start and end apart: 67 -> 65, of which waited for: 35 -> 30; matrix products, arithmetic and copies ran while one was open for 2% -> 2% of each run, Pallas kernels for 41% -> 43%
where the time goes in v3:
time: 657 us; the launch traced here: 646 us
  Pallas kernels  290 us (44%)
  waiting for transfers between devices  231 us (35%)
  local copies, waits for them, and re-layouts  50.1 us (8%)
  starting transfers between devices  38.3 us (6%)
  between operations  21.4 us (3%)
  other arithmetic  14.8 us (2%)
    ppermute x27, waiting for transfers between devices, pass_on(): return lax.ppermute(at(value, *others), 'bkt', ring)  195 us
    unnamed x198, local copies, waits for them, and re-layouts  47.5 us
    pallas_call x3, Pallas kernels, weight_grad(): pl.pallas_call(functools.partial(grad_body, len(lefts), axis), grid_spec=...  35.5 us
    pallas_call x4, Pallas kernels, product(): pl.pallas_call(functools.partial(product_body, NT if turned else NN), gri...  28.8 us
    pallas_call x2, Pallas kernels, hidden_units(): pl.pallas_call(functools.partial(hidden_body, count), grid_spec=pltpu.Pre...  28.7 us
    pallas_call x4, Pallas kernels, project(): pl.pallas_call(project_body, grid_spec=pltpu.PrefetchScalarGridSpec(num_s...  27.8 us
    pallas_call x4, Pallas kernels, core_add_kernel(): pl.pallas_call(core_add_body, grid=(rows // tile,), in_specs=[spec] + [pl...  20.9 us
    pallas_call x4, Pallas kernels, project_back(): pl.pallas_call(project_back_body, grid_spec=pltpu.PrefetchScalarGridSpec(...  20.4 us
  transfers between devices with their start and end apart: 65, of which 30 were waited for; matrix products, arithmetic and copies ran while one was open for 2% of the time, Pallas kernels for 43%

profile of v3, /device:TPU:0, one launch (start us, length us, event | category | flops | bytes accessed | tf_op | source)
XLA Modules:
  0.0 646.2 jit_solution(5514453883933666192)
XLA Ops:
  14.0 24.1 %collective-permute-done.x_ref = bf16[256,2048]{1,0:T(8,128)(2,1)S(1)} collective-permute-done((bf16[256,2048]{1,0:T(8,128)(2,1)S(1)}, bf16[256,2048]{1,0:T(8,128)(2,1)S(1)}, u32[]{:S(2)}, u32[]{:S(2)}) %collective-permute-start) | collective-permute-done | bytes 1048608 | tf_op jit(solution)/shard_map/x1/ppermute | solution.py:966
  50.6 18.5 %collective-permute-done.1.x_ref = bf16[256,2048]{1,0:T(8,128)(2,1)} collective-permute-done((bf16[256,2048]{1,0:T(8,128)(2,1)}, bf16[256,2048]{1,0:T(8,128)(2,1)}, u32[]{:S(2)}, u32[]{:S(2)}) %collective-permute-start.1) | collective-permute-done | bytes 1048608 | tf_op jit(solution)/shard_map/x2/ppermute | solution.py:966
  89.7 7.6 %shard_map.357 = (bf16[1024,2048]{1,0:T(8,128)(2,1)}, bf16[3,1024,512]{2,1,0:T(8,128)(2,1)S(1)}, bf16[1024,2048]{1,0:T(8,128)(2,1)}) custom-call(s32[1]{0:T(128)} %bitcast.2.place_ref, bf16[256,2048]{1,0:T(8,128)(2,1)} %collective-permute-done.1.x_ref, f32[1,2048]{1,0:T(1,128)S(1)} %bitcast.26, ...), custom_call_target="tpu_custom_call", output_to_operand_aliasing={{0}: (6, {}), {1}: (7, {}), {2}: (8, {})} | custom-call | flops 1 | bytes 1 | tf_op jit(solution)/shard_map/pallas_call | solution.py:95
  120.4 8.4 %shard_map.361 = (bf16[1024,512]{1,0:T(8,128)(2,1)S(1)}, f32[512,512]{1,0:T(8,128)S(1)}) custom-call(bf16[3,1024,512]{2,1,0:T(8,128)(2,1)} %copy-done, bf16[3,1024,512]{2,1,0:T(8,128)(2,1)} %copy-done, bf16[3,1024,512]{2,1,0:T(8,128)(2,1)} %copy-done, f32[256,2048]{1,0:T(8,128)S(1)} %copy-done.1, f32[256,2048]{1,0:T(8,128)S(1)} %copy-done.1, ...), custom_call_target="tpu_custom_call" | custom-call | flops 1 | bytes 1 | tf_op jit(solution)/shard_map/pallas_call | solution.py:152
  131.4 8.5 %shard_map.362 = (bf16[1024,512]{1,0:T(8,128)(2,1)S(1)}, f32[512,512]{1,0:T(8,128)S(1)}) custom-call(bf16[3,1024,512]{2,1,0:T(8,128)(2,1)} %copy-done, bf16[3,1024,512]{2,1,0:T(8,128)(2,1)} %copy-done, bf16[3,1024,512]{2,1,0:T(8,128)(2,1)} %copy-done, f32[256,2048]{1,0:T(8,128)S(1)} %copy-done.1, f32[256,2048]{1,0:T(8,128)S(1)} %copy-done.1, ...), custom_call_target="tpu_custom_call" | custom-call | flops 1 | bytes 1 | tf_op jit(solution)/shard_map/pallas_call | solution.py:152
  140.9 16.1 %collective-permute-done.9.rest_1_ = bf16[1024,512]{1,0:T(8,128)(2,1)S(1)} collective-permute-done((bf16[1024,512]{1,0:T(8,128)(2,1)S(1)}, bf16[1024,512]{1,0:T(8,128)(2,1)S(1)}, u32[]{:S(2)}, u32[]{:S(2)}) %collective-permute-start.9) | collective-permute-done | bytes 1048608 | tf_op jit(solution)/shard_map/slaba1/ppermute | solution.py:966
  158.0 25.3 %collective-permute-done.10.rest_2_ = bf16[1024,512]{1,0:T(8,128)(2,1)S(1)} collective-permute-done((bf16[1024,512]{1,0:T(8,128)(2,1)S(1)}, bf16[1024,512]{1,0:T(8,128)(2,1)S(1)}, u32[]{:S(2)}, u32[]{:S(2)}) %collective-permute-start.10) | collective-permute-done | bytes 1048608 | tf_op jit(solution)/shard_map/slaba2/ppermute | solution.py:966
  184.3 24.4 %collective-permute-done.11.rest_3_ = bf16[1024,512]{1,0:T(8,128)(2,1)S(1)} collective-permute-done((bf16[1024,512]{1,0:T(8,128)(2,1)S(1)}, bf16[1024,512]{1,0:T(8,128)(2,1)S(1)}, u32[]{:S(2)}, u32[]{:S(2)}) %collective-permute-start.11) | collective-permute-done | bytes 1048608 | tf_op jit(solution)/shard_map/slaba3/ppermute | solution.py:966
  212.4 8.4 %shard_map.363.acc_ref = f32[512,2048]{1,0:T(8,128)} custom-call(s32[4]{0:T(128)S(1)} %pad_add_fusion.place_ref, bf16[4,256,2048]{2,1,0:T(8,128)(2,1)} %bitcast.45, bf16[1024,512]{1,0:T(8,128)(2,1)S(1)} %get-tuple-element.266.rest_0_, bf16[1024,512]{1,0:T(8,128)(2,1)S(1)} %copy-done.23, bf16[1024,512]{1,0:T(8,128)(2,1)S(1)} %copy-done.26, ...), custom_call_target="tpu_custom_call" | custom-call | flops 1 | bytes 1 | tf_op jit(solution)/shard_map/pallas_call | solution.py:275
  238.7 14.5 %shard_map.365 = (bf16[512,2048]{1,0:T(8,128)(2,1)}, bf16[512,2048]{1,0:T(8,128)(2,1)}, bf16[512,2048]{1,0:T(8,128)(2,1)}) custom-call(s32[4]{0:T(128)S(1)} %pad_add_fusion.place_ref, f32[1]{0:T(128)S(6)} %convert_element_type.48.live_ref, bf16[512,2048]{1,0:T(8,128)(2,1)} %get-tuple-element.279.normed_ref.refs_0_, ...), custom_call_target="tpu_custom_call" | custom-call | flops 1 | bytes 1 | tf_op jit(solution)/shard_map/pallas_call | solution.py:373
  266.9 9.1 %shard_map.367.acc_ref = f32[512,2048]{1,0:T(8,128)} custom-call(s32[4]{0:T(128)S(1)} %pad_add_fusion.place_ref, bf16[4,256,2048]{2,1,0:T(8,128)(2,1)} %bitcast.46, bf16[1024,512]{1,0:T(8,128)(2,1)S(1)} %get-tuple-element.277.rest_0_, bf16[1024,512]{1,0:T(8,128)(2,1)S(1)} %collective-permute-done.12.rest_1_, ...), custom_call_target="tpu_custom_call" | custom-call | flops 1 | bytes 1 | tf_op jit(solution)/shard_map/pallas_call | solution.py:275
  275.9 7.2 %shard_map.368.refs_0_ = bf16[512,2048]{1,0:T(8,128)(2,1)S(1)} custom-call(bf16[512,2048]{1,0:T(8,128)(2,1)S(1)} %copy-done.30, bf16[2048,2048]{1,0:T(8,128)(2,1)} %all-gather.10.cloned.1.call-done.down_ref.right_ref), custom_call_target="tpu_custom_call" | custom-call | flops 1 | bytes 1 | tf_op jit(solution)/shard_map/pallas_call | solution.py:414
  294.3 14.2 %shard_map.371 = (bf16[512,2048]{1,0:T(8,128)(2,1)}, bf16[512,2048]{1,0:T(8,128)(2,1)}, bf16[512,2048]{1,0:T(8,128)(2,1)}) custom-call(s32[4]{0:T(128)S(1)} %pad_add_fusion.place_ref, f32[1]{0:T(128)S(6)} %convert_element_type.48.live_ref, bf16[512,2048]{1,0:T(8,128)(2,1)} %get-tuple-element.293.normed_ref.refs_1_, ...), custom_call_target="tpu_custom_call" | custom-call | flops 1 | bytes 1 | tf_op jit(solution)/shard_map/pallas_call | solution.py:373
  310.4 15.2 %shard_map.373 = (bf16[4,256,2048]{2,1,0:T(8,128)(2,1)}, bf16[256,2048]{1,0:T(8,128)(2,1)}, bf16[256,2048]{1,0:T(8,128)(2,1)}, bf16[256,2048]{1,0:T(8,128)(2,1)}, bf16[256,2048]{1,0:T(8,128)(2,1)}) custom-call(s32[1]{0:T(128)} %bitcast.12.core_ref, bf16[512,2048]{1,0:T(8,128)(2,1)} %get-tuple-element.279.normed_ref.refs_0_, ...), custom_call_target="tpu_custom_call" | custom-call | flops 1 | bytes 1 | tf_op jit(solution)/shard_map/pallas_call | solution.py:472
  325.6 7.3 %shard_map.374.part_ref = bf16[512,2048]{1,0:T(8,128)(2,1)S(1)} custom-call(bf16[512,2048]{1,0:T(8,128)(2,1)S(1)} %copy-done.33, bf16[2048,2048]{1,0:T(8,128)(2,1)} %all-gather.8.cloned.1.call-done.up_ref.right_ref), custom_call_target="tpu_custom_call" | custom-call | flops 1 | bytes 1 | tf_op jit(solution)/shard_map/pallas_call | solution.py:414
  363.9 13.7 %shard_map.379 = (bf16[4,2048,256]{2,1,0:T(8,128)(2,1)}, bf16[2048,256]{1,0:T(8,128)(2,1)}, bf16[2048,256]{1,0:T(8,128)(2,1)}, bf16[2048,256]{1,0:T(8,128)(2,1)}, bf16[2048,256]{1,0:T(8,128)(2,1)}) custom-call(s32[1]{0:T(128)} %bitcast.12.core_ref, bf16[512,2048]{1,0:T(8,128)(2,1)} %get-tuple-element.286.left_ref.refs_0_, ...), custom_call_target="tpu_custom_call" | custom-call | flops 1 | bytes 1 | tf_op jit(solution)/shard_map/pallas_call | solution.py:472
  430.5 15.2 %shard_map.387.back_ref.right_ref = bf16[3,1024,512]{2,1,0:T(8,128)(2,1)} custom-call(s32[4]{0:T(128)S(1)} %copy-done.81, bf16[3,1024,512]{2,1,0:T(8,128)(2,1)} %copy-done, bf16[3,1024,512]{2,1,0:T(8,128)(2,1)} %copy-done, bf16[3,1024,512]{2,1,0:T(8,128)(2,1)} %copy-done, f32[512,512]{1,0:T(8,128)S(1)} %copy-done.57, f32[512,512]{1,0:T(8,128)S(1)} %copy-done.59, ...), custom_call_target="tpu_custom_call" | custom-call | flops 1 | bytes 1 | tf_op jit(solution)/shard_map/pallas_call | solution.py:225
  463.3 11.1 %shard_map.390 = (bf16[4,256,1536]{2,1,0:T(8,128)(2,1)}, bf16[256,1536]{1,0:T(8,128)(2,1)S(1)}, bf16[256,1536]{1,0:T(8,128)(2,1)S(1)}, bf16[256,1536]{1,0:T(8,128)(2,1)S(1)}, bf16[256,1536]{1,0:T(8,128)(2,1)S(1)}) custom-call(s32[1]{0:T(128)} %bitcast.12.core_ref, bf16[1024,2048]{1,0:T(8,128)(2,1)} %get-tuple-element.260.left_ref, ...), custom_call_target="tpu_custom_call" | custom-call | flops 1 | bytes 1 | tf_op jit(solution)/shard_map/pallas_call | solution.py:503
  481.6 8.0 %collective-permute-done.40.arrived_ref = bf16[256,2048]{1,0:T(8,128)(2,1)S(1)} collective-permute-done((bf16[256,2048]{1,0:T(8,128)(2,1)}, bf16[256,2048]{1,0:T(8,128)(2,1)S(1)}, u32[]{:S(2)}, u32[]{:S(2)}) %collective-permute-start.40) | collective-permute-done | bytes 1048608 | tf_op jit(solution)/shard_map/back1/ppermute | solution.py:966
  510.5 11.2 %reduce-scatter.7.cloned.1.call-done.part_ref = bf16[2048,256]{1,0:T(8,128)(2,1)} async-done(((bf16[8192,256]{1,0:T(8,128)(2,1)}), bf16[2048,256]{1,0:T(8,128)(2,1)}) %reduce-scatter.7.cloned.1.call-update) | async-done | bytes 1048592 | tf_op jit(solution)/shard_map/reduce_scatter | solution.py:992
  524.3 8.4 %collective-permute-done.46.arrived_ref = bf16[256,2048]{1,0:T(8,128)(2,1)} collective-permute-done((bf16[256,2048]{1,0:T(8,128)(2,1)}, bf16[256,2048]{1,0:T(8,128)(2,1)}, u32[]{:S(2)}, u32[]{:S(2)}) %collective-permute-start.46) | collective-permute-done | bytes 1048608 | tf_op jit(solution)/shard_map/back2/ppermute | solution.py:966
  539.9 29.1 %collective-permute-done.47.arrived_ref = bf16[512,256]{1,0:T(8,128)(2,1)S(1)} collective-permute-done((bf16[512,256]{1,0:T(8,128)(2,1)S(1)}, bf16[512,256]{1,0:T(8,128)(2,1)S(1)}, u32[]{:S(2)}, u32[]{:S(2)}) %collective-permute-start.47) | collective-permute-done | bytes 262176 | tf_op jit(solution)/shard_map/out_sum2/ppermute | solution.py:966
  592.0 8.5 %collective-permute-done.54 = f32[4224]{0:T(1024)S(1)} collective-permute-done((f32[4224]{0:T(1024)S(1)}, f32[4224]{0:T(1024)S(1)}, u32[]{:S(2)}, u32[]{:S(2)}) %collective-permute-start.54) | collective-permute-done | bytes 16928 | tf_op jit(solution)/shard_map/ppermute | solution.py:1190
  610.4 18.5 %shard_map.403 = (f32[3,256,512]{2,1,0:T(8,128)}, bf16[3,256,512]{2,1,0:T(8,128)(2,1)}, f32[3,256,512]{2,1,0:T(8,128)}, f32[3,256,512]{2,1,0:T(8,128)}, f32[512,...) custom-call(f32[1]{0:T(128)} %bitcast.21.factor_ref, ...), custom_call_target="tpu_custom_call" | custom-call | flops 1 | bytes 1 | tf_op jit(solution)/shard_map/pallas_call | solution.py:845
  (396 shorter events, 292.2 us)
Async XLA Ops:
  7.2 65.8 %all-gather.6.cloned.1.call-start = ((), (), s32[]{:S(2)}) async-start(), calls=%async_computation.4 | async-start | bytes 7077888 | tf_op jit(solution)/shard_map/all_gather | solution.py:996
  9.8 106.2 %all-gather.8.cloned.1.call-start = ((), (), s32[]{:S(2)}) async-start(), calls=%async_computation.5 | async-start | bytes 9437184 | tf_op jit(solution)/shard_map/all_gather | solution.py:1004
  9.9 28.3 %collective-permute-start = (bf16[256,2048]{1,0:T(8,128)(2,1)S(1)}, bf16[256,2048]{1,0:T(8,128)(2,1)S(1)}, u32[]{:S(2)}, u32[]{:S(2)}) collective-permute-start(bf16[256,2048]{1,0:T(8,128)(2,1)S(1)} %copy-done.40), channel_id=1, source_target_pairs={{0,1},{1,2},{2,3},{3,0},{4,5},{5,6},{6,7},{7,4},{8,9},{9,10},{10,1... | collective-permute-start | bytes 3145736 | tf_op jit(solution)/shard_map/x1/ppermute | solution.py:966
  40.8 169.1 %all-gather.12.cloned.1.call-start = ((), (), s32[]{:S(2)}) async-start(), calls=%async_computation.11 | async-start | bytes 9437184 | tf_op jit(solution)/shard_map/all_gather | solution.py:1042
  40.9 28.3 %collective-permute-start.1 = (bf16[256,2048]{1,0:T(8,128)(2,1)}, bf16[256,2048]{1,0:T(8,128)(2,1)}, u32[]{:S(2)}, u32[]{:S(2)}) collective-permute-start(bf16[256,2048]{1,0:T(8,128)(2,1)} %copy-done.68), channel_id=1, source_target_pairs={{0,1},{1,2},{2,3},{3,0},{4,5},{5,6},{6,7},{7,4},{8,9},{9,10},{10,1... | collective-permute-start | bytes 3145736 | tf_op jit(solution)/shard_map/x2/ppermute | solution.py:966
  41.1 31.9 %collective-permute-start.5 = (bf16[512,256]{1,0:T(8,128)(2,1)S(1)}, bf16[512,256]{1,0:T(8,128)(2,1)}, u32[]{:S(2)}, u32[]{:S(2)}) collective-permute-start(bf16[512,256]{1,0:T(8,128)(2,1)S(1)} %shard_map.353.refs_0_), channel_id=1, source_target_pairs={{0,1},{1,2},{2,3},{3,0},{4,5},{5,6},{6,7},{7,4},{8,9},{9,10},{10,1... | collective-permute-start | bytes 786440 | tf_op jit(solution)/shard_map/out1/ppermute | solution.py:966
  73.0 28.2 %collective-permute-start.6 = (bf16[256,2048]{1,0:T(8,128)(2,1)}, bf16[256,2048]{1,0:T(8,128)(2,1)}, u32[]{:S(2)}, u32[]{:S(2)}) collective-permute-start(bf16[256,2048]{1,0:T(8,128)(2,1)} %collective-permute-done.1.x_ref), channel_id=1, source_target_pairs={{0,1},{1,2},{2,3},{3,0},{4,5},{5,6},{6,7},{7,4},{8,9},{9,10},{10,1... | collective-permute-start | bytes 3145736 | tf_op jit(solution)/shard_map/x3/ppermute | solution.py:966
  73.0 31.2 %collective-permute-start.7 = (bf16[512,256]{1,0:T(8,128)(2,1)}, bf16[512,256]{1,0:T(8,128)(2,1)}, u32[]{:S(2)}, u32[]{:S(2)}) collective-permute-start(bf16[512,256]{1,0:T(8,128)(2,1)} %collective-permute-done.5.refs_1_), channel_id=1, source_target_pairs={{0,1},{1,2},{2,3},{3,0},{4,5},{5,6},{6,7},{7,4},{8,9},{9,10},{10,1... | collective-permute-start | bytes 786440 | tf_op jit(solution)/shard_map/out2/ppermute | solution.py:966
  116.0 118.9 %all-gather.10.cloned.1.call-start = ((), (), s32[]{:S(2)}) async-start(), calls=%async_computation.6 | async-start | bytes 9437184 | tf_op jit(solution)/shard_map/all_gather | solution.py:1044
  118.8 336.0 %reduce-scatter.5.cloned.1.call-start = ((), (), s32[]{:S(2)}) async-start(), calls=%async_computation.7 | async-start | bytes 5242880 | tf_op jit(solution)/shard_map/reduce_scatter | solution.py:992
  129.9 27.1 %collective-permute-start.9 = (bf16[1024,512]{1,0:T(8,128)(2,1)S(1)}, bf16[1024,512]{1,0:T(8,128)(2,1)S(1)}, u32[]{:S(2)}, u32[]{:S(2)}) collective-permute-start(bf16[1024,512]{1,0:T(8,128)(2,1)S(1)} %get-tuple-element.266.rest_0_), channel_id=1, source_target_pairs={{0,1},{1,2},{2,3},{3,0},{4,5},{5,6},{6,7},{7,4},{8,9},{9,10},{10,1... | collective-permute-start | bytes 3145736 | tf_op jit(solution)/shard_map/slaba1/ppermute | solution.py:966
  257.9 28.2 %collective-permute-start.14 = (bf16[1024,512]{1,0:T(8,128)(2,1)}, bf16[1024,512]{1,0:T(8,128)(2,1)}, u32[]{:S(2)}, u32[]{:S(2)}) collective-permute-start(bf16[1024,512]{1,0:T(8,128)(2,1)} %collective-permute-done.13.rest_2_), channel_id=1, source_target_pairs={{0,1},{1,2},{2,3},{3,0},{4,5},{5,6},{6,7},{7,4},{8,9},{9,10},{10,1... | collective-permute-start | bytes 3145736 | tf_op jit(solution)/shard_map/slabb3/ppermute | solution.py:966
  266.8 27.3 %collective-permute-start.15 = (bf16[128,2048]{1,0:T(8,128)(2,1)S(1)}, bf16[128,2048]{1,0:T(8,128)(2,1)S(1)}, u32[]{:S(2)}, u32[]{:S(2)}) collective-permute-start(bf16[128,2048]{1,0:T(8,128)(2,1)S(1)} %constant_dynamic-slice_fusion.2), channel_id=1, source_target_pairs={{0,1},{1,2},{2,3},{3,0},{4,5},{5,6},{6,7},{7,4},{8,9},{9,10},{10,1... | collective-permute-start | bytes 1572872 | tf_op jit(solution)/shard_map/sum_a1/ppermute | solution.py:966
  359.4 131.4 %reduce-scatter.9.cloned.1.call-start = ((), (), s32[]{:S(2)}) async-start(), calls=%async_computation.9 | async-start | bytes 5242880 | tf_op jit(solution)/shard_map/reduce_scatter | solution.py:992
  413.5 108.2 %reduce-scatter.7.cloned.1.call-start = ((), (), s32[]{:S(2)}) async-start(), calls=%async_computation.8 | async-start | bytes 5242880 | tf_op jit(solution)/shard_map/reduce_scatter | solution.py:992
  429.4 27.8 %collective-permute-start.39 = (bf16[2048,256]{1,0:T(8,128)(2,1)}, bf16[2048,256]{1,0:T(8,128)(2,1)S(1)}, u32[]{:S(2)}, u32[]{:S(2)}) collective-permute-start(bf16[2048,256]{1,0:T(8,128)(2,1)} %get-tuple-element.378), channel_id=1, source_target_pairs={{0,4},{4,0},{1,5},{5,1},{2,6},{6,2},{3,7},{7,3},{8,12},{12,8},{9,1... | collective-permute-start | bytes 3145736 | tf_op jit(solution)/shard_map/out_grad_swap/ppermute | solution.py:985
  429.4 27.8 %collective-permute-start.38 = (bf16[2048,256]{1,0:T(8,128)(2,1)}, bf16[2048,256]{1,0:T(8,128)(2,1)S(1)}, u32[]{:S(2)}, u32[]{:S(2)}) collective-permute-start(bf16[2048,256]{1,0:T(8,128)(2,1)} %get-tuple-element.376), channel_id=1, source_target_pairs={{0,4},{4,0},{1,5},{5,1},{2,6},{6,2},{3,7},{7,3},{8,12},{12,8},{9,1... | collective-permute-start | bytes 3145736 | tf_op jit(solution)/shard_map/out_grad_swap/ppermute | solution.py:985
  429.9 27.3 %collective-permute-start.37 = (bf16[2048,256]{1,0:T(8,128)(2,1)}, bf16[2048,256]{1,0:T(8,128)(2,1)S(1)}, u32[]{:S(2)}, u32[]{:S(2)}) collective-permute-start(bf16[2048,256]{1,0:T(8,128)(2,1)} %get-tuple-element.374), channel_id=1, source_target_pairs={{0,4},{4,0},{1,5},{5,1},{2,6},{6,2},{3,7},{7,3},{8,12},{12,8},{9,1... | collective-permute-start | bytes 3145736 | tf_op jit(solution)/shard_map/out_grad_swap/ppermute | solution.py:985
  429.9 27.3 %collective-permute-start.36 = (bf16[2048,256]{1,0:T(8,128)(2,1)}, bf16[2048,256]{1,0:T(8,128)(2,1)}, u32[]{:S(2)}, u32[]{:S(2)}) collective-permute-start(bf16[2048,256]{1,0:T(8,128)(2,1)} %get-tuple-element.372), channel_id=1, source_target_pairs={{0,4},{4,0},{1,5},{5,1},{2,6},{6,2},{3,7},{7,3},{8,12},{12,8},{9,1... | collective-permute-start | bytes 3145736 | tf_op jit(solution)/shard_map/out_grad_swap/ppermute | solution.py:985
  462.6 117.1 %reduce-scatter.11.cloned.1.call-start = ((), (), s32[]{:S(2)}) async-start(), calls=%async_computation.10 | async-start | bytes 3932160 | tf_op jit(solution)/shard_map/reduce_scatter | solution.py:992
  504.5 28.2 %collective-permute-start.46 = (bf16[256,2048]{1,0:T(8,128)(2,1)}, bf16[256,2048]{1,0:T(8,128)(2,1)}, u32[]{:S(2)}, u32[]{:S(2)}) collective-permute-start(bf16[256,2048]{1,0:T(8,128)(2,1)} %copy-done.62), channel_id=1, source_target_pairs={{0,1},{1,2},{2,3},{3,0},{4,5},{5,6},{6,7},{7,4},{8,9},{9,10},{10,1... | collective-permute-start | bytes 3145736 | tf_op jit(solution)/shard_map/back2/ppermute | solution.py:966
  537.4 31.8 %collective-permute-start.49 = (bf16[256,2048]{1,0:T(8,128)(2,1)S(1)}, bf16[256,2048]{1,0:T(8,128)(2,1)S(1)}, u32[]{:S(2)}, u32[]{:S(2)}) collective-permute-start(bf16[256,2048]{1,0:T(8,128)(2,1)S(1)} %shard_map.396), channel_id=1, source_target_pairs={{0,1},{1,2},{2,3},{3,0},{4,5},{5,6},{6,7},{7,4},{8,9},{9,10},{10,1... | collective-permute-start | bytes 3145736 | tf_op jit(solution)/shard_map/back3/ppermute | solution.py:966
  537.4 31.6 %collective-permute-start.47 = (bf16[512,256]{1,0:T(8,128)(2,1)S(1)}, bf16[512,256]{1,0:T(8,128)(2,1)S(1)}, u32[]{:S(2)}, u32[]{:S(2)}) collective-permute-start(bf16[512,256]{1,0:T(8,128)(2,1)S(1)} %shard_map.397), channel_id=1, source_target_pairs={{0,1},{1,2},{2,3},{3,0},{4,5},{5,6},{6,7},{7,4},{8,9},{9,10},{10,1... | collective-permute-start | bytes 786440 | tf_op jit(solution)/shard_map/out_sum2/ppermute | solution.py:966
  577.5 27.7 %collective-permute-start.50 = (bf16[256,2048]{1,0:T(8,128)(2,1)}, bf16[256,2048]{1,0:T(8,128)(2,1)}, u32[]{:S(2)}, u32[]{:S(2)}) collective-permute-start(bf16[256,2048]{1,0:T(8,128)(2,1)} %shard_map.398), channel_id=1, source_target_pairs={{0,1},{1,2},{2,3},{3,0},{4,5},{5,6},{6,7},{7,4},{8,9},{9,10},{10,1... | collective-permute-start | bytes 3145736 | tf_op jit(solution)/shard_map/ffn2/ppermute | solution.py:966
  (140 other events, 1596.3 us)
Sparse Core Ops, SparseCore 0:
  10.5 48.5 all-gather.5
  61.6 54.3 all-gather.7
  118.5 54.3 all-gather.11
  175.2 55.9 all-gather.9
  359.5 50.6 reduce-scatter.4
  413.6 52.3 reduce-scatter.8
  469.0 52.7 reduce-scatter.6
  525.0 43.9 reduce-scatter.10

commit v4 on v3

--- a/solution.py
+++ b/solution.py
@@ -111,14 +111,29 @@
     )(place, x, gain, weight, cosine, sine, *(carried or ()))
 
 
-def attend_body(half, blocks, count, q_ref, k_ref, v_ref, *rest):
-    cotangents, (ring_ref, log_ref) = rest[:count], rest[count:]
+def pack_body(in_ref, out_ref):
+    out_ref[...] = in_ref[...].astype(LOW)
+
+
+def pack_half(half, cotangent, cols):
+    rows, width = cotangent.shape
+    count = width // cols
+    return pl.pallas_call(
+        pack_body,
+        grid=(count,),
+        in_specs=[pl.BlockSpec((rows // 2, cols), lambda j: (half, j))],
+        out_specs=pl.BlockSpec((rows // 2, cols), lambda j: (j, 0)),
+        out_shape=jax.ShapeDtypeStruct((count * rows // 2, cols), LOW),
+        compiler_params=params(),
+        cost_estimate=LIGHT,
+    )(cotangent)
+
+
+def attend_body(half, blocks, q_ref, k_ref, v_ref, lower_ref, ring_ref, log_ref):
     length = q_ref.shape[1]
     block = length // blocks
     rows = block // 2
-    for index in range(count):
-        first = length // 2 + index * rows
-        ring_ref[first : first + rows] = cotangents[index][...].astype(LOW)
+    ring_ref[length // 2 :] = lower_ref[...]
     for index in range(blocks):
         first = index * block + half * rows
         last = first + rows
@@ -140,47 +155,41 @@
         )
 
 
-def attend(half, blocks, qkv, cotangent):
+def attend(half, blocks, qkv, lower):
     _, length, cols = qkv.shape
     heads = cols // HD
-    rows, width = cotangent.shape
-    count = width // cols
-
-    def cotangent_spec(index):
-        return pl.BlockSpec((rows // 2, HD), lambda h: (half, index * heads + h))
-
-    return pl.pallas_call(
-        functools.partial(attend_body, half, blocks, count),
+    below = lower.shape[0]
+    return pl.pallas_call(
+        functools.partial(attend_body, half, blocks),
         grid=(heads,),
         in_specs=[
             pl.BlockSpec((1, length, HD), lambda h: (0, 0, h)),
             pl.BlockSpec((1, length, HD), lambda h: (1, 0, h)),
             pl.BlockSpec((1, length, HD), lambda h: (2, 0, h)),
-        ]
-        + [cotangent_spec(index) for index in range(count)],
+            pl.BlockSpec((below, HD), lambda h: (0, h)),
+        ],
         out_specs=[
-            pl.BlockSpec((length // 2 + count * rows // 2, HD), lambda h: (0, h)),
+            pl.BlockSpec((length // 2 + below, HD), lambda h: (0, h)),
             pl.BlockSpec((length // 2, HD), lambda h: (0, h)),
         ],
         out_shape=[
-            jax.ShapeDtypeStruct((length // 2 + count * rows // 2, cols), LOW),
+            jax.ShapeDtypeStruct((length // 2 + below, cols), LOW),
             jax.ShapeDtypeStruct((length // 2, cols), FULL),
         ],
         compiler_params=params(),
         cost_estimate=LIGHT,
-    )(qkv, qkv, qkv, *[cotangent] * count)
+    )(qkv, qkv, qkv, lower)
 
 
 def attend_back_body(blocks, place_ref, q_ref, k_ref, v_ref, log_a_ref, log_b_ref, cos_ref, sin_ref, *rest):
-    pieces = rest[: 2 * blocks]
-    out_ref, key_acc, value_acc, back_ref = rest[2 * blocks :]
+    pieces = rest[:blocks]
+    out_ref, key_acc, value_acc, back_ref = rest[blocks:]
     length = q_ref.shape[1]
     block = length // blocks
     rows = block // 2
-    for half in range(2):
-        for step in range(blocks):
-            first = pl.multiple_of(place_ref[step] * block + half * rows, rows)
-            back_ref[pl.ds(first, rows), :] = pieces[half * blocks + step][...]
+    for step in range(blocks):
+        first = pl.multiple_of(place_ref[step] * block, block)
+        back_ref[pl.ds(first, block), :] = pieces[step][...]
 
     def turn_back(one, cosine, sine):
         return one * cosine - pltpu.roll(one, HD // 2, 1) * sine
@@ -220,7 +229,7 @@
 def attend_back(places, qkv, pieces, logs, cosine, sine):
     _, length, cols = qkv.shape
     heads = cols // HD
-    blocks = len(pieces) // 2
+    blocks = len(pieces)
     column = lambda h, p: (0, h)
     return pl.pallas_call(
         functools.partial(attend_back_body, blocks),
@@ -236,7 +245,7 @@
                 pl.BlockSpec((length, HD), lambda h, p: (0, 0)),
                 pl.BlockSpec((length, HD), lambda h, p: (0, 0)),
             ]
-            + [pl.BlockSpec((length // blocks // 2, HD), column)] * (2 * blocks),
+            + [pl.BlockSpec((length // blocks, HD), column)] * blocks,
             out_specs=pl.BlockSpec((3, length, HD), lambda h, p: (0, 0, h)),
             scratch_shapes=[
                 pltpu.VMEM((length, HD), FULL),
@@ -366,9 +375,14 @@
     units = up.shape[1]
     tile = min(512, units)
     count = len(pieces)
-    cols = pieces[0].shape[1]
-    below = pieces[0].shape[0] - length
+    rows = length // count
+    cols = pieces[0][0].shape[1]
+    below = rows * width // cols
     whole = lambda i, p, l: (0, 0)
+
+    def piece_spec(index):
+        return pl.BlockSpec((below, cols), lambda i, p, l: (index, 0))
+
     column = lambda i, p, l: (0, i)
     return pl.pallas_call(
         functools.partial(hidden_body, count),
@@ -380,7 +394,7 @@
                 pl.BlockSpec((width, tile), column),
                 pl.BlockSpec((tile, width), lambda i, p, l: (i, 0)),
             ]
-            + [pl.BlockSpec((below, cols), lambda i, p, l: (length // below, 0))] * count,
+            + [piece_spec(index) for _, index in pieces],
             out_specs=[
                 pl.BlockSpec((length, tile), column),
                 pl.BlockSpec((length, tile), column),
@@ -392,9 +406,9 @@
             jax.ShapeDtypeStruct((length, units), LOW),
             jax.ShapeDtypeStruct((length, width), LOW),
         ],
-        compiler_params=params(),
-        cost_estimate=LIGHT,
-    )(places, live, normed, up, down, *pieces)
+        compiler_params=params(56 * 1024 * 1024),
+        cost_estimate=LIGHT,
+    )(places, live, normed, up, down, *[piece for piece, _ in pieces])
 
 
 def product_body(dims, left_ref, right_ref, out_ref):
@@ -732,11 +746,13 @@
     )(place.reshape(1).astype(jnp.int32), source, arrived, part, gain, *bases)
 
 
-def mix_back_body(place_ref, low_ref, weight_ref, *out_refs):
+def mix_back_body(count, place_ref, *refs):
+    lows, weight_ref, out_refs = refs[:count], refs[count], refs[count + 1 :]
     total = None
     shards, _, _, shard = weight_ref.shape
     for index in range(shards):
-        left = low_ref[:, index * shard : (index + 1) * shard]
+        span = slice(index * shard, (index + 1) * shard)
+        left = jnp.concatenate([low[:, span] for low in lows], axis=0)
         product = lax.dot_general(left, weight_ref[index, 0], NT, preferred_element_type=FULL)
         total = product if total is None else total + product
     value = total.astype(LOW)
@@ -747,25 +763,24 @@
             out[...] = value
 
 
-def mix_back(targets, low, weight):
-    rows, width = low.shape
+def mix_back(targets, lows, weight):
+    rows, width = lows[0].shape
     shards, count, cols, shard = weight.shape
-    spec = pl.BlockSpec((rows, cols), lambda i, p: (0, 0))
-    return pl.pallas_call(
-        mix_back_body,
+    total = rows * len(lows)
+    spec = pl.BlockSpec((total, cols), lambda i, p: (0, 0))
+    return pl.pallas_call(
+        functools.partial(mix_back_body, len(lows)),
         grid_spec=pltpu.PrefetchScalarGridSpec(
             num_scalar_prefetch=1,
             grid=(count,),
-            in_specs=[
-                pl.BlockSpec((rows, width), lambda i, p: (0, 0)),
-                pl.BlockSpec((shards, 1, cols, shard), lambda i, p: (0, p[i], 0, 0)),
-            ],
+            in_specs=[pl.BlockSpec((rows, width), lambda i, p: (0, 0))] * len(lows)
+            + [pl.BlockSpec((shards, 1, cols, shard), lambda i, p: (0, p[i], 0, 0))],
             out_specs=[spec] * count,
         ),
-        out_shape=[jax.ShapeDtypeStruct((rows, cols), LOW)] * count,
-        compiler_params=params(),
-        cost_estimate=LIGHT,
-    )(targets, low, weight)
+        out_shape=[jax.ShapeDtypeStruct((total, cols), LOW)] * count,
+        compiler_params=params(),
+        cost_estimate=LIGHT,
+    )(targets, *lows, weight)
 
 
 def project_back_body(place_ref, back_ref, weight_ref, out_ref):
@@ -997,6 +1012,9 @@
     x_held = [block_in, pass_on("x1", block_in)]
     (out_low,) = round_low(at(out_weight), 1)
     did(out_low)
+    cols = qkv_weight.shape[2]
+    lower_a = did(pack_half(0, at(cotangent), cols))
+    lower_b = [did(pack_half(1, at(cotangent), cols))]
     x_held[1] = wait(x_held[1])
     x_held.append(pass_on("x2", x_held[1]))
     out_held = [out_low, pass_on("out1", out_low)]
@@ -1038,24 +1056,29 @@
     did(normed_one)
     out_held[-1] = wait(out_held[-1])
     out_depth, out_width = out_weight.shape
+    lower_b.append(pass_on("cotangent_b1", lower_b[0]))
     out_line = did(lay(group, [at(out_held[0])] + out_held[1:], list(range(bkts))))
     out_full = lax.all_gather(after(out_line, up_full), tok, axis=0, tiled=False)
     (down_low,) = round_low(at(down_weight), 1)
     down_full = lax.all_gather(did(down_low), tok, axis=1, tiled=True)
-    cols = qkv.shape[2]
     seq_in = seq_in.reshape(bkts, rows, width)
 
-    slab, log_a = attend(0, bkts, at(qkv), cotangent)
+    upper = length // 2
+    slab, log_a = attend(0, bkts, at(qkv), lower_a)
     slabs = [[did(slab)], []]
 
     def next_slab(part):
         held = slabs[part]
         if len(held) > 1:
             held[-1] = wait(held[-1])
-        held.append(pass_on("slab" + "ab"[part] + str(len(held)), held[-1]))
-
+        value = held[-1]
+        if part == 1 and len(held) == bkts - 1:
+            value = value[:upper]
+        held.append(pass_on("slab" + "ab"[part] + str(len(held)), value))
+
+    lower_b[1] = wait(lower_b[1])
     next_slab(0)
-    slab, log_b = attend(1, bkts, at(qkv), cotangent)
+    slab, log_b = attend(1, bkts, at(qkv), lower_b[1])
     slabs[1].append(did(slab))
     logs = [log_a, log_b]
     for step in range(2, bkts):
@@ -1069,31 +1092,37 @@
     normed_a, middle_a, mixed_a = mix_last(places, acc, gain_float[1:2], slabs[0], out_full)
     did(normed_a)
     next_slab(1)
-    hidden_a, inner_a, low_a = hidden_units(places, live, at(normed_a), up_full, down_full, slabs[0])
+    hidden_a, inner_a, low_a = hidden_units(
+        places, live, at(normed_a), up_full, down_full, [(slab, 1) for slab in slabs[0]]
+    )
     did(inner_a)
     next_slab(1)
     back_a = did(product(at(inner_a), up_full, True))
     sum_a = did(rows_of(back_a, 1))
     arrived_a = pass_on("sum_a1", sum_a)
     acc = did(mix_first(1, places, at(seq_in), slabs[1][:-1], out_full))
-    prod_a = did(product(at(hidden_a), down_full, False))
     slabs[1][-1] = wait(slabs[1][-1])
     normed_b, middle_b, mixed_b = mix_last(places, at(acc), gain_float[1:2], slabs[1], out_full)
     did(normed_b)
     sum_a = add(arrived_a, back_a, 2)
     arrived_a = pass_on("sum_a2", sum_a)
 
-    hidden_b, inner_b, low_b = hidden_units(places, live, at(normed_b), up_full, down_full, slabs[1])
+    hidden_b, inner_b, low_b = hidden_units(
+        places,
+        live,
+        at(normed_b),
+        up_full,
+        down_full,
+        [(lower_b[0], 0), (lower_b[1], 0)] + [(slab, 1) for slab in slabs[1][1:-1]],
+    )
     did(inner_b)
     sum_a = add(arrived_a, back_a, 3)
     arrived_a = pass_on("sum_a3", sum_a)
+    back_b = did(product(at(inner_b), up_full, True))
+    sum_b = did(rows_of(at(back_b), 1))
+    arrived_b = pass_on("sum_b1", sum_b)
     up_kept, up_sent = weight_grad(core_id, [normed_a, normed_b], [at(inner_a), inner_b], chips, 0)
     did(up_kept)
-    back_b = did(product(at(inner_b), up_full, True))
-    arrived_a = wait(arrived_a)
-    sum_b = did(rows_of(at(back_b), 1))
-    arrived_b = pass_on("sum_b1", sum_b)
-    up_arrived = swap("up_grad", up_sent)
 
     first = jnp.zeros((), jnp.int32)
     targets = jnp.stack([lax.rem(group + step, bkts) for step in range(bkts)]).astype(jnp.int32)
@@ -1102,75 +1131,75 @@
         grad, gain_sum, low = norm_back(
             owner(0), middle, at(arrived), back, gain_float[1:2], [cotangent], part * half, True
         )
-        found = list(mix_back(targets, low, out_full))
-        did(found[0])
-        return grad, low, gain_sum, found
-
-    def exchange(part, found):
-        with jax.named_scope("exchange" + str(part)):
+        did(low)
+        return grad, low, gain_sum
+
+    def exchange(found):
+        with jax.named_scope("exchange"):
             for step in range(1, bkts):
                 found[step] = lax.ppermute(
                     at(found[step]), "bkt", [(i, (i + step) % bkts) for i in range(bkts)]
                 )
 
-    grad_a, mid_low_a, gain_a, pieces_a = middle_back(0, middle_a, arrived_a, back_a)
+    arrived_a = wait(arrived_a)
     sum_b = add(arrived_b, back_b, 2)
     arrived_b = pass_on("sum_b2", sum_b)
-    exchange(0, pieces_a)
+    up_arrived = swap("up_grad", up_sent)
+    grad_a, mid_low_a, gain_a = middle_back(0, middle_a, arrived_a, back_a)
+    prod_b = did(product(at(hidden_b), down_full, False))
+    sum_b = add(arrived_b, back_b, 3)
     up_core = core_add(up_kept, up_arrived)
     up_part = chip_sum(up_core)
+    arrived_b = pass_on("sum_b3", sum_b)
     down_kept, down_sent = weight_grad(core_id, [hidden_a, hidden_b], [at(low_a), low_b], chips, 1)
     did(down_kept)
-    pieces_a = pieces_a[:1] + [wait(piece) for piece in pieces_a[1:]]
-    sum_b = add(arrived_b, back_b, 3)
-    arrived_b = pass_on("sum_b3", sum_b)
+    grad_b, mid_low_b, gain_b = middle_back(1, middle_b, arrived_b, back_b)
     down_arrived = swap("down_grad", down_sent)
-    prod_b = did(product(at(hidden_b), down_full, False))
-    grad_b, mid_low_b, gain_b, pieces_b = middle_back(1, middle_b, arrived_b, back_b)
-    exchange(1, pieces_b)
+    pieces = list(mix_back(targets, [mid_low_a, at(mid_low_b)], out_full))
+    did(pieces[0])
     down_core = core_add(down_kept, down_arrived)
     down_part = chip_sum(down_core)
+    exchange(pieces)
     out_kept, out_sent = weight_grad(
         core_id, [at(mixed_a), mixed_b], [mid_low_a, mid_low_b], chips, 1
     )
     did(out_kept)
+    prod_a = did(product(at(hidden_a), down_full, False))
     prods = [prod_a, prod_b]
     ffn = did(pair_add(owner(1), half, [at(prod_a), prod_b], None, None, LOW))
-    pieces_b = pieces_b[:1] + [wait(piece) for piece in pieces_b[1:]]
+    pieces = pieces[:1] + [wait(piece) for piece in pieces[1:]]
     arrived_f = pass_on("ffn1", ffn)
     out_arrived = swap("out_grad", out_sent)
 
-    back_project = did(attend_back(places, at(qkv), pieces_a + pieces_b, logs, cosine, sine))
+    back_project = did(attend_back(places, at(qkv), pieces, logs, cosine, sine))
     total = did(project_back(owner(1), at(back_project), qkv_full, rows))
     arrived_f = wait(arrived_f)
-    up_squares = did(squares(at(up_part)))
     out_core = core_add(out_kept, out_arrived)
     out_sum = chip_sum(out_core)
     arrived = pass_on("back1", total)
+    up_squares = did(squares(at(up_part)))
     qkv_kept, qkv_sent = project_grad(core_id, normed_one, at(back_project), chips)
     did(qkv_kept)
     own = did(project_back(owner(2), at(back_project), qkv_full, rows))
     total = did(ring_add(first, at(arrived), own, LOW))
-    down_squares = did(squares(at(down_part)))
     arrived = pass_on("back2", total)
     qkv_arrived = swap("qkv_grad", qkv_sent)
     own = did(project_back(owner(3), at(back_project), qkv_full, rows))
+    last_own = did(project_back(owner(0), at(back_project), qkv_full, rows))
+    down_squares = did(squares(at(down_part)))
+    total = did(ring_add(first, at(arrived), own, LOW))
     qkv_core = core_add(qkv_kept, qkv_arrived)
     qkv_part = chip_sum(qkv_core)
-    last_own = did(project_back(owner(0), at(back_project), qkv_full, rows))
+    arrived = pass_on("back3", total)
     arrived_out = pass_on("out_sum1", rows_of(out_sum, 1))
-    total = did(ring_add(first, at(arrived), own, LOW))
-    out_part = add(arrived_out, out_sum, 2)
-    arrived_out = pass_on("out_sum2", out_part)
-    arrived = pass_on("back3", total, out_part)
     ffn = did(pair_add(owner(2), half, prods, at(arrived_f), None, LOW))
-    for step in range(3, bkts):
-        out_part = add(arrived_out, out_sum, step)
-        arrived_out = pass_on("out_sum" + str(step), out_part)
     block_in_grad, gain_one = norm_back(
         first, block_in, at(arrived), last_own, gain_float[0:1], [grad_a, grad_b], 0, False
     )
     did(gain_one)
+    for step in range(2, bkts):
+        out_part = add(arrived_out, out_sum, step)
+        arrived_out = pass_on("out_sum" + str(step), out_part)
     out_part = add_final(arrived_out, out_sum)
     arrived_f = pass_on("ffn2", ffn)
     out_squares = did(squares(at(out_part)))

time: 657 us -> 635 us (0.967)
  waiting for transfers between devices: 231 us -> 221 us
  local copies, waits for them, and re-layouts: 50.1 us -> 42.2 us
    pallas_call x4 -> x5, Pallas kernels: 30.1 us -> 22.8 us  [the longest x2 16.2 us: attend(): pl.pallas_call(functools.partial(attend_body, half, blocks), grid=(heads,...]
    unnamed x198 -> x164, local copies, waits for them, and re-layouts: 47.5 us -> 40.6 us
    ppermute x27 -> x28, starting transfers between devices: 17.2 us -> 22.3 us  [pass_on(): return lax.ppermute(at(value, *others), 'bkt', ring)]
    ppermute x27 -> x28, waiting for transfers between devices: 195 us -> 199 us  [pass_on(): return lax.ppermute(at(value, *others), 'bkt', ring)]
  transfers between devices with their start and end apart: 65 -> 63, of which waited for: 30 -> 29; matrix products, arithmetic and copies ran while one was open for 2% -> 2% of each run, Pallas kernels for 43% -> 43%
where the time goes in v4:
time: 635 us; the launch traced here: 624 us
  Pallas kernels  287 us (45%)
  waiting for transfers between devices  221 us (35%)
  local copies, waits for them, and re-layouts  42.2 us (7%)
  starting transfers between devices  38.2 us (6%)
  between operations  21.5 us (3%)
  other arithmetic  14.8 us (2%)
    ppermute x28, waiting for transfers between devices, pass_on(): return lax.ppermute(at(value, *others), 'bkt', ring)  199 us
    unnamed x164, local copies, waits for them, and re-layouts  40.6 us
    pallas_call x3, Pallas kernels, weight_grad(): pl.pallas_call(functools.partial(grad_body, len(lefts), axis), grid_spec=...  35.2 us
    pallas_call x4, Pallas kernels, product(): pl.pallas_call(functools.partial(product_body, NT if turned else NN), gri...  29.2 us
    pallas_call x2, Pallas kernels, hidden_units(): pl.pallas_call(functools.partial(hidden_body, count), grid_spec=pltpu.Pre...  29.1 us
    pallas_call x4, Pallas kernels, project(): pl.pallas_call(project_body, grid_spec=pltpu.PrefetchScalarGridSpec(num_s...  28.3 us
    ppermute x28, starting transfers between devices, pass_on(): return lax.ppermute(at(value, *others), 'bkt', ring)  22.3 us
    pallas_call x4, Pallas kernels, core_add_kernel(): pl.pallas_call(core_add_body, grid=(rows // tile,), in_specs=[spec] + [pl...  21.9 us
  transfers between devices with their start and end apart: 63, of which 29 were waited for; matrix products, arithmetic and copies ran while one was open for 2% of the time, Pallas kernels for 43%

profile of v4, /device:TPU:0, one launch (start us, length us, event | category | flops | bytes accessed | tf_op | source)
XLA Modules:
  0.0 624.5 jit_solution(12692448786102003401)
XLA Ops:
  16.1 22.1 %collective-permute-done.x_ref = bf16[256,2048]{1,0:T(8,128)(2,1)} collective-permute-done((bf16[256,2048]{1,0:T(8,128)(2,1)S(1)}, bf16[256,2048]{1,0:T(8,128)(2,1)}, u32[]{:S(2)}, u32[]{:S(2)}) %collective-permute-start) | collective-permute-done | bytes 1048608 | tf_op jit(solution)/shard_map/x1/ppermute | solution.py:981
  49.8 18.5 %collective-permute-done.1.x_ref = bf16[256,2048]{1,0:T(8,128)(2,1)} collective-permute-done((bf16[256,2048]{1,0:T(8,128)(2,1)}, bf16[256,2048]{1,0:T(8,128)(2,1)}, u32[]{:S(2)}, u32[]{:S(2)}) %collective-permute-start.1) | collective-permute-done | bytes 1048608 | tf_op jit(solution)/shard_map/x2/ppermute | solution.py:981
  89.0 7.8 %shard_map.359 = (bf16[1024,2048]{1,0:T(8,128)(2,1)}, bf16[3,1024,512]{2,1,0:T(8,128)(2,1)S(1)}, bf16[1024,2048]{1,0:T(8,128)(2,1)}) custom-call(s32[1]{0:T(128)} %bitcast.2.place_ref, bf16[256,2048]{1,0:T(8,128)(2,1)} %collective-permute-done.1.x_ref, f32[1,2048]{1,0:T(1,128)S(1)} %bitcast.26, ...), custom_call_target="tpu_custom_call", output_to_operand_aliasing={{0}: (6, {}), {1}: (7, {}), {2}: (8, {})} | custom-call | flops 1 | bytes 1 | tf_op jit(solution)/shard_map/pallas_call | solution.py:95
  121.4 7.8 %shard_map.363 = (bf16[1024,512]{1,0:T(8,128)(2,1)S(1)}, f32[512,512]{1,0:T(8,128)S(1)}) custom-call(bf16[3,1024,512]{2,1,0:T(8,128)(2,1)S(1)} %get-tuple-element.354.q_ref.k_ref.v_ref, bf16[3,1024,512]{2,1,0:T(8,128)(2,1)S(1)} %get-tuple-element.354.q_ref.k_ref.v_ref, bf16[3,1024,512]{2,1,0:T(8,128)(2,1)S(1)} %get-tuple-element.354.q_ref.k_ref.v_ref, ...), custom_call_target="tpu_custom_call" | custom-call | flops 1 | bytes 1 | tf_op jit(solution)/shard_map/pallas_call | solution.py:162
  135.0 8.4 %shard_map.364 = (bf16[1024,512]{1,0:T(8,128)(2,1)}, f32[512,512]{1,0:T(8,128)S(1)}) custom-call(bf16[3,1024,512]{2,1,0:T(8,128)(2,1)S(1)} %get-tuple-element.354.q_ref.k_ref.v_ref, bf16[3,1024,512]{2,1,0:T(8,128)(2,1)S(1)} %get-tuple-element.354.q_ref.k_ref.v_ref, bf16[3,1024,512]{2,1,0:T(8,128)(2,1)S(1)} %get-tuple-element.354.q_ref.k_ref.v_ref, ...), custom_call_target="tpu_custom_call" | custom-call | flops 1 | bytes 1 | tf_op jit(solution)/shard_map/pallas_call | solution.py:162
  144.4 16.9 %collective-permute-done.10.rest_1_ = bf16[1024,512]{1,0:T(8,128)(2,1)S(1)} collective-permute-done((bf16[1024,512]{1,0:T(8,128)(2,1)S(1)}, bf16[1024,512]{1,0:T(8,128)(2,1)S(1)}, u32[]{:S(2)}, u32[]{:S(2)}) %collective-permute-start.10) | collective-permute-done | bytes 1048608 | tf_op jit(solution)/shard_map/slaba1/ppermute | solution.py:981
  162.3 24.4 %collective-permute-done.11.rest_2_ = bf16[1024,512]{1,0:T(8,128)(2,1)S(1)} collective-permute-done((bf16[1024,512]{1,0:T(8,128)(2,1)S(1)}, bf16[1024,512]{1,0:T(8,128)(2,1)S(1)}, u32[]{:S(2)}, u32[]{:S(2)}) %collective-permute-start.11) | collective-permute-done | bytes 1048608 | tf_op jit(solution)/shard_map/slaba2/ppermute | solution.py:981
  186.7 24.5 %collective-permute-done.12.rest_3_ = bf16[1024,512]{1,0:T(8,128)(2,1)S(1)} collective-permute-done((bf16[1024,512]{1,0:T(8,128)(2,1)S(1)}, bf16[1024,512]{1,0:T(8,128)(2,1)S(1)}, u32[]{:S(2)}, u32[]{:S(2)}) %collective-permute-start.12) | collective-permute-done | bytes 1048608 | tf_op jit(solution)/shard_map/slaba3/ppermute | solution.py:981
  214.0 8.2 %shard_map.365.acc_ref = f32[512,2048]{1,0:T(8,128)} custom-call(s32[4]{0:T(128)S(1)} %pad_add_fusion.place_ref, bf16[4,256,2048]{2,1,0:T(8,128)(2,1)} %bitcast.44, bf16[1024,512]{1,0:T(8,128)(2,1)S(1)} %copy-done.19, bf16[1024,512]{1,0:T(8,128)(2,1)S(1)} %copy-done.21, bf16[1024,512]{1,0:T(8,128)(2,1)S(1)} %collective-permute-done.11.rest_2_, ...), custom_call_target="tpu_custom_call" | custom-call | flops 1 | bytes 1 | tf_op jit(solution)/shard_map/pallas_call | solution.py:284
  235.8 14.6 %shard_map.367 = (bf16[512,2048]{1,0:T(8,128)(2,1)}, bf16[512,2048]{1,0:T(8,128)(2,1)}, bf16[512,2048]{1,0:T(8,128)(2,1)}) custom-call(s32[4]{0:T(128)} %copy-done.70, f32[1]{0:T(128)S(6)} %convert_element_type.48.live_ref, bf16[512,2048]{1,0:T(8,128)(2,1)} %get-tuple-element.278.normed_ref.refs_0_, ...), custom_call_target="tpu_custom_call" | custom-call | flops 1 | bytes 1 | tf_op jit(solution)/shard_map/pallas_call | solution.py:387
  250.3 8.0 %collective-permute-done.14.rest_2_.rest_3_ = bf16[1024,512]{1,0:T(8,128)(2,1)S(1)} collective-permute-done((bf16[1024,512]{1,0:T(8,128)(2,1)S(1)}, bf16[1024,512]{1,0:T(8,128)(2,1)S(1)}, u32[]{:S(2)}, u32[]{:S(2)}) %collective-permute-start.14) | collective-permute-done | bytes 1048608 | tf_op jit(solution)/shard_map/slabb2/ppermute | solution.py:981
  260.3 7.2 %shard_map.368.part_ref = bf16[512,2048]{1,0:T(8,128)(2,1)S(1)} custom-call(bf16[512,2048]{1,0:T(8,128)(2,1)S(1)} %copy-done.27, bf16[2048,2048]{1,0:T(8,128)(2,1)} %all-gather.8.cloned.1.call-done.up_ref.right_ref), custom_call_target="tpu_custom_call" | custom-call | flops 1 | bytes 1 | tf_op jit(solution)/shard_map/pallas_call | solution.py:428
  267.6 8.4 %shard_map.369.acc_ref = f32[512,2048]{1,0:T(8,128)} custom-call(s32[4]{0:T(128)S(1)} %copy-done.71, bf16[4,256,2048]{2,1,0:T(8,128)(2,1)} %bitcast.45, bf16[1024,512]{1,0:T(8,128)(2,1)} %get-tuple-element.276.rest_0_, bf16[1024,512]{1,0:T(8,128)(2,1)S(1)} %collective-permute-done.13.rest_1_.rest_2_, ...), custom_call_target="tpu_custom_call" | custom-call | flops 1 | bytes 1 | tf_op jit(solution)/shard_map/pallas_call | solution.py:284
  283.4 14.5 %shard_map.372 = (bf16[512,2048]{1,0:T(8,128)(2,1)}, bf16[512,2048]{1,0:T(8,128)(2,1)}, bf16[512,2048]{1,0:T(8,128)(2,1)}) custom-call(s32[4]{0:T(128)} %copy-done.70, f32[1]{0:T(128)S(6)} %convert_element_type.48.live_ref, bf16[512,2048]{1,0:T(8,128)(2,1)} %get-tuple-element.292.normed_ref.refs_1_, ...), custom_call_target="tpu_custom_call" | custom-call | flops 1 | bytes 1 | tf_op jit(solution)/shard_map/pallas_call | solution.py:387
  311.5 15.0 %shard_map.375 = (bf16[4,256,2048]{2,1,0:T(8,128)(2,1)}, bf16[256,2048]{1,0:T(8,128)(2,1)}, bf16[256,2048]{1,0:T(8,128)(2,1)}, bf16[256,2048]{1,0:T(8,128)(2,1)}, bf16[256,2048]{1,0:T(8,128)(2,1)}) custom-call(s32[1]{0:T(128)} %bitcast.12.core_ref, bf16[512,2048]{1,0:T(8,128)(2,1)} %get-tuple-element.278.normed_ref.refs_0_, ...), custom_call_target="tpu_custom_call" | custom-call | flops 1 | bytes 1 | tf_op jit(solution)/shard_map/pallas_call | solution.py:486
  333.7 7.7 %shard_map.378.refs_1_ = bf16[512,2048]{1,0:T(8,128)(2,1)S(1)} custom-call(bf16[512,2048]{1,0:T(8,128)(2,1)S(1)} %copy-done.26, bf16[2048,2048]{1,0:T(8,128)(2,1)} %all-gather.10.cloned.1.call-done.down_ref.right_ref), custom_call_target="tpu_custom_call" | custom-call | flops 1 | bytes 1 | tf_op jit(solution)/shard_map/pallas_call | solution.py:428
  352.4 13.6 %shard_map.381 = (bf16[4,2048,256]{2,1,0:T(8,128)(2,1)}, bf16[2048,256]{1,0:T(8,128)(2,1)}, bf16[2048,256]{1,0:T(8,128)(2,1)}, bf16[2048,256]{1,0:T(8,128)(2,1)}, bf16[2048,256]{1,0:T(8,128)(2,1)}) custom-call(s32[1]{0:T(128)} %bitcast.12.core_ref, bf16[512,2048]{1,0:T(8,128)(2,1)} %get-tuple-element.342.refs_0_.left_ref, ...), custom_call_target="tpu_custom_call" | custom-call | flops 1 | bytes 1 | tf_op jit(solution)/shard_map/pallas_call | solution.py:486
  418.1 15.1 %shard_map.388.back_ref.right_ref = bf16[3,1024,512]{2,1,0:T(8,128)(2,1)} custom-call(s32[4]{0:T(128)S(1)} %copy-done.72, bf16[3,1024,512]{2,1,0:T(8,128)(2,1)} %copy-done, bf16[3,1024,512]{2,1,0:T(8,128)(2,1)} %copy-done, bf16[3,1024,512]{2,1,0:T(8,128)(2,1)} %copy-done, f32[512,512]{1,0:T(8,128)S(1)} %copy-done.53, f32[512,512]{1,0:T(8,128)S(1)} %copy-done.55, ...), custom_call_target="tpu_custom_call" | custom-call | flops 1 | bytes 1 | tf_op jit(solution)/shard_map/pallas_call | solution.py:234
  450.3 12.0 %shard_map.391 = (bf16[4,256,1536]{2,1,0:T(8,128)(2,1)}, bf16[256,1536]{1,0:T(8,128)(2,1)}, bf16[256,1536]{1,0:T(8,128)(2,1)}, bf16[256,1536]{1,0:T(8,128)(2,1)}, bf16[256,1536]{1,0:T(8,128)(2,1)}) custom-call(s32[1]{0:T(128)} %bitcast.12.core_ref, bf16[1024,2048]{1,0:T(8,128)(2,1)} %get-tuple-element.257.left_ref, ...), custom_call_target="tpu_custom_call" | custom-call | flops 1 | bytes 1 | tf_op jit(solution)/shard_map/pallas_call | solution.py:517
  487.5 13.2 %collective-permute-done.39.arrived_ref = bf16[256,2048]{1,0:T(8,128)(2,1)} collective-permute-done((bf16[256,2048]{1,0:T(8,128)(2,1)}, bf16[256,2048]{1,0:T(8,128)(2,1)}, u32[]{:S(2)}, u32[]{:S(2)}) %collective-permute-start.39) | collective-permute-done | bytes 1048608 | tf_op jit(solution)/shard_map/back2/ppermute | solution.py:981
  520.0 16.6 %collective-permute-done.45.arrived_ref = bf16[256,2048]{1,0:T(8,128)(2,1)} collective-permute-done((bf16[256,2048]{1,0:T(8,128)(2,1)}, bf16[256,2048]{1,0:T(8,128)(2,1)}, u32[]{:S(2)}, u32[]{:S(2)}) %collective-permute-start.45) | collective-permute-done | bytes 1048608 | tf_op jit(solution)/shard_map/back3/ppermute | solution.py:981
  541.3 8.6 %collective-permute-done.46.arrived_ref = bf16[512,256]{1,0:T(8,128)(2,1)S(1)} collective-permute-done((bf16[512,256]{1,0:T(8,128)(2,1)S(1)}, bf16[512,256]{1,0:T(8,128)(2,1)S(1)}, u32[]{:S(2)}, u32[]{:S(2)}) %collective-permute-start.46) | collective-permute-done | bytes 262176 | tf_op jit(solution)/shard_map/out_sum2/ppermute | solution.py:981
  550.0 9.5 %collective-permute-done.47.arrived_ref = bf16[512,256]{1,0:T(8,128)(2,1)S(1)} collective-permute-done((bf16[512,256]{1,0:T(8,128)(2,1)S(1)}, bf16[512,256]{1,0:T(8,128)(2,1)S(1)}, u32[]{:S(2)}, u32[]{:S(2)}) %collective-permute-start.47) | collective-permute-done | bytes 262176 | tf_op jit(solution)/shard_map/out_sum3/ppermute | solution.py:981
  588.3 18.5 %shard_map.404 = (f32[3,256,512]{2,1,0:T(8,128)}, bf16[3,256,512]{2,1,0:T(8,128)(2,1)}, f32[3,256,512]{2,1,0:T(8,128)}, f32[3,256,512]{2,1,0:T(8,128)}, f32[512,...) custom-call(f32[1]{0:T(128)} %bitcast.21.factor_ref, ...), custom_call_target="tpu_custom_call" | custom-call | flops 1 | bytes 1 | tf_op jit(solution)/shard_map/pallas_call | solution.py:860
  (360 shorter events, 281.9 us)
Async XLA Ops:
  7.2 65.0 %all-gather.6.cloned.1.call-start = ((), (), s32[]{:S(2)}) async-start(), calls=%async_computation.4 | async-start | bytes 7077888 | tf_op jit(solution)/shard_map/all_gather | solution.py:1011
  9.8 106.2 %all-gather.8.cloned.1.call-start = ((), (), s32[]{:S(2)}) async-start(), calls=%async_computation.5 | async-start | bytes 9437184 | tf_op jit(solution)/shard_map/all_gather | solution.py:1022
  9.9 28.4 %collective-permute-start = (bf16[256,2048]{1,0:T(8,128)(2,1)S(1)}, bf16[256,2048]{1,0:T(8,128)(2,1)}, u32[]{:S(2)}, u32[]{:S(2)}) collective-permute-start(bf16[256,2048]{1,0:T(8,128)(2,1)S(1)} %copy-done.33), channel_id=1, source_target_pairs={{0,1},{1,2},{2,3},{3,0},{4,5},{5,6},{6,7},{7,4},{8,9},{9,10},{10,1... | collective-permute-start | bytes 3145736 | tf_op jit(solution)/shard_map/x1/ppermute | solution.py:981
  39.9 171.5 %all-gather.12.cloned.1.call-start = ((), (), s32[]{:S(2)}) async-start(), calls=%async_computation.11 | async-start | bytes 9437184 | tf_op jit(solution)/shard_map/all_gather | solution.py:1061
  40.0 28.3 %collective-permute-start.1 = (bf16[256,2048]{1,0:T(8,128)(2,1)}, bf16[256,2048]{1,0:T(8,128)(2,1)}, u32[]{:S(2)}, u32[]{:S(2)}) collective-permute-start(bf16[256,2048]{1,0:T(8,128)(2,1)} %collective-permute-done.x_ref), channel_id=1, source_target_pairs={{0,1},{1,2},{2,3},{3,0},{4,5},{5,6},{6,7},{7,4},{8,9},{9,10},{10,1... | collective-permute-start | bytes 3145736 | tf_op jit(solution)/shard_map/x2/ppermute | solution.py:981
  40.2 31.9 %collective-permute-start.5 = (bf16[512,256]{1,0:T(8,128)(2,1)S(1)}, bf16[512,256]{1,0:T(8,128)(2,1)}, u32[]{:S(2)}, u32[]{:S(2)}) collective-permute-start(bf16[512,256]{1,0:T(8,128)(2,1)S(1)} %shard_map.353.refs_0_), channel_id=1, source_target_pairs={{0,1},{1,2},{2,3},{3,0},{4,5},{5,6},{6,7},{7,4},{8,9},{9,10},{10,1... | collective-permute-start | bytes 786440 | tf_op jit(solution)/shard_map/out1/ppermute | solution.py:981
  72.1 28.2 %collective-permute-start.6 = (bf16[256,2048]{1,0:T(8,128)(2,1)}, bf16[256,2048]{1,0:T(8,128)(2,1)}, u32[]{:S(2)}, u32[]{:S(2)}) collective-permute-start(bf16[256,2048]{1,0:T(8,128)(2,1)} %collective-permute-done.1.x_ref), channel_id=1, source_target_pairs={{0,1},{1,2},{2,3},{3,0},{4,5},{5,6},{6,7},{7,4},{8,9},{9,10},{10,1... | collective-permute-start | bytes 3145736 | tf_op jit(solution)/shard_map/x3/ppermute | solution.py:981
  72.1 31.2 %collective-permute-start.7 = (bf16[512,256]{1,0:T(8,128)(2,1)}, bf16[512,256]{1,0:T(8,128)(2,1)}, u32[]{:S(2)}, u32[]{:S(2)}) collective-permute-start(bf16[512,256]{1,0:T(8,128)(2,1)} %collective-permute-done.5.refs_1_), channel_id=1, source_target_pairs={{0,1},{1,2},{2,3},{3,0},{4,5},{5,6},{6,7},{7,4},{8,9},{9,10},{10,1... | collective-permute-start | bytes 786440 | tf_op jit(solution)/shard_map/out2/ppermute | solution.py:981
  116.0 119.7 %all-gather.10.cloned.1.call-start = ((), (), s32[]{:S(2)}) async-start(), calls=%async_computation.6 | async-start | bytes 9437184 | tf_op jit(solution)/shard_map/all_gather | solution.py:1063
  118.8 329.2 %reduce-scatter.5.cloned.1.call-start = ((), (), s32[]{:S(2)}) async-start(), calls=%async_computation.7 | async-start | bytes 5242880 | tf_op jit(solution)/shard_map/reduce_scatter | solution.py:1007
  352.2 132.9 %reduce-scatter.7.cloned.1.call-start = ((), (), s32[]{:S(2)}) async-start(), calls=%async_computation.8 | async-start | bytes 5242880 | tf_op jit(solution)/shard_map/reduce_scatter | solution.py:1007
  388.3 125.5 %reduce-scatter.9.cloned.1.call-start = ((), (), s32[]{:S(2)}) async-start(), calls=%async_computation.9 | async-start | bytes 5242880 | tf_op jit(solution)/shard_map/reduce_scatter | solution.py:1007
  411.1 28.9 %collective-permute-start.37 = (bf16[2048,256]{1,0:T(8,128)(2,1)}, bf16[2048,256]{1,0:T(8,128)(2,1)S(1)}, u32[]{:S(2)}, u32[]{:S(2)}) collective-permute-start(bf16[2048,256]{1,0:T(8,128)(2,1)} %get-tuple-element.367), channel_id=1, source_target_pairs={{0,4},{4,0},{1,5},{5,1},{2,6},{6,2},{3,7},{7,3},{8,12},{12,8},{9,1... | collective-permute-start | bytes 3145736 | tf_op jit(solution)/shard_map/out_grad_swap/ppermute | solution.py:1000
  411.1 28.9 %collective-permute-start.36 = (bf16[2048,256]{1,0:T(8,128)(2,1)}, bf16[2048,256]{1,0:T(8,128)(2,1)S(1)}, u32[]{:S(2)}, u32[]{:S(2)}) collective-permute-start(bf16[2048,256]{1,0:T(8,128)(2,1)} %get-tuple-element.365), channel_id=1, source_target_pairs={{0,4},{4,0},{1,5},{5,1},{2,6},{6,2},{3,7},{7,3},{8,12},{12,8},{9,1... | collective-permute-start | bytes 3145736 | tf_op jit(solution)/shard_map/out_grad_swap/ppermute | solution.py:1000
  411.6 28.4 %collective-permute-start.33 = (bf16[256,2048]{1,0:T(8,128)(2,1)S(1)}, bf16[256,2048]{1,0:T(8,128)(2,1)S(1)}, u32[]{:S(2)}, u32[]{:S(2)}) collective-permute-start(bf16[256,2048]{1,0:T(8,128)(2,1)S(1)} %shard_map.387), channel_id=1, source_target_pairs={{0,1},{1,2},{2,3},{3,0},{4,5},{5,6},{6,7},{7,4},{8,9},{9,10},{10,1... | collective-permute-start | bytes 3145736 | tf_op jit(solution)/shard_map/ffn1/ppermute | solution.py:981
  445.9 116.4 %reduce-scatter.11.cloned.1.call-start = ((), (), s32[]{:S(2)}) async-start(), calls=%async_computation.10 | async-start | bytes 3932160 | tf_op jit(solution)/shard_map/reduce_scatter | solution.py:1007
  446.0 27.2 %collective-permute-start.38 = (bf16[256,2048]{1,0:T(8,128)(2,1)S(1)}, bf16[256,2048]{1,0:T(8,128)(2,1)S(1)}, u32[]{:S(2)}, u32[]{:S(2)}) collective-permute-start(bf16[256,2048]{1,0:T(8,128)(2,1)S(1)} %shard_map.389), channel_id=1, source_target_pairs={{0,1},{1,2},{2,3},{3,0},{4,5},{5,6},{6,7},{7,4},{8,9},{9,10},{10,1... | collective-permute-start | bytes 3145736 | tf_op jit(solution)/shard_map/back1/ppermute | solution.py:981
  474.4 26.3 %collective-permute-start.39 = (bf16[256,2048]{1,0:T(8,128)(2,1)}, bf16[256,2048]{1,0:T(8,128)(2,1)}, u32[]{:S(2)}, u32[]{:S(2)}) collective-permute-start(bf16[256,2048]{1,0:T(8,128)(2,1)} %shard_map.393), channel_id=1, source_target_pairs={{0,1},{1,2},{2,3},{3,0},{4,5},{5,6},{6,7},{7,4},{8,9},{9,10},{10,1... | collective-permute-start | bytes 3145736 | tf_op jit(solution)/shard_map/back2/ppermute | solution.py:981
  474.4 28.8 %collective-permute-start.43 = (bf16[256,1536]{1,0:T(8,128)(2,1)}, bf16[256,1536]{1,0:T(8,128)(2,1)}, u32[]{:S(2)}, u32[]{:S(2)}) collective-permute-start(bf16[256,1536]{1,0:T(8,128)(2,1)} %get-tuple-element.387), channel_id=1, source_target_pairs={{0,4},{4,0},{1,5},{5,1},{2,6},{6,2},{3,7},{7,3},{8,12},{12,8},{9,1... | collective-permute-start | bytes 2359304 | tf_op jit(solution)/shard_map/qkv_grad_swap/ppermute | solution.py:1000
  474.4 28.8 %collective-permute-start.42 = (bf16[256,1536]{1,0:T(8,128)(2,1)}, bf16[256,1536]{1,0:T(8,128)(2,1)}, u32[]{:S(2)}, u32[]{:S(2)}) collective-permute-start(bf16[256,1536]{1,0:T(8,128)(2,1)} %get-tuple-element.385), channel_id=1, source_target_pairs={{0,4},{4,0},{1,5},{5,1},{2,6},{6,2},{3,7},{7,3},{8,12},{12,8},{9,1... | collective-permute-start | bytes 2359304 | tf_op jit(solution)/shard_map/qkv_grad_swap/ppermute | solution.py:1000
  474.9 28.3 %collective-permute-start.41 = (bf16[256,1536]{1,0:T(8,128)(2,1)}, bf16[256,1536]{1,0:T(8,128)(2,1)}, u32[]{:S(2)}, u32[]{:S(2)}) collective-permute-start(bf16[256,1536]{1,0:T(8,128)(2,1)} %get-tuple-element.383), channel_id=1, source_target_pairs={{0,4},{4,0},{1,5},{5,1},{2,6},{6,2},{3,7},{7,3},{8,12},{12,8},{9,1... | collective-permute-start | bytes 2359304 | tf_op jit(solution)/shard_map/qkv_grad_swap/ppermute | solution.py:1000
  474.9 28.3 %collective-permute-start.40 = (bf16[256,1536]{1,0:T(8,128)(2,1)}, bf16[256,1536]{1,0:T(8,128)(2,1)}, u32[]{:S(2)}, u32[]{:S(2)}) collective-permute-start(bf16[256,1536]{1,0:T(8,128)(2,1)} %get-tuple-element.381), channel_id=1, source_target_pairs={{0,4},{4,0},{1,5},{5,1},{2,6},{6,2},{3,7},{7,3},{8,12},{12,8},{9,1... | collective-permute-start | bytes 2359304 | tf_op jit(solution)/shard_map/qkv_grad_swap/ppermute | solution.py:1000
  508.3 28.3 %collective-permute-start.45 = (bf16[256,2048]{1,0:T(8,128)(2,1)}, bf16[256,2048]{1,0:T(8,128)(2,1)}, u32[]{:S(2)}, u32[]{:S(2)}) collective-permute-start(bf16[256,2048]{1,0:T(8,128)(2,1)} %copy-done.58), channel_id=1, source_target_pairs={{0,1},{1,2},{2,3},{3,0},{4,5},{5,6},{6,7},{7,4},{8,9},{9,10},{10,1... | collective-permute-start | bytes 3145736 | tf_op jit(solution)/shard_map/back3/ppermute | solution.py:981
  514.8 26.3 %collective-permute-start.44 = (bf16[512,256]{1,0:T(8,128)(2,1)S(1)}, bf16[512,256]{1,0:T(8,128)(2,1)S(1)}, u32[]{:S(2)}, u32[]{:S(2)}) collective-permute-start(bf16[512,256]{1,0:T(8,128)(2,1)S(1)} %constant_dynamic-slice_fusion), channel_id=1, source_target_pairs={{0,1},{1,2},{2,3},{3,0},{4,5},{5,6},{6,7},{7,4},{8,9},{9,10},{10,1... | collective-permute-start | bytes 786440 | tf_op jit(solution)/shard_map/out_sum1/ppermute | solution.py:981
  (121 other events, 1366.7 us)
Sparse Core Ops, SparseCore 0:
  10.5 48.5 all-gather.5
  61.6 54.3 all-gather.7
  118.5 54.4 all-gather.11
  175.3 55.9 all-gather.9
  352.3 49.9 reduce-scatter.4
  405.4 52.6 reduce-scatter.6
  461.1 52.6 reduce-scatter.8
  517.1 43.9 reduce-scatter.10

commit v5 on v4

--- a/solution.py
+++ b/solution.py
@@ -641,9 +641,10 @@
 
 def pair_add(place, block_rows, parts, arrived, bases, kind):
     rows, width = 2 * block_rows, parts[0].shape[1]
-    block = pl.BlockSpec((rows // 2, width), lambda i, p: (p[0], 0))
-    whole = pl.BlockSpec((rows, width), lambda i, p: (0, 0))
-    half = pl.BlockSpec((rows // 2, width), lambda i, p: (0, 0))
+    tile = min(512, width)
+    block = pl.BlockSpec((rows // 2, tile), lambda i, p: (p[0], i))
+    whole = pl.BlockSpec((rows, tile), lambda i, p: (0, i))
+    half = pl.BlockSpec((rows // 2, tile), lambda i, p: (0, i))
     operands, in_specs = list(parts), [block, block]
     if arrived is not None:
         operands.append(arrived)
@@ -654,7 +655,7 @@
     return pl.pallas_call(
         functools.partial(pair_add_body, len(operands)),
         grid_spec=pltpu.PrefetchScalarGridSpec(
-            num_scalar_prefetch=1, grid=(1,), in_specs=in_specs, out_specs=whole
+            num_scalar_prefetch=1, grid=(width // tile,), in_specs=in_specs, out_specs=whole
         ),
         out_shape=jax.ShapeDtypeStruct((rows, width), kind),
         compiler_params=params(),

time: 635 us -> 637 us (level)
  transfers between devices with their start and end apart: 63 -> 63, of which waited for: 29 -> 29; matrix products, arithmetic and copies ran while one was open for 2% -> 2% of each run, Pallas kernels for 43% -> 44%
where the time goes in v5:
time: 637 us; the launch traced here: 626 us
  Pallas kernels  290 us (46%)
  waiting for transfers between devices  218 us (34%)
  local copies, waits for them, and re-layouts  41.9 us (7%)
  starting transfers between devices  38.7 us (6%)
  between operations  21.5 us (3%)
  other arithmetic  14.8 us (2%)
    ppermute x28, waiting for transfers between devices, pass_on(): return lax.ppermute(at(value, *others), 'bkt', ring)  197 us
    unnamed x164, local copies, waits for them, and re-layouts  40.3 us
    pallas_call x3, Pallas kernels, weight_grad(): pl.pallas_call(functools.partial(grad_body, len(lefts), axis), grid_spec=...  35.2 us
    pallas_call x4, Pallas kernels, product(): pl.pallas_call(functools.partial(product_body, NT if turned else NN), gri...  29.2 us
    pallas_call x2, Pallas kernels, hidden_units(): pl.pallas_call(functools.partial(hidden_body, count), grid_spec=pltpu.Pre...  29.1 us
    pallas_call x4, Pallas kernels, project(): pl.pallas_call(project_body, grid_spec=pltpu.PrefetchScalarGridSpec(num_s...  28.3 us
    ppermute x28, starting transfers between devices, pass_on(): return lax.ppermute(at(value, *others), 'bkt', ring)  22.8 us
    pallas_call x4, Pallas kernels, core_add_kernel(): pl.pallas_call(core_add_body, grid=(rows // tile,), in_specs=[spec] + [pl...  21.9 us
  transfers between devices with their start and end apart: 63, of which 29 were waited for; matrix products, arithmetic and copies ran while one was open for 2% of the time, Pallas kernels for 44%

profile of v5, /device:TPU:0, one launch (start us, length us, event | category | flops | bytes accessed | tf_op | source)
XLA Modules:
  0.0 625.5 jit_solution(13539923056365384375)
XLA Ops:
  16.1 22.1 %collective-permute-done.x_ref = bf16[256,2048]{1,0:T(8,128)(2,1)} collective-permute-done((bf16[256,2048]{1,0:T(8,128)(2,1)S(1)}, bf16[256,2048]{1,0:T(8,128)(2,1)}, u32[]{:S(2)}, u32[]{:S(2)}) %collective-permute-start) | collective-permute-done | bytes 1048608 | tf_op jit(solution)/shard_map/x1/ppermute | solution.py:982
  49.8 18.5 %collective-permute-done.1.x_ref = bf16[256,2048]{1,0:T(8,128)(2,1)} collective-permute-done((bf16[256,2048]{1,0:T(8,128)(2,1)}, bf16[256,2048]{1,0:T(8,128)(2,1)}, u32[]{:S(2)}, u32[]{:S(2)}) %collective-permute-start.1) | collective-permute-done | bytes 1048608 | tf_op jit(solution)/shard_map/x2/ppermute | solution.py:982
  89.0 7.8 %shard_map.359 = (bf16[1024,2048]{1,0:T(8,128)(2,1)}, bf16[3,1024,512]{2,1,0:T(8,128)(2,1)S(1)}, bf16[1024,2048]{1,0:T(8,128)(2,1)}) custom-call(s32[1]{0:T(128)} %bitcast.2.place_ref, bf16[256,2048]{1,0:T(8,128)(2,1)} %collective-permute-done.1.x_ref, f32[1,2048]{1,0:T(1,128)S(1)} %bitcast.26, ...), custom_call_target="tpu_custom_call", output_to_operand_aliasing={{0}: (6, {}), {1}: (7, {}), {2}: (8, {})} | custom-call | flops 1 | bytes 1 | tf_op jit(solution)/shard_map/pallas_call | solution.py:95
  121.4 7.8 %shard_map.363 = (bf16[1024,512]{1,0:T(8,128)(2,1)S(1)}, f32[512,512]{1,0:T(8,128)S(1)}) custom-call(bf16[3,1024,512]{2,1,0:T(8,128)(2,1)S(1)} %get-tuple-element.354.q_ref.k_ref.v_ref, bf16[3,1024,512]{2,1,0:T(8,128)(2,1)S(1)} %get-tuple-element.354.q_ref.k_ref.v_ref, bf16[3,1024,512]{2,1,0:T(8,128)(2,1)S(1)} %get-tuple-element.354.q_ref.k_ref.v_ref, ...), custom_call_target="tpu_custom_call" | custom-call | flops 1 | bytes 1 | tf_op jit(solution)/shard_map/pallas_call | solution.py:162
  135.0 8.4 %shard_map.364 = (bf16[1024,512]{1,0:T(8,128)(2,1)}, f32[512,512]{1,0:T(8,128)S(1)}) custom-call(bf16[3,1024,512]{2,1,0:T(8,128)(2,1)S(1)} %get-tuple-element.354.q_ref.k_ref.v_ref, bf16[3,1024,512]{2,1,0:T(8,128)(2,1)S(1)} %get-tuple-element.354.q_ref.k_ref.v_ref, bf16[3,1024,512]{2,1,0:T(8,128)(2,1)S(1)} %get-tuple-element.354.q_ref.k_ref.v_ref, ...), custom_call_target="tpu_custom_call" | custom-call | flops 1 | bytes 1 | tf_op jit(solution)/shard_map/pallas_call | solution.py:162
  144.4 16.9 %collective-permute-done.10.rest_1_ = bf16[1024,512]{1,0:T(8,128)(2,1)S(1)} collective-permute-done((bf16[1024,512]{1,0:T(8,128)(2,1)S(1)}, bf16[1024,512]{1,0:T(8,128)(2,1)S(1)}, u32[]{:S(2)}, u32[]{:S(2)}) %collective-permute-start.10) | collective-permute-done | bytes 1048608 | tf_op jit(solution)/shard_map/slaba1/ppermute | solution.py:982
  162.3 24.4 %collective-permute-done.11.rest_2_ = bf16[1024,512]{1,0:T(8,128)(2,1)S(1)} collective-permute-done((bf16[1024,512]{1,0:T(8,128)(2,1)S(1)}, bf16[1024,512]{1,0:T(8,128)(2,1)S(1)}, u32[]{:S(2)}, u32[]{:S(2)}) %collective-permute-start.11) | collective-permute-done | bytes 1048608 | tf_op jit(solution)/shard_map/slaba2/ppermute | solution.py:982
  186.7 24.5 %collective-permute-done.12.rest_3_ = bf16[1024,512]{1,0:T(8,128)(2,1)S(1)} collective-permute-done((bf16[1024,512]{1,0:T(8,128)(2,1)S(1)}, bf16[1024,512]{1,0:T(8,128)(2,1)S(1)}, u32[]{:S(2)}, u32[]{:S(2)}) %collective-permute-start.12) | collective-permute-done | bytes 1048608 | tf_op jit(solution)/shard_map/slaba3/ppermute | solution.py:982
  214.0 8.2 %shard_map.365.acc_ref = f32[512,2048]{1,0:T(8,128)} custom-call(s32[4]{0:T(128)S(1)} %pad_add_fusion.place_ref, bf16[4,256,2048]{2,1,0:T(8,128)(2,1)} %bitcast.44, bf16[1024,512]{1,0:T(8,128)(2,1)S(1)} %copy-done.19, bf16[1024,512]{1,0:T(8,128)(2,1)S(1)} %copy-done.21, bf16[1024,512]{1,0:T(8,128)(2,1)S(1)} %collective-permute-done.11.rest_2_, ...), custom_call_target="tpu_custom_call" | custom-call | flops 1 | bytes 1 | tf_op jit(solution)/shard_map/pallas_call | solution.py:284
  235.8 14.6 %shard_map.367 = (bf16[512,2048]{1,0:T(8,128)(2,1)}, bf16[512,2048]{1,0:T(8,128)(2,1)}, bf16[512,2048]{1,0:T(8,128)(2,1)}) custom-call(s32[4]{0:T(128)} %copy-done.70, f32[1]{0:T(128)S(6)} %convert_element_type.48.live_ref, bf16[512,2048]{1,0:T(8,128)(2,1)} %get-tuple-element.278.normed_ref.refs_0_, ...), custom_call_target="tpu_custom_call" | custom-call | flops 1 | bytes 1 | tf_op jit(solution)/shard_map/pallas_call | solution.py:387
  250.3 8.0 %collective-permute-done.14.rest_2_.rest_3_ = bf16[1024,512]{1,0:T(8,128)(2,1)S(1)} collective-permute-done((bf16[1024,512]{1,0:T(8,128)(2,1)S(1)}, bf16[1024,512]{1,0:T(8,128)(2,1)S(1)}, u32[]{:S(2)}, u32[]{:S(2)}) %collective-permute-start.14) | collective-permute-done | bytes 1048608 | tf_op jit(solution)/shard_map/slabb2/ppermute | solution.py:982
  260.3 7.2 %shard_map.368.part_ref = bf16[512,2048]{1,0:T(8,128)(2,1)S(1)} custom-call(bf16[512,2048]{1,0:T(8,128)(2,1)S(1)} %copy-done.27, bf16[2048,2048]{1,0:T(8,128)(2,1)} %all-gather.8.cloned.1.call-done.up_ref.right_ref), custom_call_target="tpu_custom_call" | custom-call | flops 1 | bytes 1 | tf_op jit(solution)/shard_map/pallas_call | solution.py:428
  267.6 8.4 %shard_map.369.acc_ref = f32[512,2048]{1,0:T(8,128)} custom-call(s32[4]{0:T(128)S(1)} %copy-done.71, bf16[4,256,2048]{2,1,0:T(8,128)(2,1)} %bitcast.45, bf16[1024,512]{1,0:T(8,128)(2,1)} %get-tuple-element.276.rest_0_, bf16[1024,512]{1,0:T(8,128)(2,1)S(1)} %collective-permute-done.13.rest_1_.rest_2_, ...), custom_call_target="tpu_custom_call" | custom-call | flops 1 | bytes 1 | tf_op jit(solution)/shard_map/pallas_call | solution.py:284
  283.4 14.5 %shard_map.372 = (bf16[512,2048]{1,0:T(8,128)(2,1)}, bf16[512,2048]{1,0:T(8,128)(2,1)}, bf16[512,2048]{1,0:T(8,128)(2,1)}) custom-call(s32[4]{0:T(128)} %copy-done.70, f32[1]{0:T(128)S(6)} %convert_element_type.48.live_ref, bf16[512,2048]{1,0:T(8,128)(2,1)} %get-tuple-element.292.normed_ref.refs_1_, ...), custom_call_target="tpu_custom_call" | custom-call | flops 1 | bytes 1 | tf_op jit(solution)/shard_map/pallas_call | solution.py:387
  311.5 15.0 %shard_map.375 = (bf16[4,256,2048]{2,1,0:T(8,128)(2,1)}, bf16[256,2048]{1,0:T(8,128)(2,1)}, bf16[256,2048]{1,0:T(8,128)(2,1)}, bf16[256,2048]{1,0:T(8,128)(2,1)}, bf16[256,2048]{1,0:T(8,128)(2,1)}) custom-call(s32[1]{0:T(128)} %bitcast.12.core_ref, bf16[512,2048]{1,0:T(8,128)(2,1)} %get-tuple-element.278.normed_ref.refs_0_, ...), custom_call_target="tpu_custom_call" | custom-call | flops 1 | bytes 1 | tf_op jit(solution)/shard_map/pallas_call | solution.py:486
  333.7 7.7 %shard_map.378.refs_1_ = bf16[512,2048]{1,0:T(8,128)(2,1)S(1)} custom-call(bf16[512,2048]{1,0:T(8,128)(2,1)S(1)} %copy-done.26, bf16[2048,2048]{1,0:T(8,128)(2,1)} %all-gather.10.cloned.1.call-done.down_ref.right_ref), custom_call_target="tpu_custom_call" | custom-call | flops 1 | bytes 1 | tf_op jit(solution)/shard_map/pallas_call | solution.py:428
  352.4 13.6 %shard_map.381 = (bf16[4,2048,256]{2,1,0:T(8,128)(2,1)}, bf16[2048,256]{1,0:T(8,128)(2,1)}, bf16[2048,256]{1,0:T(8,128)(2,1)}, bf16[2048,256]{1,0:T(8,128)(2,1)}, bf16[2048,256]{1,0:T(8,128)(2,1)}) custom-call(s32[1]{0:T(128)} %bitcast.12.core_ref, bf16[512,2048]{1,0:T(8,128)(2,1)} %get-tuple-element.342.refs_0_.left_ref, ...), custom_call_target="tpu_custom_call" | custom-call | flops 1 | bytes 1 | tf_op jit(solution)/shard_map/pallas_call | solution.py:486
  418.1 15.1 %shard_map.388.back_ref.right_ref = bf16[3,1024,512]{2,1,0:T(8,128)(2,1)} custom-call(s32[4]{0:T(128)S(1)} %copy-done.72, bf16[3,1024,512]{2,1,0:T(8,128)(2,1)} %copy-done, bf16[3,1024,512]{2,1,0:T(8,128)(2,1)} %copy-done, bf16[3,1024,512]{2,1,0:T(8,128)(2,1)} %copy-done, f32[512,512]{1,0:T(8,128)S(1)} %copy-done.53, f32[512,512]{1,0:T(8,128)S(1)} %copy-done.55, ...), custom_call_target="tpu_custom_call" | custom-call | flops 1 | bytes 1 | tf_op jit(solution)/shard_map/pallas_call | solution.py:234
  450.3 12.0 %shard_map.391 = (bf16[4,256,1536]{2,1,0:T(8,128)(2,1)}, bf16[256,1536]{1,0:T(8,128)(2,1)}, bf16[256,1536]{1,0:T(8,128)(2,1)}, bf16[256,1536]{1,0:T(8,128)(2,1)}, bf16[256,1536]{1,0:T(8,128)(2,1)}) custom-call(s32[1]{0:T(128)} %bitcast.12.core_ref, bf16[1024,2048]{1,0:T(8,128)(2,1)} %get-tuple-element.257.left_ref, ...), custom_call_target="tpu_custom_call" | custom-call | flops 1 | bytes 1 | tf_op jit(solution)/shard_map/pallas_call | solution.py:517
  487.5 13.2 %collective-permute-done.39.arrived_ref = bf16[256,2048]{1,0:T(8,128)(2,1)} collective-permute-done((bf16[256,2048]{1,0:T(8,128)(2,1)}, bf16[256,2048]{1,0:T(8,128)(2,1)}, u32[]{:S(2)}, u32[]{:S(2)}) %collective-permute-start.39) | collective-permute-done | bytes 1048608 | tf_op jit(solution)/shard_map/back2/ppermute | solution.py:982
  521.1 15.5 %collective-permute-done.45.arrived_ref = bf16[256,2048]{1,0:T(8,128)(2,1)} collective-permute-done((bf16[256,2048]{1,0:T(8,128)(2,1)}, bf16[256,2048]{1,0:T(8,128)(2,1)}, u32[]{:S(2)}, u32[]{:S(2)}) %collective-permute-start.45) | collective-permute-done | bytes 1048608 | tf_op jit(solution)/shard_map/back3/ppermute | solution.py:982
  541.3 8.6 %collective-permute-done.46.arrived_ref = bf16[512,256]{1,0:T(8,128)(2,1)S(1)} collective-permute-done((bf16[512,256]{1,0:T(8,128)(2,1)S(1)}, bf16[512,256]{1,0:T(8,128)(2,1)S(1)}, u32[]{:S(2)}, u32[]{:S(2)}) %collective-permute-start.46) | collective-permute-done | bytes 262176 | tf_op jit(solution)/shard_map/out_sum2/ppermute | solution.py:982
  550.0 9.5 %collective-permute-done.47.arrived_ref = bf16[512,256]{1,0:T(8,128)(2,1)S(1)} collective-permute-done((bf16[512,256]{1,0:T(8,128)(2,1)S(1)}, bf16[512,256]{1,0:T(8,128)(2,1)S(1)}, u32[]{:S(2)}, u32[]{:S(2)}) %collective-permute-start.47) | collective-permute-done | bytes 262176 | tf_op jit(solution)/shard_map/out_sum3/ppermute | solution.py:982
  588.8 18.5 %shard_map.404 = (f32[3,256,512]{2,1,0:T(8,128)}, bf16[3,256,512]{2,1,0:T(8,128)(2,1)}, f32[3,256,512]{2,1,0:T(8,128)}, f32[3,256,512]{2,1,0:T(8,128)}, f32[512,...) custom-call(f32[1]{0:T(128)} %bitcast.21.factor_ref, ...), custom_call_target="tpu_custom_call" | custom-call | flops 1 | bytes 1 | tf_op jit(solution)/shard_map/pallas_call | solution.py:861
  (360 shorter events, 284.1 us)
Async XLA Ops:
  7.2 65.0 %all-gather.6.cloned.1.call-start = ((), (), s32[]{:S(2)}) async-start(), calls=%async_computation.4 | async-start | bytes 7077888 | tf_op jit(solution)/shard_map/all_gather | solution.py:1012
  9.8 106.2 %all-gather.8.cloned.1.call-start = ((), (), s32[]{:S(2)}) async-start(), calls=%async_computation.5 | async-start | bytes 9437184 | tf_op jit(solution)/shard_map/all_gather | solution.py:1023
  9.9 28.4 %collective-permute-start = (bf16[256,2048]{1,0:T(8,128)(2,1)S(1)}, bf16[256,2048]{1,0:T(8,128)(2,1)}, u32[]{:S(2)}, u32[]{:S(2)}) collective-permute-start(bf16[256,2048]{1,0:T(8,128)(2,1)S(1)} %copy-done.33), channel_id=1, source_target_pairs={{0,1},{1,2},{2,3},{3,0},{4,5},{5,6},{6,7},{7,4},{8,9},{9,10},{10,1... | collective-permute-start | bytes 3145736 | tf_op jit(solution)/shard_map/x1/ppermute | solution.py:982
  39.9 171.5 %all-gather.12.cloned.1.call-start = ((), (), s32[]{:S(2)}) async-start(), calls=%async_computation.11 | async-start | bytes 9437184 | tf_op jit(solution)/shard_map/all_gather | solution.py:1062
  40.0 28.3 %collective-permute-start.1 = (bf16[256,2048]{1,0:T(8,128)(2,1)}, bf16[256,2048]{1,0:T(8,128)(2,1)}, u32[]{:S(2)}, u32[]{:S(2)}) collective-permute-start(bf16[256,2048]{1,0:T(8,128)(2,1)} %collective-permute-done.x_ref), channel_id=1, source_target_pairs={{0,1},{1,2},{2,3},{3,0},{4,5},{5,6},{6,7},{7,4},{8,9},{9,10},{10,1... | collective-permute-start | bytes 3145736 | tf_op jit(solution)/shard_map/x2/ppermute | solution.py:982
  40.2 31.9 %collective-permute-start.5 = (bf16[512,256]{1,0:T(8,128)(2,1)S(1)}, bf16[512,256]{1,0:T(8,128)(2,1)}, u32[]{:S(2)}, u32[]{:S(2)}) collective-permute-start(bf16[512,256]{1,0:T(8,128)(2,1)S(1)} %shard_map.353.refs_0_), channel_id=1, source_target_pairs={{0,1},{1,2},{2,3},{3,0},{4,5},{5,6},{6,7},{7,4},{8,9},{9,10},{10,1... | collective-permute-start | bytes 786440 | tf_op jit(solution)/shard_map/out1/ppermute | solution.py:982
  72.1 28.2 %collective-permute-start.6 = (bf16[256,2048]{1,0:T(8,128)(2,1)}, bf16[256,2048]{1,0:T(8,128)(2,1)}, u32[]{:S(2)}, u32[]{:S(2)}) collective-permute-start(bf16[256,2048]{1,0:T(8,128)(2,1)} %collective-permute-done.1.x_ref), channel_id=1, source_target_pairs={{0,1},{1,2},{2,3},{3,0},{4,5},{5,6},{6,7},{7,4},{8,9},{9,10},{10,1... | collective-permute-start | bytes 3145736 | tf_op jit(solution)/shard_map/x3/ppermute | solution.py:982
  72.1 31.2 %collective-permute-start.7 = (bf16[512,256]{1,0:T(8,128)(2,1)}, bf16[512,256]{1,0:T(8,128)(2,1)}, u32[]{:S(2)}, u32[]{:S(2)}) collective-permute-start(bf16[512,256]{1,0:T(8,128)(2,1)} %collective-permute-done.5.refs_1_), channel_id=1, source_target_pairs={{0,1},{1,2},{2,3},{3,0},{4,5},{5,6},{6,7},{7,4},{8,9},{9,10},{10,1... | collective-permute-start | bytes 786440 | tf_op jit(solution)/shard_map/out2/ppermute | solution.py:982
  116.0 119.7 %all-gather.10.cloned.1.call-start = ((), (), s32[]{:S(2)}) async-start(), calls=%async_computation.6 | async-start | bytes 9437184 | tf_op jit(solution)/shard_map/all_gather | solution.py:1064
  118.8 329.2 %reduce-scatter.5.cloned.1.call-start = ((), (), s32[]{:S(2)}) async-start(), calls=%async_computation.7 | async-start | bytes 5242880 | tf_op jit(solution)/shard_map/reduce_scatter | solution.py:1008
  352.2 132.9 %reduce-scatter.7.cloned.1.call-start = ((), (), s32[]{:S(2)}) async-start(), calls=%async_computation.8 | async-start | bytes 5242880 | tf_op jit(solution)/shard_map/reduce_scatter | solution.py:1008
  388.3 125.5 %reduce-scatter.9.cloned.1.call-start = ((), (), s32[]{:S(2)}) async-start(), calls=%async_computation.9 | async-start | bytes 5242880 | tf_op jit(solution)/shard_map/reduce_scatter | solution.py:1008
  411.1 28.9 %collective-permute-start.37 = (bf16[2048,256]{1,0:T(8,128)(2,1)}, bf16[2048,256]{1,0:T(8,128)(2,1)S(1)}, u32[]{:S(2)}, u32[]{:S(2)}) collective-permute-start(bf16[2048,256]{1,0:T(8,128)(2,1)} %get-tuple-element.367), channel_id=1, source_target_pairs={{0,4},{4,0},{1,5},{5,1},{2,6},{6,2},{3,7},{7,3},{8,12},{12,8},{9,1... | collective-permute-start | bytes 3145736 | tf_op jit(solution)/shard_map/out_grad_swap/ppermute | solution.py:1001
  411.1 28.9 %collective-permute-start.36 = (bf16[2048,256]{1,0:T(8,128)(2,1)}, bf16[2048,256]{1,0:T(8,128)(2,1)S(1)}, u32[]{:S(2)}, u32[]{:S(2)}) collective-permute-start(bf16[2048,256]{1,0:T(8,128)(2,1)} %get-tuple-element.365), channel_id=1, source_target_pairs={{0,4},{4,0},{1,5},{5,1},{2,6},{6,2},{3,7},{7,3},{8,12},{12,8},{9,1... | collective-permute-start | bytes 3145736 | tf_op jit(solution)/shard_map/out_grad_swap/ppermute | solution.py:1001
  411.6 28.4 %collective-permute-start.33 = (bf16[256,2048]{1,0:T(8,128)(2,1)S(1)}, bf16[256,2048]{1,0:T(8,128)(2,1)S(1)}, u32[]{:S(2)}, u32[]{:S(2)}) collective-permute-start(bf16[256,2048]{1,0:T(8,128)(2,1)S(1)} %shard_map.387), channel_id=1, source_target_pairs={{0,1},{1,2},{2,3},{3,0},{4,5},{5,6},{6,7},{7,4},{8,9},{9,10},{10,1... | collective-permute-start | bytes 3145736 | tf_op jit(solution)/shard_map/ffn1/ppermute | solution.py:982
  445.9 116.4 %reduce-scatter.11.cloned.1.call-start = ((), (), s32[]{:S(2)}) async-start(), calls=%async_computation.10 | async-start | bytes 3932160 | tf_op jit(solution)/shard_map/reduce_scatter | solution.py:1008
  446.0 27.2 %collective-permute-start.38 = (bf16[256,2048]{1,0:T(8,128)(2,1)S(1)}, bf16[256,2048]{1,0:T(8,128)(2,1)S(1)}, u32[]{:S(2)}, u32[]{:S(2)}) collective-permute-start(bf16[256,2048]{1,0:T(8,128)(2,1)S(1)} %shard_map.389), channel_id=1, source_target_pairs={{0,1},{1,2},{2,3},{3,0},{4,5},{5,6},{6,7},{7,4},{8,9},{9,10},{10,1... | collective-permute-start | bytes 3145736 | tf_op jit(solution)/shard_map/back1/ppermute | solution.py:982
  474.4 26.3 %collective-permute-start.39 = (bf16[256,2048]{1,0:T(8,128)(2,1)}, bf16[256,2048]{1,0:T(8,128)(2,1)}, u32[]{:S(2)}, u32[]{:S(2)}) collective-permute-start(bf16[256,2048]{1,0:T(8,128)(2,1)} %shard_map.393), channel_id=1, source_target_pairs={{0,1},{1,2},{2,3},{3,0},{4,5},{5,6},{6,7},{7,4},{8,9},{9,10},{10,1... | collective-permute-start | bytes 3145736 | tf_op jit(solution)/shard_map/back2/ppermute | solution.py:982
  474.4 28.8 %collective-permute-start.43 = (bf16[256,1536]{1,0:T(8,128)(2,1)}, bf16[256,1536]{1,0:T(8,128)(2,1)}, u32[]{:S(2)}, u32[]{:S(2)}) collective-permute-start(bf16[256,1536]{1,0:T(8,128)(2,1)} %get-tuple-element.387), channel_id=1, source_target_pairs={{0,4},{4,0},{1,5},{5,1},{2,6},{6,2},{3,7},{7,3},{8,12},{12,8},{9,1... | collective-permute-start | bytes 2359304 | tf_op jit(solution)/shard_map/qkv_grad_swap/ppermute | solution.py:1001
  474.4 28.8 %collective-permute-start.42 = (bf16[256,1536]{1,0:T(8,128)(2,1)}, bf16[256,1536]{1,0:T(8,128)(2,1)}, u32[]{:S(2)}, u32[]{:S(2)}) collective-permute-start(bf16[256,1536]{1,0:T(8,128)(2,1)} %get-tuple-element.385), channel_id=1, source_target_pairs={{0,4},{4,0},{1,5},{5,1},{2,6},{6,2},{3,7},{7,3},{8,12},{12,8},{9,1... | collective-permute-start | bytes 2359304 | tf_op jit(solution)/shard_map/qkv_grad_swap/ppermute | solution.py:1001
  474.9 28.3 %collective-permute-start.41 = (bf16[256,1536]{1,0:T(8,128)(2,1)}, bf16[256,1536]{1,0:T(8,128)(2,1)}, u32[]{:S(2)}, u32[]{:S(2)}) collective-permute-start(bf16[256,1536]{1,0:T(8,128)(2,1)} %get-tuple-element.383), channel_id=1, source_target_pairs={{0,4},{4,0},{1,5},{5,1},{2,6},{6,2},{3,7},{7,3},{8,12},{12,8},{9,1... | collective-permute-start | bytes 2359304 | tf_op jit(solution)/shard_map/qkv_grad_swap/ppermute | solution.py:1001
  474.9 28.3 %collective-permute-start.40 = (bf16[256,1536]{1,0:T(8,128)(2,1)}, bf16[256,1536]{1,0:T(8,128)(2,1)}, u32[]{:S(2)}, u32[]{:S(2)}) collective-permute-start(bf16[256,1536]{1,0:T(8,128)(2,1)} %get-tuple-element.381), channel_id=1, source_target_pairs={{0,4},{4,0},{1,5},{5,1},{2,6},{6,2},{3,7},{7,3},{8,12},{12,8},{9,1... | collective-permute-start | bytes 2359304 | tf_op jit(solution)/shard_map/qkv_grad_swap/ppermute | solution.py:1001
  508.3 28.3 %collective-permute-start.45 = (bf16[256,2048]{1,0:T(8,128)(2,1)}, bf16[256,2048]{1,0:T(8,128)(2,1)}, u32[]{:S(2)}, u32[]{:S(2)}) collective-permute-start(bf16[256,2048]{1,0:T(8,128)(2,1)} %copy-done.58), channel_id=1, source_target_pairs={{0,1},{1,2},{2,3},{3,0},{4,5},{5,6},{6,7},{7,4},{8,9},{9,10},{10,1... | collective-permute-start | bytes 3145736 | tf_op jit(solution)/shard_map/back3/ppermute | solution.py:982
  514.8 26.3 %collective-permute-start.44 = (bf16[512,256]{1,0:T(8,128)(2,1)S(1)}, bf16[512,256]{1,0:T(8,128)(2,1)S(1)}, u32[]{:S(2)}, u32[]{:S(2)}) collective-permute-start(bf16[512,256]{1,0:T(8,128)(2,1)S(1)} %constant_dynamic-slice_fusion), channel_id=1, source_target_pairs={{0,1},{1,2},{2,3},{3,0},{4,5},{5,6},{6,7},{7,4},{8,9},{9,10},{10,1... | collective-permute-start | bytes 786440 | tf_op jit(solution)/shard_map/out_sum1/ppermute | solution.py:982
  (121 other events, 1367.6 us)
Sparse Core Ops, SparseCore 0:
  10.5 48.5 all-gather.5
  61.6 54.3 all-gather.7
  118.5 54.4 all-gather.11
  175.3 55.9 all-gather.9
  352.3 49.9 reduce-scatter.4
  405.4 52.6 reduce-scatter.6
  461.1 52.6 reduce-scatter.8
  517.1 43.9 reduce-scatter.10
